TPU v7x, 32 devices: a whole 2x2x4 slice. The times are simulated.
32 devices in a mesh: depth: 4 (over y, core), strips: 8 (over z, x).
Axes of the slice: x: 2, y: 2, z: 4, core: 2. Of those that a mesh axis runs over, the one named last changes fastest.
Arguments:
- pressure: float32 [32, 1024, 1024], P('depth', 'strips'), may hold values from -3 to 3
- texture: int32 [32, 1024, 1024], P('depth', 'strips'), may hold values from 0 to 11
- active: int32 [32, 1024, 1024], P('depth', 'strips'), may hold values 0 or 1
- rain: float32 [1024, 1024], P('strips'), may hold values from 0 to 40
- k_sat: float32 [12], replicated, may hold values from 0.05 to 2
- alpha: float32 [12], replicated, may hold values from 0.5 to 4
- theta_sat: float32 [12], replicated, may hold values from 0.35 to 0.5
- head_old: float32 [1024, 1024], P('strips', 'depth'), may hold values from -4 to 4
- cell_code: int32 [1024, 1024], P('strips', 'depth'), may hold values from 0 to 2
- section: float32 [1024, 1024], P('strips', 'depth'), may hold values from -4 to 4
Outputs:
- moisture_new: float32 [32, 1024, 1024], P('depth', 'strips')
- head: float32 [1024, 1024], P('strips', 'depth')
All inputs are finite; a program needn't handle non-finite values. No bound on the sum of `active` on one device may be relied on, other than what follows from the above.
Results may differ from a plain program's by a relative error of at most 0.00002.
Values sent between devices are 32-bit elements; how exact they have to be, the bound alone decides.
No kernel may reach another device: no remote copies, remote signals or barrier semaphores. Data moves between devices by JAX's collectives and lax.ppermute only.
A program may use at most 128 MiB of HBM per device.

v0:
```python
import jax
import jax.numpy as jnp
from jax import lax
from jax.sharding import PartitionSpec as P

SWEEPS = 3


layer_thick = 0.05
soil_step = 0.0002
spec_yield = 0.02
leak_rate = 0.5
river_cond = 0.5
fixed_cond = 3.0


def shifted(value, axis, steps):
    count = lax.axis_size(axis)
    leading, last = (max(0, -steps), min(count, count - steps))
    return lax.ppermute(value, axis, [(source, source + steps) for source in range(leading, last)])


def with_halo(cells, sides, width):
    for axis, dim in sides:
        count = lax.axis_size(axis)
        ends = count - 1
        head = lax.slice_in_dim(cells, 0, width, axis=dim)
        tail = lax.slice_in_dim(cells, cells.shape[dim] - width, cells.shape[dim], axis=dim)
        cells = jnp.concatenate(
            [
                lax.ppermute(tail, axis, [(i, (i + 1) % count) for i in range(ends)]),
                cells,
                lax.ppermute(head, axis, [((i + 1) % count, i) for i in range(ends)]),
            ],
            axis=dim,
        )
    return cells


def lookup(texture, table):
    result = jnp.zeros(texture.shape, jnp.float32)
    for class_id in range(table.shape[0]):
        result = result + jnp.where(texture == class_id, table[class_id], jnp.float32(0.0))
    return result


def face_flux(psi_up, cond_up, psi_low, cond_low):
    return 0.5 * (cond_up + cond_low) * ((psi_up - psi_low) / layer_thick + 1.0)


def neighbour(padded, shift_a, shift_b):
    return padded[
        1 + shift_a : padded.shape[0] - 1 + shift_a, 1 + shift_b : padded.shape[1] - 1 + shift_b
    ]


def sweep(head_pad, trans_pad, base, rhs):
    centre = neighbour(trans_pad, 0, 0)
    total = base
    accum = rhs
    for shift_a, shift_b in ((1, 0), (-1, 0), (0, 1), (0, -1)):
        face = jnp.sqrt(centre * neighbour(trans_pad, shift_a, shift_b))
        accum = accum + face * neighbour(head_pad, shift_a, shift_b)
        total = total + face
    inside = total > 0.0
    return jnp.where(inside, accum / jnp.where(inside, total, 1.0), 0.0)


def shards(pressure, texture, active, rain, k_sat, alpha, theta_sat, head_old, cell_code, section):
    depth_index = lax.axis_index("depth")
    is_top = depth_index == 0
    is_bottom = depth_index == lax.axis_size("depth") - 1
    sat_cond = lookup(texture, k_sat)
    shape_par = lookup(texture, alpha)
    porous = lookup(texture, theta_sat)
    suction = jnp.minimum(pressure, 0.0)
    wetness = jnp.exp(0.5 * shape_par * suction)
    conduct = sat_cond * jnp.exp(shape_par * suction) * active.astype(jnp.float32)
    moisture = porous * (0.15 + 0.85 * wetness)
    below = shifted(jnp.concatenate([pressure[:1], conduct[:1]], axis=0), "depth", -1)
    inner = face_flux(pressure[:-1], conduct[:-1], pressure[1:], conduct[1:])
    last_face = face_flux(pressure[-1], conduct[-1], below[0], below[1])
    above = shifted(last_face, "depth", 1)
    upper = jnp.concatenate([jnp.where(is_top, rain, above)[None], inner], axis=0)
    lower_last = last_face
    trans_part = jnp.sum(conduct, axis=0)
    store_part = jnp.sum(0.85 * porous * (1.0 - wetness), axis=0)
    charge_part = jnp.sum(conduct * wetness, axis=0)
    tile_cols = head_old.shape[1]
    summed = lax.psum((trans_part, store_part, charge_part), "depth")
    trans_sum = lax.dynamic_slice_in_dim(summed[0], depth_index * tile_cols, tile_cols, 1)
    store_sum = lax.dynamic_slice_in_dim(summed[1], depth_index * tile_cols, tile_cols, 1)
    charge_sum = lax.dynamic_slice_in_dim(summed[2], depth_index * tile_cols, tile_cols, 1)
    trans = trans_sum * layer_thick
    store = spec_yield + store_sum * layer_thick
    recharge = leak_rate * (charge_sum * layer_thick)
    river = jnp.where(
        cell_code == 1,
        jnp.float32(river_cond),
        jnp.where(cell_code == 2, jnp.float32(fixed_cond), jnp.float32(0.0)),
    )
    base = store + river
    rhs = store * head_old + recharge + river * section
    trans_pad = with_halo(trans, (("strips", 0), ("depth", 1)), 1)
    head = head_old
    for sweep_id in range(SWEEPS):
        head_pad = with_halo(head, (("strips", 0), ("depth", 1)), 1)
        head = sweep(head_pad, trans_pad, base, rhs)
    full_head = lax.all_gather(head, "depth", axis=1, tiled=True)
    bottom = conduct[-1] * ((pressure[-1] - full_head) / (0.5 * layer_thick) + 1.0)
    lower_last = jnp.where(is_bottom, bottom, lower_last)
    lower = jnp.concatenate([inner, lower_last[None]], axis=0)
    moisture_new = moisture + soil_step / layer_thick * (upper - lower)
    return (moisture_new, head)


def solution(mesh):
    in_specs = (
        P("depth", "strips", None),
        P("depth", "strips", None),
        P("depth", "strips", None),
        P("strips", None),
        P(),
        P(),
        P(),
        P("strips", "depth"),
        P("strips", "depth"),
        P("strips", "depth"),
    )
    out_specs = (P("depth", "strips", None), P("strips", "depth"))
    return jax.shard_map(shards, mesh=mesh, in_specs=in_specs, out_specs=out_specs, check_vma=False)
```

profile of v0, /device:TPU:0, one launch (start us, length us, event | category | flops | bytes accessed | tf_op | source)
XLA Modules:
  0.0 189.5 jit_solution(8877950505763064282)
XLA Ops:
  7.2 0.0 all-reduce.3.cloned.1.call-start
  7.2 0.0 copy-start
  7.3 9.7 %broadcast_compare_fusion.11 = (pred[8,128,1024]{2,1,0:T(8,128)(4,1)S(1)}, pred[8,128,1024]{2,1,0:T(8,128)(4,1)S(1)}, pred[8,128,1024]{2,1,0:T(8,128)(4,1)S(1)},...) fusion(s32[8,128,1024]{2,1,0:T(8,128)} %param.11), kind=kLoop, calls=%fused_computation.23 | loop fusion | flops 12582912 | bytes 16777216 | tf_op jit(solution)/shard_map/eq | solution.py:43
  17.0 0.7 fusion.65
  17.7 0.7 fusion.64
  18.4 0.7 fusion.63
  19.1 0.0 copy-start.4
  19.1 0.0 copy-start.7
  19.1 0.0 copy-start.8
  19.1 40.2 %fusion.53 = (f32[128,1024]{1,0:T(8,128)}, f32[128,1024]{1,0:T(8,128)}, f32[128,1024]{1,0:T(8,128)}, f32[8,128,1024]{2,1,0:T(8,128)}, f32[8,128,1024]{2,1,0:T(8,128)}, /*index=5*/f32[8,128,1024]{2,1,0:T(8,128)}) fusion(pred[8,128,1024]{2,1,0:T(8,128)(4,1)S(1)} %get-tuple-element.27, f32[]{:T(128)} %bitcast.11, ...), kind=kLoop, calls=%fused_computation.123 | loop fusion | flops 86638592 | bytes 35127440 | tf_op jit(solution)/shard_map/reduce_sum | solution.py:86
  59.3 0.0 all-reduce.3.cloned.1.call-update
  59.4 1.4 collective-permute-start.6
  60.8 5.5 %collective-permute-start.7 = (f32[1,256]{1,0:T(1,128)S(1)}, f32[1,256]{1,0:T(1,128)S(1)}, u32[]{:S(2)}, u32[]{:S(2)}) collective-permute-start(f32[1,256]{1,0:T(1,128)S(1)} %get-tuple-element.43), channel_id=1, source_target_pairs={{0,1},{1,2},{2,3},{3,4},{4,5},{5,6},{6,7},{8,9},{9,10},{10,11},{11... | collective-permute-start | bytes 3080 | tf_op jit(solution)/shard_map/ppermute | solution.py:31
  66.3 0.0 collective-permute-done.6
  66.3 1.3 collective-permute-done.7
  67.6 37.9 %all-reduce.3.cloned.1.call-done = (f32[128,1024]{1,0:T(8,128)}, f32[128,1024]{1,0:T(8,128)}, f32[128,1024]{1,0:T(8,128)}) async-done(((f32[128,1024]{1,0:T(8,128)}, f32[128,1024]{1,0:T(8,128)}, f32[128,1024]{1,0:T(8,128)}), (f32[128,1024]{1,0:T(8,128)}, f32[128,1024]{1,0:T(8,128)}, f32[128,1024]{1,0:T(8,128)})) %all-reduce.3.cloned.1.call-update) | async-done | bytes 1572880 | tf_op jit(solution)/shard_map/psum | solution.py:90
  105.4 0.9 dynamic-slice_multiply_fusion
  106.4 1.3 collective-permute-start.2
  107.7 4.5 %collective-permute-start.3 = (f32[1,256]{1,0:T(1,128)S(1)}, f32[1,256]{1,0:T(1,128)S(1)}, u32[]{:S(2)}, u32[]{:S(2)}) collective-permute-start(f32[1,256]{1,0:T(1,128)S(1)} %get-tuple-element.41), channel_id=1, source_target_pairs={{0,1},{1,2},{2,3},{3,4},{4,5},{5,6},{6,7},{8,9},{9,10},{10,11},{11... | collective-permute-start | bytes 3080 | tf_op jit(solution)/shard_map/ppermute | solution.py:31
  112.2 0.1 fusion.58
  112.3 1.3 collective-permute-start.8
  113.6 3.0 %collective-permute-start.9 = (f32[130,1]{1,0:T(8,128)S(1)}, f32[130,1]{1,0:T(8,128)S(1)}, u32[]{:S(2)}, u32[]{:S(2)}) collective-permute-start(f32[130,1]{1,0:T(8,128)S(1)} %get-tuple-element.36), channel_id=1, source_target_pairs={{0,8},{8,16},{16,24},{1,9},{9,17},{17,25},{2,10},{10,18},{18,26},{... | collective-permute-start | bytes 1568 | tf_op jit(solution)/shard_map/ppermute | solution.py:31
  116.6 0.0 collective-permute-done.2
  116.7 0.0 collective-permute-done.3
  116.7 0.1 fusion.57
  116.8 1.3 collective-permute-start.4
  118.1 3.0 %collective-permute-start.5 = (f32[130,1]{1,0:T(8,128)S(1)}, f32[130,1]{1,0:T(8,128)S(1)}, u32[]{:S(2)}, u32[]{:S(2)}) collective-permute-start(f32[130,1]{1,0:T(8,128)S(1)} %get-tuple-element.33), channel_id=1, source_target_pairs={{0,8},{8,16},{16,24},{1,9},{9,17},{17,25},{2,10},{10,18},{18,26},{... | collective-permute-start | bytes 1568 | tf_op jit(solution)/shard_map/ppermute | solution.py:31
  121.1 0.0 collective-permute-done.8
  121.1 0.0 collective-permute-done.9
  121.1 0.0 collective-permute-done.4
  121.1 0.9 collective-permute-done.5
  122.0 1.4 fusion.38
  123.4 1.3 collective-permute-start.10
  124.7 4.9 %collective-permute-start.11 = (f32[1,256]{1,0:T(1,128)S(1)}, f32[1,256]{1,0:T(1,128)S(1)}, u32[]{:S(2)}, u32[]{:S(2)}) collective-permute-start(f32[1,256]{1,0:T(1,128)S(1)} %get-tuple-element.39), channel_id=1, source_target_pairs={{0,1},{1,2},{2,3},{3,4},{4,5},{5,6},{6,7},{8,9},{9,10},{10,11},{11... | collective-permute-start | bytes 3080 | tf_op jit(solution)/shard_map/ppermute | solution.py:31
  129.6 1.1 slice.339
  130.7 0.2 collective-permute-done.11
  130.9 0.1 fusion.56
  131.0 1.3 collective-permute-start.12
  132.3 4.2 %collective-permute-start.13 = (f32[130,1]{1,0:T(8,128)S(1)}, f32[130,1]{1,0:T(8,128)S(1)}, u32[]{:S(2)}, u32[]{:S(2)}) collective-permute-start(f32[130,1]{1,0:T(8,128)S(1)} %get-tuple-element.32), channel_id=1, source_target_pairs={{0,8},{8,16},{16,24},{1,9},{9,17},{17,25},{2,10},{10,18},{18,26},{... | collective-permute-start | bytes 1568 | tf_op jit(solution)/shard_map/ppermute | solution.py:31
  136.5 0.1 pad_maximum_fusion
  136.5 1.3 collective-permute-start
  137.8 0.0 collective-permute-done.12
  137.9 0.0 collective-permute-done.13
  137.9 1.3 fusion.28
  139.2 1.3 collective-permute-start.14
  140.5 5.2 %collective-permute-start.15 = (f32[1,256]{1,0:T(1,128)S(1)}, f32[1,256]{1,0:T(1,128)S(1)}, u32[]{:S(2)}, u32[]{:S(2)}) collective-permute-start(f32[1,256]{1,0:T(1,128)S(1)} %get-tuple-element.37), channel_id=1, source_target_pairs={{0,1},{1,2},{2,3},{3,4},{4,5},{5,6},{6,7},{8,9},{9,10},{10,11},{11... | collective-permute-start | bytes 3080 | tf_op jit(solution)/shard_map/ppermute | solution.py:31
  145.6 1.3 collective-permute-done.15
  146.9 0.1 fusion.55
  147.0 1.3 collective-permute-start.16
  148.3 5.4 %collective-permute-start.17 = (f32[130,1]{1,0:T(8,128)S(1)}, f32[130,1]{1,0:T(8,128)S(1)}, u32[]{:S(2)}, u32[]{:S(2)}) collective-permute-start(f32[130,1]{1,0:T(8,128)S(1)} %get-tuple-element.30), channel_id=1, source_target_pairs={{0,8},{8,16},{16,24},{1,9},{9,17},{17,25},{2,10},{10,18},{18,26},{... | collective-permute-start | bytes 1568 | tf_op jit(solution)/shard_map/ppermute | solution.py:31
  153.7 0.0 collective-permute-done.16
  153.7 0.9 collective-permute-done.17
  154.6 1.3 fusion.18
  155.9 0.0 copy-start.5
  155.9 11.0 %all_gather.3 = f32[128,1024]{1,0:T(8,128)S(1)} all-gather(f32[128,256]{1,0:T(8,128)S(1)} %fusion.18), channel_id=1, replica_groups=mesh['depth'=4,'strips'=8] {'depth'}, dimensions={1}, use_global_device_ids=true | all-gather | bytes 655360 | tf_op jit(solution)/shard_map/all_gather | solution.py:109
  166.9 2.3 %fusion.14 = (f32[1,128,1024]{2,1,0:T(8,128)S(1)}, f32[128,1024]{1,0:T(8,128)}) fusion(f32[128,1024]{1,0:T(8,128)S(1)} %all_gather.3, f32[8,128,1024]{2,1,0:T(8,128)} %get-tuple-element.16, f32[8,128,1024]{2,1,0:T(8,128)} %param.10, pred[]{:T(512)S(6)} %eq.91, f32[2,128,1024]{2,1,0:T(8,128)S(1)} %collective-permute-done), kind=kLoop, calls=%fused_computation.39 | loop fusion | flops 1441792 | bytes 3670017 | tf_op jit(solution)/shard_map/broadcast_in_dim | solution.py:112
  169.2 2.3 %collective-permute-start.1 = (f32[128,1024]{1,0:T(8,128)}, f32[128,1024]{1,0:T(8,128)S(1)}, u32[]{:S(2)}, u32[]{:S(2)}) collective-permute-start(f32[128,1024]{1,0:T(8,128)} %get-tuple-element.9), channel_id=1, source_target_pairs={{0,8},{8,16},{16,24},{1,9},{9,17},{17,25},{2,10},{10,18},{18,26},{... | collective-permute-start | bytes 1572872 | tf_op jit(solution)/shard_map/ppermute | solution.py:20
  171.5 0.0 copy-start.6
  171.5 0.0 copy-start.1
  171.5 7.3 %fusion.3 = f32[7,128,1024]{2,1,0:T(8,128)S(1)} fusion(f32[8,128,1024]{2,1,0:T(8,128)} %get-tuple-element.16, f32[8,128,1024]{2,1,0:T(8,128)} %param.10), kind=kLoop, calls=%fused_computation.11 | loop fusion | flops 5505024 | bytes 18350080 | tf_op jit(solution)/shard_map/mul | solution.py:48
  178.8 0.0 collective-permute-done.1
  178.8 0.1 select_bitcast_fusion
  178.9 0.5 copy-done.2
  179.4 3.3 %fusion.1 = f32[8,128,1024]{2,1,0:T(8,128)} fusion(f32[7,128,1024]{2,1,0:T(8,128)S(1)} %fusion.3, f32[1,128,1024]{2,1,0:T(8,128)S(1)} %select_bitcast_fusion, f32[1,128,1024]{2,1,0:T(8,128)S(1)} %get-tuple-element.8, f32[8,128,1024]{2,1,0:T(8,128)S(1)} %copy-done.1, f32[8,128,1024]{2,1,0:T(8,128)S(1)} %copy-done.2), kind=kLoop, calls=%fused_computation.2 | loop fusion | flops 8388608 | bytes 17301504 | tf_op jit(solution)/shard_map/add | solution.py:113
  (29 shorter events, 0.1 us)
Async XLA Ops:
  7.2 9.8 %copy-start.9 = (f32[12]{0:T(128)S(1)}, f32[12]{0:T(128)}, u32[]{:S(2)}) copy-start(f32[12]{0:T(128)} %param.16) | copy-start | bytes 148
  7.2 10.5 %copy-start.10 = (f32[12]{0:T(128)S(1)}, f32[12]{0:T(128)}, u32[]{:S(2)}) copy-start(f32[12]{0:T(128)} %param.15) | copy-start | bytes 148
  7.2 11.2 %copy-start.11 = (f32[12]{0:T(128)S(1)}, f32[12]{0:T(128)}, u32[]{:S(2)}) copy-start(f32[12]{0:T(128)} %param.14) | copy-start | bytes 148
  7.2 98.2 %all-reduce.3.cloned.1.call-start = ((), (), s32[]{:S(2)}) async-start(), calls=%async_computation | async-start | bytes 3145728 | tf_op jit(solution)/shard_map/psum | solution.py:90
  7.2 11.8 %copy-start = (f32[8,128,1024]{2,1,0:T(8,128)S(1)}, f32[8,128,1024]{2,1,0:T(8,128)}, u32[]{:S(2)}) copy-start(f32[8,128,1024]{2,1,0:T(8,128)} %param.10) | copy-start | bytes 12582916
  7.3 11.8 %copy-start.3 = (s32[8,128,1024]{2,1,0:T(8,128)S(1)}, s32[8,128,1024]{2,1,0:T(8,128)}, u32[]{:S(2)}) copy-start(s32[8,128,1024]{2,1,0:T(8,128)} %param.12) | copy-start | bytes 12582916
  19.1 40.2 %copy-start.4 = (f32[128,256]{1,0:T(8,128)S(1)}, f32[128,256]{1,0:T(8,128)}, u32[]{:S(2)}) copy-start(f32[128,256]{1,0:T(8,128)} %param.17) | copy-start | bytes 393220
  19.1 102.9 %copy-start.7 = (f32[128,256]{1,0:T(8,128)S(1)}, f32[128,256]{1,0:T(8,128)}, u32[]{:S(2)}) copy-start(f32[128,256]{1,0:T(8,128)} %param.19) | copy-start | bytes 393220
  19.1 102.9 %copy-start.8 = (s32[128,256]{1,0:T(8,128)S(1)}, s32[128,256]{1,0:T(8,128)}, u32[]{:S(2)}) copy-start(s32[128,256]{1,0:T(8,128)} %param.18) | copy-start | bytes 393220
  59.3 77.1 %slice-start = ((f32[8,128,1024]{2,1,0:T(8,128)}), f32[1,128,1024]{2,1,0:T(8,128)S(1)}, s32[]{:S(2)}) async-start(f32[8,128,1024]{2,1,0:T(8,128)} %param.10), calls=%async_computation.1 | async-start | bytes 1048576 | tf_op jit(solution)/shard_map/slice | solution.py:80
  59.4 6.9 %collective-permute-start.6 = (f32[1,256]{1,0:T(1,128)S(1)}, f32[1,256]{1,0:T(1,128)S(1)}, u32[]{:S(2)}, u32[]{:S(2)}) collective-permute-start(f32[1,256]{1,0:T(1,128)S(1)} %get-tuple-element.44), channel_id=1, source_target_pairs={{1,0},{2,1},{3,2},{4,3},{5,4},{6,5},{7,6},{9,8},{10,9},{11,10},{12... | collective-permute-start | bytes 3080 | tf_op jit(solution)/shard_map/ppermute | solution.py:33
  60.8 6.8 %collective-permute-start.7 = (f32[1,256]{1,0:T(1,128)S(1)}, f32[1,256]{1,0:T(1,128)S(1)}, u32[]{:S(2)}, u32[]{:S(2)}) collective-permute-start(f32[1,256]{1,0:T(1,128)S(1)} %get-tuple-element.43), channel_id=1, source_target_pairs={{0,1},{1,2},{2,3},{3,4},{4,5},{5,6},{6,7},{8,9},{9,10},{10,11},{11... | collective-permute-start | bytes 3080 | tf_op jit(solution)/shard_map/ppermute | solution.py:31
  106.4 10.3 %collective-permute-start.2 = (f32[1,256]{1,0:T(1,128)S(1)}, f32[1,256]{1,0:T(1,128)S(1)}, u32[]{:S(2)}, u32[]{:S(2)}) collective-permute-start(f32[1,256]{1,0:T(1,128)S(1)} %get-tuple-element.42), channel_id=1, source_target_pairs={{1,0},{2,1},{3,2},{4,3},{5,4},{6,5},{7,6},{9,8},{10,9},{11,10},{12... | collective-permute-start | bytes 3080 | tf_op jit(solution)/shard_map/ppermute | solution.py:33
  107.7 9.0 %collective-permute-start.3 = (f32[1,256]{1,0:T(1,128)S(1)}, f32[1,256]{1,0:T(1,128)S(1)}, u32[]{:S(2)}, u32[]{:S(2)}) collective-permute-start(f32[1,256]{1,0:T(1,128)S(1)} %get-tuple-element.41), channel_id=1, source_target_pairs={{0,1},{1,2},{2,3},{3,4},{4,5},{5,6},{6,7},{8,9},{9,10},{10,11},{11... | collective-permute-start | bytes 3080 | tf_op jit(solution)/shard_map/ppermute | solution.py:31
  112.3 8.8 %collective-permute-start.8 = (f32[130,1]{1,0:T(8,128)S(1)}, f32[130,1]{1,0:T(8,128)S(1)}, u32[]{:S(2)}, u32[]{:S(2)}) collective-permute-start(f32[130,1]{1,0:T(8,128)S(1)} %get-tuple-element.35), channel_id=1, source_target_pairs={{8,0},{16,8},{24,16},{9,1},{17,9},{25,17},{10,2},{18,10},{26,18},{... | collective-permute-start | bytes 1568 | tf_op jit(solution)/shard_map/ppermute | solution.py:33
  113.6 7.5 %collective-permute-start.9 = (f32[130,1]{1,0:T(8,128)S(1)}, f32[130,1]{1,0:T(8,128)S(1)}, u32[]{:S(2)}, u32[]{:S(2)}) collective-permute-start(f32[130,1]{1,0:T(8,128)S(1)} %get-tuple-element.36), channel_id=1, source_target_pairs={{0,8},{8,16},{16,24},{1,9},{9,17},{17,25},{2,10},{10,18},{18,26},{... | collective-permute-start | bytes 1568 | tf_op jit(solution)/shard_map/ppermute | solution.py:31
  116.8 4.4 %collective-permute-start.4 = (f32[130,1]{1,0:T(8,128)S(1)}, f32[130,1]{1,0:T(8,128)S(1)}, u32[]{:S(2)}, u32[]{:S(2)}) collective-permute-start(f32[130,1]{1,0:T(8,128)S(1)} %get-tuple-element.34), channel_id=1, source_target_pairs={{8,0},{16,8},{24,16},{9,1},{17,9},{25,17},{10,2},{18,10},{26,18},{... | collective-permute-start | bytes 1568 | tf_op jit(solution)/shard_map/ppermute | solution.py:33
  118.1 3.9 %collective-permute-start.5 = (f32[130,1]{1,0:T(8,128)S(1)}, f32[130,1]{1,0:T(8,128)S(1)}, u32[]{:S(2)}, u32[]{:S(2)}) collective-permute-start(f32[130,1]{1,0:T(8,128)S(1)} %get-tuple-element.33), channel_id=1, source_target_pairs={{0,8},{8,16},{16,24},{1,9},{9,17},{17,25},{2,10},{10,18},{18,26},{... | collective-permute-start | bytes 1568 | tf_op jit(solution)/shard_map/ppermute | solution.py:31
  123.4 7.3 %collective-permute-start.10 = (f32[1,256]{1,0:T(1,128)S(1)}, f32[1,256]{1,0:T(1,128)S(1)}, u32[]{:S(2)}, u32[]{:S(2)}) collective-permute-start(f32[1,256]{1,0:T(1,128)S(1)} %get-tuple-element.40), channel_id=1, source_target_pairs={{1,0},{2,1},{3,2},{4,3},{5,4},{6,5},{7,6},{9,8},{10,9},{11,10},{12... | collective-permute-start | bytes 3080 | tf_op jit(solution)/shard_map/ppermute | solution.py:33
  124.7 6.2 %collective-permute-start.11 = (f32[1,256]{1,0:T(1,128)S(1)}, f32[1,256]{1,0:T(1,128)S(1)}, u32[]{:S(2)}, u32[]{:S(2)}) collective-permute-start(f32[1,256]{1,0:T(1,128)S(1)} %get-tuple-element.39), channel_id=1, source_target_pairs={{0,1},{1,2},{2,3},{3,4},{4,5},{5,6},{6,7},{8,9},{9,10},{10,11},{11... | collective-permute-start | bytes 3080 | tf_op jit(solution)/shard_map/ppermute | solution.py:31
  131.0 6.9 %collective-permute-start.12 = (f32[130,1]{1,0:T(8,128)S(1)}, f32[130,1]{1,0:T(8,128)S(1)}, u32[]{:S(2)}, u32[]{:S(2)}) collective-permute-start(f32[130,1]{1,0:T(8,128)S(1)} %get-tuple-element.31), channel_id=1, source_target_pairs={{8,0},{16,8},{24,16},{9,1},{17,9},{25,17},{10,2},{18,10},{26,18},{... | collective-permute-start | bytes 1568 | tf_op jit(solution)/shard_map/ppermute | solution.py:33
  132.3 5.6 %collective-permute-start.13 = (f32[130,1]{1,0:T(8,128)S(1)}, f32[130,1]{1,0:T(8,128)S(1)}, u32[]{:S(2)}, u32[]{:S(2)}) collective-permute-start(f32[130,1]{1,0:T(8,128)S(1)} %get-tuple-element.32), channel_id=1, source_target_pairs={{0,8},{8,16},{16,24},{1,9},{9,17},{17,25},{2,10},{10,18},{18,26},{... | collective-permute-start | bytes 1568 | tf_op jit(solution)/shard_map/ppermute | solution.py:31
  136.5 30.3 %collective-permute-start = (f32[2,128,1024]{2,1,0:T(8,128)S(1)}, f32[2,128,1024]{2,1,0:T(8,128)S(1)}, u32[]{:S(2)}, u32[]{:S(2)}) collective-permute-start(f32[2,128,1024]{2,1,0:T(8,128)S(1)} %pad_maximum_fusion), channel_id=1, source_target_pairs={{8,0},{16,8},{24,16},{9,1},{17,9},{25,17},{10,2},{18,10},{26,18},{... | collective-permute-start | bytes 3145736 | tf_op jit(solution)/shard_map/ppermute | solution.py:20
  139.2 6.5 %collective-permute-start.14 = (f32[1,256]{1,0:T(1,128)S(1)}, f32[1,256]{1,0:T(1,128)S(1)}, u32[]{:S(2)}, u32[]{:S(2)}) collective-permute-start(f32[1,256]{1,0:T(1,128)S(1)} %get-tuple-element.38), channel_id=1, source_target_pairs={{1,0},{2,1},{3,2},{4,3},{5,4},{6,5},{7,6},{9,8},{10,9},{11,10},{12... | collective-permute-start | bytes 3080 | tf_op jit(solution)/shard_map/ppermute | solution.py:33
  140.5 6.5 %collective-permute-start.15 = (f32[1,256]{1,0:T(1,128)S(1)}, f32[1,256]{1,0:T(1,128)S(1)}, u32[]{:S(2)}, u32[]{:S(2)}) collective-permute-start(f32[1,256]{1,0:T(1,128)S(1)} %get-tuple-element.37), channel_id=1, source_target_pairs={{0,1},{1,2},{2,3},{3,4},{4,5},{5,6},{6,7},{8,9},{9,10},{10,11},{11... | collective-permute-start | bytes 3080 | tf_op jit(solution)/shard_map/ppermute | solution.py:31
  147.0 6.7 %collective-permute-start.16 = (f32[130,1]{1,0:T(8,128)S(1)}, f32[130,1]{1,0:T(8,128)S(1)}, u32[]{:S(2)}, u32[]{:S(2)}) collective-permute-start(f32[130,1]{1,0:T(8,128)S(1)} %get-tuple-element.29), channel_id=1, source_target_pairs={{8,0},{16,8},{24,16},{9,1},{17,9},{25,17},{10,2},{18,10},{26,18},{... | collective-permute-start | bytes 1568 | tf_op jit(solution)/shard_map/ppermute | solution.py:33
  148.3 6.3 %collective-permute-start.17 = (f32[130,1]{1,0:T(8,128)S(1)}, f32[130,1]{1,0:T(8,128)S(1)}, u32[]{:S(2)}, u32[]{:S(2)}) collective-permute-start(f32[130,1]{1,0:T(8,128)S(1)} %get-tuple-element.30), channel_id=1, source_target_pairs={{0,8},{8,16},{16,24},{1,9},{9,17},{17,25},{2,10},{10,18},{18,26},{... | collective-permute-start | bytes 1568 | tf_op jit(solution)/shard_map/ppermute | solution.py:31
  155.9 22.9 %copy-start.5 = (f32[128,256]{1,0:T(8,128)}, f32[128,256]{1,0:T(8,128)S(1)}, u32[]{:S(2)}) copy-start(f32[128,256]{1,0:T(8,128)S(1)} %fusion.18) | copy-start | bytes 393220
  169.2 9.6 %collective-permute-start.1 = (f32[128,1024]{1,0:T(8,128)}, f32[128,1024]{1,0:T(8,128)S(1)}, u32[]{:S(2)}, u32[]{:S(2)}) collective-permute-start(f32[128,1024]{1,0:T(8,128)} %get-tuple-element.9), channel_id=1, source_target_pairs={{0,8},{8,16},{16,24},{1,9},{9,17},{17,25},{2,10},{10,18},{18,26},{... | collective-permute-start | bytes 1572872 | tf_op jit(solution)/shard_map/ppermute | solution.py:20
  171.5 7.3 %copy-start.6 = (f32[128,1024]{1,0:T(8,128)S(1)}, f32[128,1024]{1,0:T(8,128)}, u32[]{:S(2)}) copy-start(f32[128,1024]{1,0:T(8,128)} %param.13) | copy-start | bytes 1572868
  171.5 7.4 %copy-start.1 = (f32[8,128,1024]{2,1,0:T(8,128)S(1)}, f32[8,128,1024]{2,1,0:T(8,128)}, u32[]{:S(2)}) copy-start(f32[8,128,1024]{2,1,0:T(8,128)} %get-tuple-element.14) | copy-start | bytes 12582916
  171.5 7.9 %copy-start.2 = (f32[8,128,1024]{2,1,0:T(8,128)S(1)}, f32[8,128,1024]{2,1,0:T(8,128)}, u32[]{:S(2)}) copy-start(f32[8,128,1024]{2,1,0:T(8,128)} %get-tuple-element.15) | copy-start | bytes 12582916
Sparse Core Ops, SparseCore 0:
  59.5 45.9 all-reduce.2
where the time goes:
time: 193 us; the launch traced here: 190 us
  other arithmetic  67.8 us (35%)
  starting transfers between devices  49.8 us (26%)
  waiting for transfers between devices  42.3 us (22%)
  between operations  14.5 us (8%)
  blocking collectives  11 us (6%)
  local copies, waits for them, and re-layouts  4.04 us (2%)
    reduce_sum x1, other arithmetic, shards(): trans_part = jnp.sum(conduct, axis=0)  40.2 us
    psum x1, waiting for transfers between devices, shards(): summed = lax.psum((trans_part, store_part, charge_part), 'depth')  37.9 us
    ppermute x8, starting transfers between devices, with_halo(): lax.ppermute(tail, axis, [(i, (i + 1) % count) for i in range(ends)])  35.7 us
    all_gather x1, blocking collectives, shards(): full_head = lax.all_gather(head, 'depth', axis=1, tiled=True)  11 us
    ppermute x8, starting transfers between devices, with_halo(): lax.ppermute(head, axis, [((i + 1) % count, i) for i in range(ends)])  10.5 us
    eq x1, other arithmetic, lookup(): texture == class_id  9.72 us
    mul x1, other arithmetic, face_flux(): return 0.5 * (cond_up + cond_low) * ((psi_up - psi_low) / layer_thick + 1.0)  7.25 us
    ppermute x8, waiting for transfers between devices, with_halo(): lax.ppermute(tail, axis, [(i, (i + 1) % count) for i in range(ends)])  4.45 us
  transfers between devices with their start and end apart: 19, of which 6 were waited for; matrix products, arithmetic and copies ran while one was open for 6% of the time, Pallas kernels for 0%

commit v1 on v0

v1 whole, which is shorter than its diff:
```python
import functools
import math

import jax
import jax.numpy as jnp
from jax import lax
from jax.experimental import pallas as pl
from jax.experimental.pallas import tpu as pltpu
from jax.sharding import PartitionSpec as P

SWEEPS = 3
SUB = 8
LANE = 128

layer_thick = 0.05
soil_step = 0.0002
spec_yield = 0.02
leak_rate = 0.5
river_cond = 0.5
fixed_cond = 3.0
residual = 0.15
mobile = 0.85

VMEM = pl.BlockSpec(memory_space=pltpu.VMEM)
ANY = pl.BlockSpec(memory_space=pl.ANY)


def params(mib):
    return pltpu.CompilerParams(vmem_limit_bytes=mib * 2**20)


def cost(flops, nbytes, trans=0):
    return pl.CostEstimate(flops=int(flops), bytes_accessed=int(nbytes), transcendentals=int(trans))


def place():
    depth = lax.axis_index("depth")
    return depth // 2, depth % 2


def gathered(table, classes):
    return jnp.take_along_axis(table, classes, axis=1, mode="promise_in_bounds")


def picked(options, bits):
    for bit in bits:
        options = [
            jnp.where(bit, options[i + 1], options[i]) if i + 1 < len(options) else options[i]
            for i in range(0, len(options), 2)
        ]
    return options[0]


def soil_kernel(
    sat_ref, alpha_ref, theta_ref, psi_ref, tex_ref, act_ref,
    moist_ref, keep_ref, send_ref, core_ref, chip_ref, tab, part,
):
    step = pl.program_id(0)
    _, core = place()
    layers, rows, cols = psi_ref.shape
    classes = sat_ref.shape[1]

    @pl.when(step == 0)
    def _():
        for i, (ref, scale) in enumerate(
            ((sat_ref, 1.0), (alpha_ref, 0.5 * math.log2(math.e)), (theta_ref, mobile))
        ):
            tab[i, :, :classes] = jnp.broadcast_to(ref[...] * scale, (SUB, classes))

    sat_tab, par_tab = tab[0], tab[1]
    theta = [jnp.broadcast_to(tab[2, :, i : i + 1], (SUB, LANE)) for i in range(classes)]
    nbits = max(1, (classes - 1).bit_length())
    face = 0.5 * soil_step / layer_thick
    core_layer = (1 - core) * (layers - 1)
    chip_layer = core * (layers - 1)

    def columns(q, carry):
        lanes = pl.ds(pl.multiple_of(q * LANE, LANE), LANE)
        for r in range(0, rows, SUB):
            rws = slice(r, r + SUB)
            trans = store = charge = jnp.zeros((SUB, LANE), jnp.float32)
            for layer in range(layers):
                kind = tex_ref[layer, rws, lanes]
                psi = psi_ref[layer, rws, lanes]
                active = act_ref[layer, rws, lanes].astype(jnp.float32)
                bits = [(kind & (1 << b)) != 0 for b in range(nbits)]
                wet = jnp.exp2(gathered(par_tab, kind) * jnp.minimum(psi, 0.0))
                cond = gathered(sat_tab, kind) * active * (wet * wet)
                mob = picked(theta, bits)
                mobwet = mob * wet
                trans = trans + cond
                charge = charge + cond * wet
                store = store + (mob - mobwet)
                held = mob * (residual / mobile) + mobwet
                if layer == 0:
                    first, own = cond, held
                else:
                    flux = (cond_up + cond) * ((psi_up - psi) * (face / layer_thick) + face)
                    moist_ref[layer - 1, rws, lanes] = own - flux
                    own = held + flux
                psi_up, cond_up = psi, cond
            moist_ref[layers - 1, rws, lanes] = own
            part[r // SUB, 0, :, lanes] = trans
            part[r // SUB, 1, :, lanes] = store
            part[r // SUB, 2, :, lanes] = charge
            core_ref[0, rws, lanes] = psi_ref[core_layer, rws, lanes]
            core_ref[1, rws, lanes] = jnp.where(core == 0, cond, first)
            chip_ref[0, rws, lanes] = psi_ref[chip_layer, rws, lanes]
            chip_ref[1, rws, lanes] = jnp.where(core == 0, first, cond)
        return carry

    lax.fori_loop(0, cols // LANE, columns, 0, unroll=2)

    blocks = rows // SUB
    half = keep_ref.shape[0] - 1
    for r in range(blocks):
        block = step * blocks + r

        def put(ref, at):
            ref[at] = part[r]

        @pl.when((block <= half) & (core == 0))
        def _():
            put(keep_ref, block)

        @pl.when((block <= half) & (core == 1))
        def _():
            put(send_ref, block)

        @pl.when((block >= half - 1) & (core == 0))
        def _():
            put(send_ref, block - (half - 1))

        @pl.when((block >= half - 1) & (core == 1))
        def _():
            put(keep_ref, block - (half - 1))


def soil(k_sat, alpha, theta_sat, pressure, texture, active):
    layers, nrows, cols = pressure.shape
    classes = k_sat.shape[0]
    rows = nrows // 4
    blocks = nrows // (2 * SUB) + 1
    whole = pl.BlockSpec((1, classes), lambda j: (0, 0))
    block = pl.BlockSpec((layers, rows, cols), lambda j: (0, j, 0))
    pair = pl.BlockSpec((2, rows, cols), lambda j: (0, j, 0))
    msg = jax.ShapeDtypeStruct((blocks, 3, SUB, cols), jnp.float32)
    msg_spec = pl.BlockSpec((blocks, 3, SUB, cols), lambda j: (0, 0, 0, 0))
    layer2 = jax.ShapeDtypeStruct((2, nrows, cols), jnp.float32)
    size = layers * nrows * cols
    return pl.pallas_call(
        soil_kernel,
        grid=(nrows // rows,),
        in_specs=[whole, whole, whole, block, block, block],
        out_specs=[block, msg_spec, msg_spec, pair, pair],
        out_shape=[jax.ShapeDtypeStruct((layers, nrows, cols), jnp.float32), msg, msg, layer2, layer2],
        scratch_shapes=[
            pltpu.VMEM((3, SUB, LANE), jnp.float32),
            pltpu.VMEM((rows // SUB, 3, SUB, cols), jnp.float32),
        ],
        compiler_params=params(56),
        cost_estimate=cost(60 * size, 20 * size, size),
        name="soil",
    )(k_sat[None], alpha[None], theta_sat[None], pressure, texture, active)


def lane_group(shape, start):
    lane = lax.broadcasted_iota(jnp.int32, shape, len(shape) - 1)
    return (lane >= start) & (lane < start + SUB)


def edge_lane(chip):
    return (1 - chip) * (LANE - SUB)


def tile_rows(own_ref, other_ref, core, which, array, first, width):
    mine = own_ref[array, pl.ds(first, SUB), width[0] : width[0] + width[1]]
    theirs = other_ref[array, pl.ds(first, SUB), width[0] : width[0] + width[1]]
    return jnp.where(core == which, mine, theirs)


def pack_kernel(keep_ref, recv_ref, own_ref, other_ref, out_ref, edge_ref):
    chip, core = place()
    blocks, _, _, cols = keep_ref.shape
    half = cols // 2
    tile = half // 2
    away = pl.ds(pl.multiple_of((1 - chip) * half, half), half)
    edge = core * (blocks - 1)
    for j in range(blocks - 1):
        b = j + (1 - core)
        out_ref[j] = keep_ref[b, :, :, away] + recv_ref[b, :, :, away]
    edge_ref[:3] = keep_ref[edge, :, :, away] + recv_ref[edge, :, :, away]
    slab = pl.ds(pl.multiple_of(half - LANE + chip * LANE, LANE), LANE)
    per = half // LANE
    base = edge_lane(chip)
    shape = (SUB, LANE)
    for b in range(blocks):
        first = pl.multiple_of(core * (blocks - 2) * SUB + b * SUB, SUB)
        packed = jnp.zeros(shape, jnp.float32)
        for a in range(6):
            if a < 3:
                piece = keep_ref[b, a, :, slab] + recv_ref[b, a, :, slab]
            else:
                left = tile_rows(own_ref, other_ref, core, 1, a - 3, first, (tile - LANE, LANE))
                right = tile_rows(own_ref, other_ref, core, 0, a - 3, first, (0, LANE))
                piece = jnp.where(chip == 0, left, right)
            piece = jnp.where(lane_group(shape, base), piece, 0.0)
            packed = packed + (pltpu.roll(piece, SUB * a, 1) if a else piece)
        edge_ref[3 + b // per, :, (b % per) * LANE : (b % per + 1) * LANE] = packed


def pack(keep, recv, own, other):
    blocks, _, _, cols = keep.shape
    half = cols // 2
    planes = 3 + -(-blocks // (half // LANE))
    return pl.pallas_call(
        pack_kernel,
        in_specs=[VMEM] * 4,
        out_specs=[VMEM] * 2,
        out_shape=[
            jax.ShapeDtypeStruct((blocks - 1, 3, SUB, half), jnp.float32),
            jax.ShapeDtypeStruct((planes, SUB, half), jnp.float32),
        ],
        compiler_params=params(24),
        cost_estimate=cost(keep.size, 12 * keep.size),
        name="pack",
    )(keep, recv, own, other)


def cells(keep_ref, recv_ref, own_ref, other_ref, far_ref, edge_ref, b, chip, core, put):
    blocks, _, _, cols = keep_ref.shape
    half = cols // 2
    tile = half // 2
    per = half // LANE
    near = pl.ds(pl.multiple_of(chip * half, half), half)
    first = pl.multiple_of(core * (blocks - 2) * SUB + b * SUB, SUB)

    def finish(sums, old, river, inflow, mask):
        trans = sums[0] * layer_thick
        store = spec_yield + sums[1] * layer_thick
        base = store + river
        rhs = store * old + leak_rate * layer_thick * sums[2] + inflow
        if mask is None:
            return trans, base, rhs, old
        zero = jnp.zeros_like(trans)
        return (
            jnp.where(mask, trans, zero),
            jnp.where(mask, base, zero + 1.0),
            jnp.where(mask, rhs, zero),
            jnp.where(mask, old, zero),
        )

    sums = [keep_ref[b, a, :, near] + recv_ref[b, a, :, near] + far_ref(a) for a in range(3)]
    for which in range(2):
        lanes = slice(which * tile, (which + 1) * tile)
        ins = [tile_rows(own_ref, other_ref, core, which, a, first, (0, tile)) for a in range(3)]
        for i, value in enumerate(finish([s[:, lanes] for s in sums], *ins, None)):
            put(i, lanes, value)
    slab = pl.ds(pl.multiple_of(half - chip * LANE, LANE), LANE)
    shape = (SUB, LANE)
    base = edge_lane(1 - chip)
    plane = 3 + b // per
    at = pl.ds(pl.multiple_of((b % per) * LANE, LANE), LANE)
    packed = edge_ref[plane, :, at]
    unpacked = [pltpu.roll(packed, LANE - SUB * a, 1) if a else packed for a in range(6)]
    sums = [keep_ref[b, a, :, slab] + recv_ref[b, a, :, slab] + unpacked[a] for a in range(3)]
    for i, value in enumerate(finish(sums, *unpacked[3:], lane_group(shape, base))):
        put(i, slice(half, half + LANE), value)


def rim_kernel(keep_ref, recv_ref, own_ref, other_ref, edge_ref, out_ref):
    chip, core = place()
    blocks = keep_ref.shape[0]

    def put(i, lanes, value):
        out_ref[i, :, lanes] = value

    cells(
        keep_ref, recv_ref, own_ref, other_ref, lambda a: edge_ref[a], edge_ref,
        core * (blocks - 1), chip, core, put,
    )


def rim(keep, recv, own, other, edge):
    half = keep.shape[3] // 2
    return pl.pallas_call(
        rim_kernel,
        in_specs=[VMEM] * 5,
        out_specs=VMEM,
        out_shape=jax.ShapeDtypeStruct((4, SUB, half + LANE), jnp.float32),
        compiler_params=params(24),
        cost_estimate=cost(keep.size, 8 * keep.size),
        name="rim",
    )(keep, recv, own, other, edge)


def sweep_kernel(keep_ref, recv_ref, own_ref, other_ref, far_ref, edge_ref, rim_ref, out_ref, work):
    chip, core = place()
    strip = lax.axis_index("strips")
    blocks = keep_ref.shape[0]
    half = keep_ref.shape[3] // 2
    edge = core * (blocks - 1)
    for b in range(blocks):
        row = jnp.clip(b - (1 - core), 0, blocks - 2)

        def far(a):
            return jnp.where(b == edge, edge_ref[a], far_ref[row, a])

        def put(i, lanes, value):
            work[i, b * SUB : (b + 1) * SUB, lanes] = value

        cells(keep_ref, recv_ref, own_ref, other_ref, far, edge_ref, b, chip, core, put)
    outside = ((core == 0) & (strip == 0)) | ((core == 1) & (strip == lax.axis_size("strips") - 1))
    for i in range(4):
        work[i, blocks * SUB :, :] = jnp.where(outside, 1.0 if i == 1 else 0.0, rim_ref[i])

    trans, base, rhs, head = (work[i] for i in range(4))
    rows, lanes = trans.shape
    right = jnp.sqrt(trans * pltpu.roll(trans, lanes - 1, 1))
    left = pltpu.roll(right, 1, 1)
    down = jnp.sqrt(trans * pltpu.roll(trans, rows - 1, 0))
    up = pltpu.roll(down, 1, 0)
    inverse = 1.0 / (base + right + left + down + up)
    for _ in range(SWEEPS):
        head = inverse * (
            rhs
            + right * pltpu.roll(head, lanes - 1, 1)
            + left * pltpu.roll(head, 1, 1)
            + down * pltpu.roll(head, rows - 1, 0)
            + up * pltpu.roll(head, 1, 0)
        )
    work[0] = head
    out_ref[...] = work[0, pl.ds(pl.multiple_of(core * SUB, SUB), out_ref.shape[0]), :half]


def sweeps(keep, recv, own, other, far, edge, rim_rows):
    blocks = keep.shape[0]
    half = keep.shape[3] // 2
    return pl.pallas_call(
        sweep_kernel,
        in_specs=[VMEM] * 7,
        out_specs=VMEM,
        out_shape=jax.ShapeDtypeStruct(((blocks - 1) * SUB, half), jnp.float32),
        scratch_shapes=[pltpu.VMEM((4, (blocks + 1) * SUB, half + LANE), jnp.float32)],
        compiler_params=params(24),
        cost_estimate=cost(20 * keep.size, 12 * keep.size),
        name="sweeps",
    )(keep, recv, own, other, far, edge, rim_rows)


def faces_kernel(moist_in, core_ref, chip_ref, core_far, chip_far, rain_ref, moist_out, ends, sems):
    del moist_in
    chip, core = place()
    layers = moist_out.shape[0]
    loads = [
        pltpu.make_async_copy(moist_out.at[layer], ends.at[i], sems.at[i])
        for i, layer in enumerate((0, layers - 1))
    ]
    for c in loads:
        c.start()
    for c in loads:
        c.wait()
    gain = soil_step / layer_thick
    face = 0.5 * gain

    def flux(upper, lower):
        return (upper[1] + lower[1]) * ((upper[0] - lower[0]) * (face / layer_thick) + face)

    @pl.when(core == 0)
    def _():
        ends[1] = ends[1] - flux(core_ref, core_far)

    @pl.when(core == 1)
    def _():
        ends[0] = ends[0] + flux(core_far, core_ref)

    @pl.when((core == 0) & (chip == 0))
    def _():
        ends[0] = ends[0] + gain * rain_ref[...]

    @pl.when((core == 0) & (chip == 1))
    def _():
        ends[0] = ends[0] + flux(chip_far, chip_ref)

    @pl.when((core == 1) & (chip == 0))
    def _():
        ends[1] = ends[1] - flux(chip_ref, chip_far)

    stores = [
        pltpu.make_async_copy(ends.at[i], moist_out.at[layer], sems.at[i])
        for i, layer in enumerate((0, layers - 1))
    ]
    for c in stores:
        c.start()
    for c in stores:
        c.wait()


def faces(moist, core_pair, chip_pair, core_far, chip_far, rain):
    return pl.pallas_call(
        faces_kernel,
        in_specs=[ANY] + [VMEM] * 5,
        out_specs=ANY,
        out_shape=jax.ShapeDtypeStruct(moist.shape, moist.dtype),
        input_output_aliases={0: 0},
        scratch_shapes=[pltpu.VMEM((2,) + moist.shape[1:], jnp.float32), pltpu.SemaphoreType.DMA((2,))],
        compiler_params=params(24),
        cost_estimate=cost(20 * rain.size, 32 * rain.size),
        name="faces",
    )(moist, core_pair, chip_pair, core_far, chip_far, rain)


def bottom_kernel(
    moist_in, chip_pair, own_ref, core_far, chip_far, both_far, moist_out, head_ref, last, sem
):
    del moist_in
    chip, core = place()
    layers = moist_out.shape[0]
    rows, half = own_ref.shape
    tile = half // 2
    mine = pl.ds(pl.multiple_of(core * rows, rows), rows)
    theirs = pl.ds(pl.multiple_of((1 - core) * rows, rows), rows)

    @pl.when((core == 1) & (chip == 1))
    def _():
        load = pltpu.make_async_copy(moist_out.at[layers - 1], last, sem)
        load.start()
        load.wait()
        gain = soil_step / layer_thick
        for ref, where, lanes in (
            (own_ref, mine, slice(half, 2 * half)),
            (core_far, theirs, slice(half, 2 * half)),
            (chip_far, mine, slice(0, half)),
            (both_far, theirs, slice(0, half)),
        ):
            drop = (chip_pair[0, where, lanes] - ref[...]) / (0.5 * layer_thick) + 1.0
            last[where, lanes] = last[where, lanes] - gain * chip_pair[1, where, lanes] * drop
        store = pltpu.make_async_copy(last, moist_out.at[layers - 1], sem)
        store.start()
        store.wait()

    lanes = pl.ds(pl.multiple_of(core * tile, tile), tile)
    head_ref[mine, :] = own_ref[:, lanes]
    head_ref[theirs, :] = core_far[:, lanes]


def bottom(moist, chip_pair, own, core_far, chip_far, both_far):
    rows, half = own.shape
    return pl.pallas_call(
        bottom_kernel,
        in_specs=[ANY] + [VMEM] * 5,
        out_specs=[ANY, VMEM],
        out_shape=[
            jax.ShapeDtypeStruct(moist.shape, moist.dtype),
            jax.ShapeDtypeStruct((2 * rows, half // 2), jnp.float32),
        ],
        input_output_aliases={0: 0},
        scratch_shapes=[pltpu.VMEM(moist.shape[1:], jnp.float32), pltpu.SemaphoreType.DMA],
        compiler_params=params(24),
        cost_estimate=cost(10 * own.size, 40 * own.size),
        name="bottom",
    )(moist, chip_pair, own, core_far, chip_far, both_far)


def core_swap(value):
    return lax.ppermute(value, "depth", [(i, i ^ 1) for i in range(lax.axis_size("depth"))])


def chip_swap(value):
    return lax.ppermute(value, "depth", [(i, i ^ 2) for i in range(lax.axis_size("depth"))])


def middle_swap(value):
    return lax.ppermute(value, "depth", [(1, 2), (2, 1)])


def strip_swap(value):
    depth, strips = lax.axis_size("depth"), lax.axis_size("strips")
    pairs = []
    for d in range(1, depth, 2):
        for s in range(strips):
            lower, upper = d * strips + s, (d - 1) * strips + (s + 1) % strips
            pairs += [(lower, upper), (upper, lower)]
    return lax.ppermute(value, ("depth", "strips"), pairs)


def shards(pressure, texture, active, rain, k_sat, alpha, theta_sat, head_old, cell_code, section):
    river = jnp.where(
        cell_code == 1,
        jnp.float32(river_cond),
        jnp.where(cell_code == 2, jnp.float32(fixed_cond), jnp.float32(0.0)),
    )
    own = jnp.stack([head_old, river, river * section])
    other = core_swap(own)
    moist, keep, send, core_pair, chip_pair = soil(k_sat, alpha, theta_sat, pressure, texture, active)
    recv = core_swap(send)
    core_far = core_swap(core_pair)
    out, edge = pack(keep, recv, own, other)
    edge = chip_swap(edge)
    far = chip_swap(out)
    chip_far = middle_swap(chip_pair)
    rim_rows = strip_swap(rim(keep, recv, own, other, edge))
    heads = sweeps(keep, recv, own, other, far, edge, rim_rows)
    heads_chip = chip_swap(heads)
    heads_core = core_swap(heads)
    heads_both = core_swap(heads_chip)
    moist = faces(moist, core_pair, chip_pair, core_far, chip_far, rain)
    return bottom(moist, chip_pair, heads, heads_core, heads_chip, heads_both)


def solution(mesh):
    in_specs = (
        P("depth", "strips", None),
        P("depth", "strips", None),
        P("depth", "strips", None),
        P("strips", None),
        P(),
        P(),
        P(),
        P("strips", "depth"),
        P("strips", "depth"),
        P("strips", "depth"),
    )
    out_specs = (P("depth", "strips", None), P("strips", "depth"))
    return jax.shard_map(shards, mesh=mesh, in_specs=in_specs, out_specs=out_specs, check_vma=False)
```

time: 193 us -> 58.4 us (0.30); the launches traced: 190 us -> 57.7 us
  other arithmetic: 67.8 us -> 0.11 us
  starting transfers between devices: 49.8 us -> 9.03 us
  Pallas kernels: 0 us -> 16.3 us
  between operations: 14.5 us -> 0.78 us
  waiting for transfers between devices: 42.3 us -> 30.3 us
  blocking collectives: 11 us -> 0 us
  local copies, waits for them, and re-layouts: 4.04 us -> 1.19 us
    ppermute x18 -> x10, starting transfers between devices: 49.7 us -> 9.03 us  [the longest x3 4.06 us: chip_swap(): lax.ppermute(value, 'depth', [(i, i ^ 2) for i in range(lax.axis_size('de...]
    reduce_sum x1 -> x0, other arithmetic: 40.2 us -> none  [shards(): trans_part = jnp.sum(conduct, axis=0)]
    psum x1 -> x0, waiting for transfers between devices: 37.9 us -> none  [shards(): summed = lax.psum((trans_part, store_part, charge_part), 'depth')]
    ppermute x18 -> x10, waiting for transfers between devices: 4.47 us -> 30.3 us  [the longest x3 25.2 us: chip_swap(): lax.ppermute(value, 'depth', [(i, i ^ 2) for i in range(lax.axis_size('de...]
    pallas_call x0 -> x6, Pallas kernels: none -> 16.3 us  [the longest x1 12 us: soil(): pl.pallas_call(soil_kernel, grid=(nrows // rows,), in_specs=[whole, whole...]
    all_gather x1 -> x0, blocking collectives: 11 us -> none  [shards(): full_head = lax.all_gather(head, 'depth', axis=1, tiled=True)]
    eq x1 -> x0, other arithmetic: 9.72 us -> none  [lookup(): texture == class_id]
    mul x2 -> x0, other arithmetic: 8.17 us -> none  [the longest x1 7.25 us: face_flux(): return 0.5 * (cond_up + cond_low) * ((psi_up - psi_low) / layer_thick + 1.0)]
  transfers between devices with their start and end apart: 19 -> 10, of which waited for: 6 -> 4; matrix products, arithmetic and copies ran while one was open for 6% -> 0% of each run, Pallas kernels for 0% -> 6%
where the time goes in v1:
time: 58.4 us; the launch traced here: 57.7 us
  waiting for transfers between devices  30.3 us (52%)
  Pallas kernels  16.3 us (28%)
  starting transfers between devices  9.03 us (15%)
  local copies, waits for them, and re-layouts  1.19 us (2%)
  between operations  0.78 us (1%)
    ppermute x3, waiting for transfers between devices, chip_swap(): lax.ppermute(value, 'depth', [(i, i ^ 2) for i in range(lax.axis_size('de...  25.2 us
    pallas_call x1, Pallas kernels, soil(): pl.pallas_call(soil_kernel, grid=(nrows // rows,), in_specs=[whole, whole...  12 us
    ppermute x3, starting transfers between devices, chip_swap(): lax.ppermute(value, 'depth', [(i, i ^ 2) for i in range(lax.axis_size('de...  4.06 us
    ppermute x1, waiting for transfers between devices, strip_swap(): return lax.ppermute(value, ('depth', 'strips'), pairs)  3.35 us
    ppermute x1, starting transfers between devices, strip_swap(): return lax.ppermute(value, ('depth', 'strips'), pairs)  3.23 us
    pallas_call x1, Pallas kernels, faces(): pl.pallas_call(faces_kernel, in_specs=[ANY] + [VMEM] * 5, out_specs=ANY,...  2.39 us
    ppermute x5, waiting for transfers between devices, core_swap(): lax.ppermute(value, 'depth', [(i, i ^ 1) for i in range(lax.axis_size('de...  1.74 us
    unnamed x14, local copies, waits for them, and re-layouts  1.19 us
  transfers between devices with their start and end apart: 10, of which 4 were waited for; matrix products, arithmetic and copies ran while one was open for 0% of the time, Pallas kernels for 6%

profile of v1, /device:TPU:0, one launch (start us, length us, event | category | flops | bytes accessed | tf_op | source)
XLA Modules:
  0.0 57.7 jit_solution(11740850358880779636)
XLA Ops:
  0.6 0.0 copy-start.4
  0.6 0.0 copy-start.5
  0.7 0.0 copy-start.6
  0.7 12.0 %soil.1 = (f32[8,128,1024]{2,1,0:T(8,128)}, f32[9,3,8,1024]{3,2,1,0:T(8,128)}, f32[9,3,8,1024]{3,2,1,0:T(8,128)}, f32[2,128,1024]{2,1,0:T(8,128)}, f32[2,128,1024]{2,1,0:T(8,128)}) custom-call(f32[1,12]{1,0:T(1,128)} %bitcast.9, f32[1,12]{1,0:T(1,128)} %bitcast.10, f32[1,12]{1,0:T(1,128)} %bitcast.11, f32[8,128,1024]{2,1,0:T(8,128)} %psi_ref.1, ...), custom_call_target="tpu_custom_call" | custom-call | flops 62914560 | bytes 20971520 | tf_op jit(solution)/shard_map/soil/pallas_call | solution.py:151
  12.7 0.4 collective-permute-start.2
  13.1 0.0 copy-done.4
  13.2 0.0 copy-done.5
  13.2 0.0 copy-done.6
  13.3 0.1 collective-permute-start.3
  13.4 0.4 collective-permute-start
  13.8 0.7 %collective-permute-start.1 = (f32[2,128,1024]{2,1,0:T(8,128)}, f32[2,128,1024]{2,1,0:T(8,128)S(1)}, u32[]{:S(2)}, u32[]{:S(2)}) collective-permute-start(f32[2,128,1024]{2,1,0:T(8,128)} %get-tuple-element.11.chip_ref.chip_pair), channel_id=1, source_target_pairs={{8,16},{16,8},{9,17},{17,9},{10,18},{18,10},{11,19},{19,11},{12,20... | collective-permute-start | bytes 3145736 | tf_op jit(solution)/shard_map/ppermute | solution.py:474
  14.6 1.7 %collective-permute-done.3.other_ref = f32[3,128,256]{2,1,0:T(8,128)S(1)} collective-permute-done((f32[3,128,256]{2,1,0:T(8,128)S(1)}, f32[3,128,256]{2,1,0:T(8,128)S(1)}, u32[]{:S(2)}, u32[]{:S(2)}) %collective-permute-start.3) | collective-permute-done | bytes 393248 | tf_op jit(solution)/shard_map/ppermute | solution.py:466
  16.3 0.0 collective-permute-done.2.recv_ref
  16.3 0.0 copy-start
  16.3 1.2 %copy-done = f32[9,3,8,1024]{3,2,1,0:T(8,128)S(1)} copy-done((f32[9,3,8,1024]{3,2,1,0:T(8,128)S(1)}, f32[9,3,8,1024]{3,2,1,0:T(8,128)}, u32[]{:S(2)}) %copy-start) | copy-done | bytes 884760
  17.4 0.0 copy-start.1
  17.5 0.0 copy-start.2
  17.5 0.0 copy-start.3
  17.5 0.2 pack.1
  17.6 3.0 %collective-permute-start.4 = (f32[8,3,8,512]{3,2,1,0:T(8,128)S(1)}, f32[8,3,8,512]{3,2,1,0:T(8,128)S(1)}, u32[]{:S(2)}, u32[]{:S(2)}) collective-permute-start(f32[8,3,8,512]{3,2,1,0:T(8,128)S(1)} %get-tuple-element.14), channel_id=1, source_target_pairs={{0,16},{8,24},{16,0},{24,8},{1,17},{9,25},{17,1},{25,9},{2,18},{10... | collective-permute-start | bytes 1179656 | tf_op jit(solution)/shard_map/ppermute | solution.py:470
  20.6 0.1 collective-permute-start.5
  20.7 21.2 %collective-permute-done.5.edge_ref = f32[6,8,512]{2,1,0:T(8,128)S(1)} collective-permute-done((f32[6,8,512]{2,1,0:T(8,128)S(1)}, f32[6,8,512]{2,1,0:T(8,128)S(1)}, u32[]{:S(2)}, u32[]{:S(2)}) %collective-permute-start.5) | collective-permute-done | bytes 98336 | tf_op jit(solution)/shard_map/ppermute | solution.py:470
  41.8 0.1 rim.1
  41.9 3.2 %collective-permute-start.6 = (f32[4,8,640]{2,1,0:T(8,128)S(1)}, f32[4,8,640]{2,1,0:T(8,128)S(1)}, u32[]{:S(2)}, u32[]{:S(2)}) collective-permute-start(f32[4,8,640]{2,1,0:T(8,128)S(1)} %rim.1), channel_id=1, source_target_pairs={{8,1},{1,8},{9,2},{2,9},{10,3},{3,10},{11,4},{4,11},{12,5},{5,12},... | collective-permute-start | bytes 245768 | tf_op jit(solution)/shard_map/ppermute | solution.py:484
  45.1 3.4 %collective-permute-done.6.rim_ref = f32[4,8,640]{2,1,0:T(8,128)S(1)} collective-permute-done((f32[4,8,640]{2,1,0:T(8,128)S(1)}, f32[4,8,640]{2,1,0:T(8,128)S(1)}, u32[]{:S(2)}, u32[]{:S(2)}) %collective-permute-start.6) | collective-permute-done | bytes 81952 | tf_op jit(solution)/shard_map/ppermute | solution.py:484
  48.5 0.0 collective-permute-done.4.far_ref
  48.5 1.0 %sweeps.1.own_ref = f32[64,512]{1,0:T(8,128)S(1)} custom-call(f32[9,3,8,1024]{3,2,1,0:T(8,128)S(1)} %copy-done, f32[9,3,8,1024]{3,2,1,0:T(8,128)S(1)} %collective-permute-done.2.recv_ref, f32[3,128,256]{2,1,0:T(8,128)S(1)} %pad_maximum_fusion.own_ref, f32[3,128,256]{2,1,0:T(8,128)S(1)} %collective-permute-done.3.other_ref, ...), custom_call_target="tpu_custom_call" | custom-call | flops 4423680 | bytes 2654208 | tf_op jit(solution)/shard_map/sweeps/pallas_call | solution.py:339
  49.5 1.0 %collective-permute-start.8 = (f32[64,512]{1,0:T(8,128)S(1)}, f32[64,512]{1,0:T(8,128)S(1)}, u32[]{:S(2)}, u32[]{:S(2)}) collective-permute-start(f32[64,512]{1,0:T(8,128)S(1)} %sweeps.1.own_ref), channel_id=1, source_target_pairs={{0,16},{8,24},{16,0},{24,8},{1,17},{9,25},{17,1},{25,9},{2,18},{10... | collective-permute-start | bytes 393224 | tf_op jit(solution)/shard_map/ppermute | solution.py:470
  50.5 0.0 collective-permute-start.7
  50.5 4.0 %collective-permute-done.8.chip_far = f32[64,512]{1,0:T(8,128)S(1)} collective-permute-done((f32[64,512]{1,0:T(8,128)S(1)}, f32[64,512]{1,0:T(8,128)S(1)}, u32[]{:S(2)}, u32[]{:S(2)}) %collective-permute-start.8) | collective-permute-done | bytes 131104 | tf_op jit(solution)/shard_map/ppermute | solution.py:470
  54.5 0.0 collective-permute-start.9
  54.5 0.0 collective-permute-done.core_far
  54.5 0.0 collective-permute-done.1.chip_far
  54.5 0.0 copy-done.1
  54.5 0.0 copy-done.2
  54.5 0.0 copy-done.3
  54.6 2.4 %faces.1.moist_in = f32[8,128,1024]{2,1,0:T(8,128)} custom-call(f32[8,128,1024]{2,1,0:T(8,128)} %get-tuple-element.9.moist_in, f32[2,128,1024]{2,1,0:T(8,128)S(1)} %copy-done.2, f32[2,128,1024]{2,1,0:T(8,128)S(1)} %copy-done.1, f32[2,128,1024]{2,1,0:T(8,128)S(1)} %collective-permute-done.core_far, ...), custom_call_target="tpu_custom_call", output_to_operand_aliasing={{}: (0, {})} | custom-call | flops 2621440 | bytes 4194304 | tf_op jit(solution)/shard_map/faces/pallas_call | solution.py:400
  57.0 0.0 collective-permute-done.7.core_far
  57.0 0.0 collective-permute-done.9.both_far
  57.0 0.7 %bottom.1 = (f32[8,128,1024]{2,1,0:T(8,128)}, f32[128,256]{1,0:T(8,128)}) custom-call(f32[8,128,1024]{2,1,0:T(8,128)} %faces.1.moist_in, f32[2,128,1024]{2,1,0:T(8,128)S(1)} %copy-done.1, f32[64,512]{1,0:T(8,128)S(1)} %sweeps.1.own_ref, f32[64,512]{1,0:T(8,128)S(1)} %collective-permute-done.7.core_far, ...), custom_call_target="tpu_custom_call", output_to_operand_aliasing={{0}: (0, {})} | custom-call | flops 327680 | bytes 1310720 | tf_op jit(solution)/shard_map/bottom/pallas_call | solution.py:449
  (3 shorter events, 0.1 us)
Async XLA Ops:
  0.6 12.5 %copy-start.4 = (s32[128,256]{1,0:T(8,128)S(1)}, s32[128,256]{1,0:T(8,128)}, u32[]{:S(2)}) copy-start(s32[128,256]{1,0:T(8,128)} %param.18) | copy-start | bytes 393220
  0.6 12.5 %copy-start.5 = (f32[128,256]{1,0:T(8,128)S(1)}, f32[128,256]{1,0:T(8,128)}, u32[]{:S(2)}) copy-start(f32[128,256]{1,0:T(8,128)} %param.19) | copy-start | bytes 393220
  0.7 12.6 %copy-start.6 = (f32[128,256]{1,0:T(8,128)S(1)}, f32[128,256]{1,0:T(8,128)}, u32[]{:S(2)}) copy-start(f32[128,256]{1,0:T(8,128)} %param.17) | copy-start | bytes 393220
  12.7 3.6 %collective-permute-start.2 = (f32[9,3,8,1024]{3,2,1,0:T(8,128)}, f32[9,3,8,1024]{3,2,1,0:T(8,128)S(1)}, u32[]{:S(2)}, u32[]{:S(2)}) collective-permute-start(f32[9,3,8,1024]{3,2,1,0:T(8,128)} %get-tuple-element.13), channel_id=1, source_target_pairs={{0,8},{8,0},{16,24},{24,16},{1,9},{9,1},{17,25},{25,17},{2,10},{10... | collective-permute-start | bytes 2654216 | tf_op jit(solution)/shard_map/ppermute | solution.py:466
  13.3 3.0 %collective-permute-start.3 = (f32[3,128,256]{2,1,0:T(8,128)S(1)}, f32[3,128,256]{2,1,0:T(8,128)S(1)}, u32[]{:S(2)}, u32[]{:S(2)}) collective-permute-start(f32[3,128,256]{2,1,0:T(8,128)S(1)} %pad_maximum_fusion.own_ref), channel_id=1, source_target_pairs={{0,8},{8,0},{16,24},{24,16},{1,9},{9,1},{17,25},{25,17},{2,10},{10... | collective-permute-start | bytes 1179656 | tf_op jit(solution)/shard_map/ppermute | solution.py:466
  13.4 41.1 %collective-permute-start = (f32[2,128,1024]{2,1,0:T(8,128)}, f32[2,128,1024]{2,1,0:T(8,128)S(1)}, u32[]{:S(2)}, u32[]{:S(2)}) collective-permute-start(f32[2,128,1024]{2,1,0:T(8,128)} %get-tuple-element.10.core_ref), channel_id=1, source_target_pairs={{0,8},{8,0},{16,24},{24,16},{1,9},{9,1},{17,25},{25,17},{2,10},{10... | collective-permute-start | bytes 3145736 | tf_op jit(solution)/shard_map/ppermute | solution.py:466
  13.8 40.7 %collective-permute-start.1 = (f32[2,128,1024]{2,1,0:T(8,128)}, f32[2,128,1024]{2,1,0:T(8,128)S(1)}, u32[]{:S(2)}, u32[]{:S(2)}) collective-permute-start(f32[2,128,1024]{2,1,0:T(8,128)} %get-tuple-element.11.chip_ref.chip_pair), channel_id=1, source_target_pairs={{8,16},{16,8},{9,17},{17,9},{10,18},{18,10},{11,19},{19,11},{12,20... | collective-permute-start | bytes 3145736 | tf_op jit(solution)/shard_map/ppermute | solution.py:474
  16.3 1.2 %copy-start = (f32[9,3,8,1024]{3,2,1,0:T(8,128)S(1)}, f32[9,3,8,1024]{3,2,1,0:T(8,128)}, u32[]{:S(2)}) copy-start(f32[9,3,8,1024]{3,2,1,0:T(8,128)} %get-tuple-element.12.keep_ref) | copy-start | bytes 2654212
  17.4 37.1 %copy-start.1 = (f32[2,128,1024]{2,1,0:T(8,128)S(1)}, f32[2,128,1024]{2,1,0:T(8,128)}, u32[]{:S(2)}) copy-start(f32[2,128,1024]{2,1,0:T(8,128)} %get-tuple-element.11.chip_ref.chip_pair) | copy-start | bytes 3145732
  17.5 37.1 %copy-start.2 = (f32[2,128,1024]{2,1,0:T(8,128)S(1)}, f32[2,128,1024]{2,1,0:T(8,128)}, u32[]{:S(2)}) copy-start(f32[2,128,1024]{2,1,0:T(8,128)} %get-tuple-element.10.core_ref) | copy-start | bytes 3145732
  17.5 37.1 %copy-start.3 = (f32[128,1024]{1,0:T(8,128)S(1)}, f32[128,1024]{1,0:T(8,128)}, u32[]{:S(2)}) copy-start(f32[128,1024]{1,0:T(8,128)} %rain_ref.1) | copy-start | bytes 1572868
  17.6 30.9 %collective-permute-start.4 = (f32[8,3,8,512]{3,2,1,0:T(8,128)S(1)}, f32[8,3,8,512]{3,2,1,0:T(8,128)S(1)}, u32[]{:S(2)}, u32[]{:S(2)}) collective-permute-start(f32[8,3,8,512]{3,2,1,0:T(8,128)S(1)} %get-tuple-element.14), channel_id=1, source_target_pairs={{0,16},{8,24},{16,0},{24,8},{1,17},{9,25},{17,1},{25,9},{2,18},{10... | collective-permute-start | bytes 1179656 | tf_op jit(solution)/shard_map/ppermute | solution.py:470
  20.6 21.2 %collective-permute-start.5 = (f32[6,8,512]{2,1,0:T(8,128)S(1)}, f32[6,8,512]{2,1,0:T(8,128)S(1)}, u32[]{:S(2)}, u32[]{:S(2)}) collective-permute-start(f32[6,8,512]{2,1,0:T(8,128)S(1)} %get-tuple-element.15), channel_id=1, source_target_pairs={{0,16},{8,24},{16,0},{24,8},{1,17},{9,25},{17,1},{25,9},{2,18},{10... | collective-permute-start | bytes 294920 | tf_op jit(solution)/shard_map/ppermute | solution.py:470
  41.9 6.6 %collective-permute-start.6 = (f32[4,8,640]{2,1,0:T(8,128)S(1)}, f32[4,8,640]{2,1,0:T(8,128)S(1)}, u32[]{:S(2)}, u32[]{:S(2)}) collective-permute-start(f32[4,8,640]{2,1,0:T(8,128)S(1)} %rim.1), channel_id=1, source_target_pairs={{8,1},{1,8},{9,2},{2,9},{10,3},{3,10},{11,4},{4,11},{12,5},{5,12},... | collective-permute-start | bytes 245768 | tf_op jit(solution)/shard_map/ppermute | solution.py:484
  49.5 5.0 %collective-permute-start.8 = (f32[64,512]{1,0:T(8,128)S(1)}, f32[64,512]{1,0:T(8,128)S(1)}, u32[]{:S(2)}, u32[]{:S(2)}) collective-permute-start(f32[64,512]{1,0:T(8,128)S(1)} %sweeps.1.own_ref), channel_id=1, source_target_pairs={{0,16},{8,24},{16,0},{24,8},{1,17},{9,25},{17,1},{25,9},{2,18},{10... | collective-permute-start | bytes 393224 | tf_op jit(solution)/shard_map/ppermute | solution.py:470
  50.5 6.5 %collective-permute-start.7 = (f32[64,512]{1,0:T(8,128)S(1)}, f32[64,512]{1,0:T(8,128)S(1)}, u32[]{:S(2)}, u32[]{:S(2)}) collective-permute-start(f32[64,512]{1,0:T(8,128)S(1)} %sweeps.1.own_ref), channel_id=1, source_target_pairs={{0,8},{8,0},{16,24},{24,16},{1,9},{9,1},{17,25},{25,17},{2,10},{10... | collective-permute-start | bytes 393224 | tf_op jit(solution)/shard_map/ppermute | solution.py:466
  54.5 2.5 %collective-permute-start.9 = (f32[64,512]{1,0:T(8,128)S(1)}, f32[64,512]{1,0:T(8,128)S(1)}, u32[]{:S(2)}, u32[]{:S(2)}) collective-permute-start(f32[64,512]{1,0:T(8,128)S(1)} %collective-permute-done.8.chip_far), channel_id=1, source_target_pairs={{0,8},{8,0},{16,24},{24,16},{1,9},{9,1},{17,25},{25,17},{2,10},{10... | collective-permute-start | bytes 393224 | tf_op jit(solution)/shard_map/ppermute | solution.py:466

commit v2 on v1

v2 whole, which is shorter than its diff:
```python
import functools
import math

import jax
import jax.numpy as jnp
from jax import lax
from jax.experimental import pallas as pl
from jax.experimental.pallas import tpu as pltpu
from jax.sharding import PartitionSpec as P

SWEEPS = 3
SUB = 8
LANE = 128
WIDTH = 4

layer_thick = 0.05
soil_step = 0.0002
spec_yield = 0.02
leak_rate = 0.5
river_cond = 0.5
fixed_cond = 3.0
residual = 0.15
mobile = 0.85

VMEM = pl.BlockSpec(memory_space=pltpu.VMEM)
ANY = pl.BlockSpec(memory_space=pl.ANY)


def params(mib):
    return pltpu.CompilerParams(vmem_limit_bytes=mib * 2**20)


def cost(flops, nbytes, trans=0):
    return pl.CostEstimate(flops=int(flops), bytes_accessed=int(nbytes), transcendentals=int(trans))


def place():
    depth = lax.axis_index("depth")
    return depth // 2, depth % 2


def gathered(table, classes):
    return jnp.take_along_axis(table, classes, axis=1, mode="promise_in_bounds")


def picked(options, bits):
    for bit in bits:
        options = [
            jnp.where(bit, options[i + 1], options[i]) if i + 1 < len(options) else options[i]
            for i in range(0, len(options), 2)
        ]
    return options[0]


def fill_tables(tab, sat_ref, alpha_ref, theta_ref):
    classes = sat_ref.shape[1]
    scaled = (sat_ref, 1.0), (alpha_ref, 0.5 * math.log2(math.e)), (theta_ref, mobile)
    for i, (ref, scale) in enumerate(scaled):
        tab[i, :, :classes] = jnp.broadcast_to(ref[...] * scale, (SUB, classes))


def face_kernel(sat_ref, alpha_ref, theta_ref, psi_hbm, tex_hbm, act_hbm, out_ref, kinds, acts, tab, sems):
    _, core = place()
    layer = core * (psi_hbm.shape[0] - 1)
    nrows, cols = psi_hbm.shape[1:]
    chunk = nrows // 4

    def copies(i):
        rows = pl.ds(i * chunk, chunk)
        return [
            pltpu.make_async_copy(src.at[layer, rows], dst.at[rows], sems.at[i, k])
            for k, (src, dst) in enumerate(
                ((psi_hbm, out_ref.at[0]), (tex_hbm, kinds), (act_hbm, acts))
            )
        ]

    for i in range(4):
        for c in copies(i):
            c.start()
    fill_tables(tab, sat_ref, alpha_ref, theta_ref)
    for i in range(4):
        for c in copies(i):
            c.wait()

        def columns(q, carry):
            lanes = pl.ds(pl.multiple_of(q * LANE, LANE), LANE)
            for r in range(i * chunk, (i + 1) * chunk, SUB):
                rws = slice(r, r + SUB)
                kind = kinds[rws, lanes]
                wet = jnp.exp2(gathered(tab[1], kind) * jnp.minimum(out_ref[0, rws, lanes], 0.0))
                active = acts[rws, lanes].astype(jnp.float32)
                out_ref[1, rws, lanes] = gathered(tab[0], kind) * active * (wet * wet)
            return carry

        lax.fori_loop(0, cols // LANE, columns, 0, unroll=4)


def in_hbm(*arrays):
    return [pltpu.with_memory_space_constraint(x, pltpu.HBM) for x in arrays]


def face(tables, pressure, texture, active):
    _, nrows, cols = pressure.shape
    size = nrows * cols
    return pl.pallas_call(
        face_kernel,
        grid=(1,),
        in_specs=[pl.BlockSpec(t.shape, lambda j: (0, 0)) for t in tables]
        + [pl.BlockSpec(memory_space=pltpu.HBM)] * 3,
        out_specs=pl.BlockSpec((2, nrows, cols), lambda j: (0, 0, 0)),
        out_shape=jax.ShapeDtypeStruct((2, nrows, cols), jnp.float32),
        scratch_shapes=[
            pltpu.VMEM((nrows, cols), jnp.int32),
            pltpu.VMEM((nrows, cols), jnp.int32),
            pltpu.VMEM((3, SUB, LANE), jnp.float32),
            pltpu.SemaphoreType.DMA((4, 3)),
        ],
        compiler_params=params(8),
        cost_estimate=cost(20 * size, 20 * size, size),
        name="face",
    )(*in_hbm(*tables, pressure, texture, active))


def soil_kernel(
    sat_ref, alpha_ref, theta_ref, psi_ref, tex_ref, act_ref,
    moist_ref, keep_ref, send_ref, core_ref, tab, part,
):
    step = pl.program_id(0)
    _, core = place()
    layers, rows, cols = psi_ref.shape
    classes = sat_ref.shape[1]

    @pl.when(step == 0)
    def _():
        fill_tables(tab, sat_ref, alpha_ref, theta_ref)

    sat_tab, par_tab = tab[0], tab[1]
    theta = [jnp.broadcast_to(tab[2, :, i : i + 1], (SUB, LANE)) for i in range(classes)]
    nbits = max(1, (classes - 1).bit_length())
    face = 0.5 * soil_step / layer_thick
    core_layer = (1 - core) * (layers - 1)

    def columns(q, carry):
        lanes = pl.ds(pl.multiple_of(q * LANE, LANE), LANE)
        for r in range(0, rows, SUB):
            rws = slice(r, r + SUB)
            trans = store = charge = jnp.zeros((SUB, LANE), jnp.float32)
            for layer in range(layers):
                kind = tex_ref[layer, rws, lanes]
                psi = psi_ref[layer, rws, lanes]
                active = act_ref[layer, rws, lanes].astype(jnp.float32)
                bits = [(kind & (1 << b)) != 0 for b in range(nbits)]
                wet = jnp.exp2(gathered(par_tab, kind) * jnp.minimum(psi, 0.0))
                cond = gathered(sat_tab, kind) * active * (wet * wet)
                mob = picked(theta, bits)
                mobwet = mob * wet
                trans = trans + cond
                charge = charge + cond * wet
                store = store + (mob - mobwet)
                held = mob * (residual / mobile) + mobwet
                if layer == 0:
                    first, own = cond, held
                else:
                    flux = (cond_up + cond) * ((psi_up - psi) * (face / layer_thick) + face)
                    moist_ref[layer - 1, rws, lanes] = own - flux
                    own = held + flux
                psi_up, cond_up = psi, cond
            moist_ref[layers - 1, rws, lanes] = own
            part[r // SUB, 0, :, lanes] = trans
            part[r // SUB, 1, :, lanes] = store
            part[r // SUB, 2, :, lanes] = charge
            core_ref[0, rws, lanes] = psi_ref[core_layer, rws, lanes]
            core_ref[1, rws, lanes] = jnp.where(core == 0, cond, first)
        return carry

    lax.fori_loop(0, cols // LANE, columns, 0, unroll=4)

    blocks = rows // SUB
    half = keep_ref.shape[0] - 1
    for r in range(blocks):
        block = step * blocks + r

        def put(ref, at):
            ref[at] = part[r]

        @pl.when((block <= half) & (core == 0))
        def _():
            put(keep_ref, block)

        @pl.when((block <= half) & (core == 1))
        def _():
            put(send_ref, block)

        @pl.when((block >= half - 1) & (core == 0))
        def _():
            put(send_ref, block - (half - 1))

        @pl.when((block >= half - 1) & (core == 1))
        def _():
            put(keep_ref, block - (half - 1))


def soil(tables, pressure, texture, active):
    layers, nrows, cols = pressure.shape
    classes = tables[0].shape[1]
    rows = nrows // 4
    blocks = nrows // (2 * SUB) + 1
    whole = pl.BlockSpec((1, classes), lambda j: (0, 0))
    block = pl.BlockSpec((layers, rows, cols), lambda j: (0, j, 0))
    pair = pl.BlockSpec((2, rows, cols), lambda j: (0, j, 0))
    msg = jax.ShapeDtypeStruct((blocks, 3, SUB, cols), jnp.float32)
    msg_spec = pl.BlockSpec((blocks, 3, SUB, cols), lambda j: (0, 0, 0, 0))
    layer2 = jax.ShapeDtypeStruct((2, nrows, cols), jnp.float32)
    size = layers * nrows * cols
    return pl.pallas_call(
        soil_kernel,
        grid=(nrows // rows,),
        in_specs=[whole, whole, whole, block, block, block],
        out_specs=[block, msg_spec, msg_spec, pair],
        out_shape=[jax.ShapeDtypeStruct((layers, nrows, cols), jnp.float32), msg, msg, layer2],
        scratch_shapes=[
            pltpu.VMEM((3, SUB, LANE), jnp.float32),
            pltpu.VMEM((rows // SUB, 3, SUB, cols), jnp.float32),
        ],
        compiler_params=params(32),
        cost_estimate=cost(60 * size, 20 * size, size),
        name="soil",
    )(*in_hbm(*tables, pressure, texture, active))


def edge_lane(chip):
    return (1 - chip) * (LANE - WIDTH)


def on_edge(value, chip):
    lane = lax.broadcasted_iota(jnp.int32, value.shape, 1)
    base = edge_lane(chip)
    return jnp.where((lane >= base) & (lane < base + WIDTH), value, 0.0)


def shift(array, block=0):
    return WIDTH * (6 * block + array)


SHARE = LANE // (6 * WIDTH)


def packed(pieces, chip, block=0):
    total = None
    for a, piece in enumerate(pieces):
        moved = pltpu.roll(on_edge(piece, chip), shift(a, block), 1)
        total = moved if total is None else total + moved
    return total


def unpacked(tile, array, block=0):
    return pltpu.roll(tile, LANE - shift(array, block), 1)


def half_lanes(which, half):
    return pl.ds(pl.multiple_of(which * half, half), half)


def slab_lanes(chip, half):
    return pl.ds(pl.multiple_of(half - LANE + chip * LANE, LANE), LANE)


def first_row(core, blocks, b):
    return pl.multiple_of((core * (blocks - 2) + b) * SUB, SUB)


def tile_rows(own_ref, other_ref, core, which, array, first, lanes):
    mine = own_ref[array, pl.ds(first, SUB), lanes]
    theirs = other_ref[array, pl.ds(first, SUB), lanes]
    return jnp.where(core == which, mine, theirs)


def edge_inputs(own_ref, other_ref, chip, core, first):
    tile = own_ref.shape[2]
    out = []
    for a in range(3):
        left = tile_rows(own_ref, other_ref, core, 1, a, first, slice(tile - LANE, tile))
        right = tile_rows(own_ref, other_ref, core, 0, a, first, slice(0, LANE))
        out.append(jnp.where(chip == 0, left, right))
    return out


def pack_kernel(keep_ref, recv_ref, own_ref, other_ref, out_ref):
    chip, core = place()
    blocks, _, _, cols = keep_ref.shape
    half = cols // 2
    away = half_lanes(1 - chip, half)
    slab = slab_lanes(chip, half)
    tiles = [None] * -(-blocks // SHARE)
    for b in range(blocks):
        out_ref[3 * b : 3 * b + 3] = keep_ref[b, :, :, away] + recv_ref[b, :, :, away]
        pieces = [keep_ref[b, a, :, slab] + recv_ref[b, a, :, slab] for a in range(3)]
        pieces += edge_inputs(own_ref, other_ref, chip, core, first_row(core, blocks, b))
        piece = packed(pieces, chip, b % SHARE)
        i = b // SHARE
        tiles[i] = piece if tiles[i] is None else tiles[i] + piece
    per = half // LANE
    for i, tile in enumerate(tiles):
        out_ref[3 * blocks + i // per, :, (i % per) * LANE : (i % per + 1) * LANE] = tile


def pack(keep, recv, own, other):
    blocks, _, _, cols = keep.shape
    half = cols // 2
    tiles = -(-blocks // SHARE)
    planes = 3 * blocks - (-tiles // (half // LANE))
    return pl.pallas_call(
        pack_kernel,
        in_specs=[VMEM] * 4,
        out_specs=VMEM,
        out_shape=jax.ShapeDtypeStruct((planes, SUB, half), jnp.float32),
        compiler_params=params(8),
        cost_estimate=cost(keep.size, 12 * keep.size),
        name="pack",
    )(keep, recv, own, other)


def rim_kernel(keep_ref, recv_ref, own_ref, other_ref, first, side_ref, cross_ref):
    del first
    chip, core = place()
    blocks, _, _, cols = keep_ref.shape
    half = cols // 2
    tile = half // 2
    b = core * (blocks - 1)
    row = first_row(core, blocks, b)
    near, away = half_lanes(chip, half), half_lanes(1 - chip, half)
    side_ref[:3] = keep_ref[b, :, :, near] + recv_ref[b, :, :, near]
    cross_ref[:3] = keep_ref[b, :, :, away] + recv_ref[b, :, :, away]
    for which in range(2):
        for a in range(3):
            side_ref[3 + a, :, which * tile : (which + 1) * tile] = tile_rows(
                own_ref, other_ref, core, which, a, row, slice(0, tile)
            )

    def sums(slab):
        return [keep_ref[b, a, :, slab] + recv_ref[b, a, :, slab] for a in range(3)]

    side_ref[6, :, :LANE] = packed(sums(slab_lanes(1 - chip, half)), 1 - chip)
    inputs = edge_inputs(own_ref, other_ref, chip, core, row)
    cross_ref[3, :, :LANE] = packed(sums(slab_lanes(chip, half)) + inputs, chip)


def rim(keep, recv, own, other, first):
    half = keep.shape[3] // 2
    return pl.pallas_call(
        rim_kernel,
        in_specs=[VMEM] * 4 + [ANY],
        out_specs=[VMEM] * 2,
        out_shape=[jax.ShapeDtypeStruct((n, SUB, half), jnp.float32) for n in (7, 4)],
        compiler_params=params(8),
        cost_estimate=cost(keep.size // 8, keep.size),
        name="rim",
    )(keep, recv, own, other, first)


def sweep_kernel(keep_ref, recv_ref, own_ref, other_ref, far_ref, side_ref, cross_ref, first, out_ref, work):
    del first
    chip, core = place()
    strip = lax.axis_index("strips")
    blocks, _, _, cols = keep_ref.shape
    half = cols // 2
    tile = half // 2
    per = half // LANE

    def cells(at, lanes, sums, inputs):
        trans = sums[0] * layer_thick
        store = spec_yield + sums[1] * layer_thick
        old, river, inflow = inputs
        rows = slice(at * SUB, (at + 1) * SUB)
        work[0, rows, lanes] = trans
        work[1, rows, lanes] = store + river
        work[2, rows, lanes] = store * old + leak_rate * layer_thick * sums[2] + inflow
        work[3, rows, lanes] = old

    def halo(at, sums, inputs):
        cells(at, slice(half, half + LANE), [on_edge(v, 1 - chip) for v in sums], [on_edge(v, 1 - chip) for v in inputs])

    near, slab = half_lanes(chip, half), slab_lanes(1 - chip, half)
    for b in range(blocks):
        sums = [keep_ref[b, a, :, near] + recv_ref[b, a, :, near] + far_ref[3 * b + a] for a in range(3)]
        first_at = first_row(core, blocks, b)
        for which in range(2):
            lanes = slice(which * tile, (which + 1) * tile)
            inputs = [tile_rows(own_ref, other_ref, core, which, a, first_at, slice(0, tile)) for a in range(3)]
            cells(b, lanes, [s[:, lanes] for s in sums], inputs)
        i = b // SHARE
        far = far_ref[3 * blocks + i // per, :, (i % per) * LANE : (i % per + 1) * LANE]
        far = [unpacked(far, a, b % SHARE) for a in range(6)]
        sums = [keep_ref[b, a, :, slab] + recv_ref[b, a, :, slab] + far[a] for a in range(3)]
        halo(b, sums, far[3:])
    outside = ((core == 0) & (strip == 0)) | ((core == 1) & (strip == lax.axis_size("strips") - 1))

    def inside(value):
        return jnp.where(outside, 0.0, value)

    sums = [inside(side_ref[a] + cross_ref[a]) for a in range(3)]
    cells(blocks, slice(0, half), sums, [inside(side_ref[3 + a]) for a in range(3)])
    side, cross = side_ref[6, :, :LANE], cross_ref[3, :, :LANE]
    sums = [inside(unpacked(side, a) + unpacked(cross, a)) for a in range(3)]
    halo(blocks, sums, [inside(unpacked(cross, a)) for a in range(3, 6)])

    trans, base, rhs, head = (work[i] for i in range(4))
    rows, lanes = trans.shape
    right = jnp.sqrt(trans * pltpu.roll(trans, lanes - 1, 1))
    left = pltpu.roll(right, 1, 1)
    down = jnp.sqrt(trans * pltpu.roll(trans, rows - 1, 0))
    up = pltpu.roll(down, 1, 0)
    inverse = 1.0 / (base + right + left + down + up)
    for _ in range(SWEEPS):
        head = inverse * (
            rhs
            + right * pltpu.roll(head, lanes - 1, 1)
            + left * pltpu.roll(head, 1, 1)
            + down * pltpu.roll(head, rows - 1, 0)
            + up * pltpu.roll(head, 1, 0)
        )
    work[0] = head
    out_ref[...] = work[0, pl.ds(pl.multiple_of(core * SUB, SUB), out_ref.shape[0]), :half]


def sweeps(keep, recv, own, other, far, side, cross, first):
    blocks = keep.shape[0]
    half = keep.shape[3] // 2
    return pl.pallas_call(
        sweep_kernel,
        in_specs=[VMEM] * 7 + [pl.BlockSpec(memory_space=pltpu.HBM)],
        out_specs=VMEM,
        out_shape=jax.ShapeDtypeStruct(((blocks - 1) * SUB, half), jnp.float32),
        scratch_shapes=[pltpu.VMEM((4, (blocks + 1) * SUB, half + LANE), jnp.float32)],
        compiler_params=params(12),
        cost_estimate=cost(20 * keep.size, 12 * keep.size),
        name="sweeps",
    )(keep, recv, own, other, far, side, cross, *in_hbm(first))


def faces_kernel(moist_in, core_ref, chip_ref, core_far, chip_far, rain_ref, moist_out, ends, sems):
    del moist_in
    chip, core = place()
    layers = moist_out.shape[0]
    loads = [
        pltpu.make_async_copy(moist_out.at[layer], ends.at[i], sems.at[i])
        for i, layer in enumerate((0, layers - 1))
    ]
    for c in loads:
        c.start()
    for c in loads:
        c.wait()
    gain = soil_step / layer_thick
    face = 0.5 * gain

    def flux(upper, lower):
        return (upper[1] + lower[1]) * ((upper[0] - lower[0]) * (face / layer_thick) + face)

    @pl.when(core == 0)
    def _():
        ends[1] = ends[1] - flux(core_ref, core_far)

    @pl.when(core == 1)
    def _():
        ends[0] = ends[0] + flux(core_far, core_ref)

    @pl.when((core == 0) & (chip == 0))
    def _():
        ends[0] = ends[0] + gain * rain_ref[...]

    @pl.when((core == 0) & (chip == 1))
    def _():
        ends[0] = ends[0] + flux(chip_far, chip_ref)

    @pl.when((core == 1) & (chip == 0))
    def _():
        ends[1] = ends[1] - flux(chip_ref, chip_far)

    stores = [
        pltpu.make_async_copy(ends.at[i], moist_out.at[layer], sems.at[i])
        for i, layer in enumerate((0, layers - 1))
    ]
    for c in stores:
        c.start()
    for c in stores:
        c.wait()


def faces(moist, core_pair, chip_pair, core_far, chip_far, rain):
    return pl.pallas_call(
        faces_kernel,
        in_specs=[ANY] + [VMEM] * 5,
        out_specs=ANY,
        out_shape=jax.ShapeDtypeStruct(moist.shape, moist.dtype),
        input_output_aliases={0: 0},
        scratch_shapes=[pltpu.VMEM((2,) + moist.shape[1:], jnp.float32), pltpu.SemaphoreType.DMA((2,))],
        compiler_params=params(12),
        cost_estimate=cost(20 * rain.size, 32 * rain.size),
        name="faces",
    )(moist, core_pair, chip_pair, core_far, chip_far, rain)


def bottom_kernel(
    moist_in, chip_pair, own_ref, core_far, chip_far, both_far, moist_out, head_ref, last, sem
):
    del moist_in
    chip, core = place()
    layers = moist_out.shape[0]
    rows, half = own_ref.shape
    tile = half // 2
    mine = pl.ds(pl.multiple_of(core * rows, rows), rows)
    theirs = pl.ds(pl.multiple_of((1 - core) * rows, rows), rows)

    @pl.when((core == 1) & (chip == 1))
    def _():
        load = pltpu.make_async_copy(moist_out.at[layers - 1], last, sem)
        load.start()
        load.wait()
        gain = soil_step / layer_thick
        for ref, where, lanes in (
            (own_ref, mine, slice(half, 2 * half)),
            (core_far, theirs, slice(half, 2 * half)),
            (chip_far, mine, slice(0, half)),
            (both_far, theirs, slice(0, half)),
        ):
            drop = (chip_pair[0, where, lanes] - ref[...]) / (0.5 * layer_thick) + 1.0
            last[where, lanes] = last[where, lanes] - gain * chip_pair[1, where, lanes] * drop
        store = pltpu.make_async_copy(last, moist_out.at[layers - 1], sem)
        store.start()
        store.wait()

    lanes = pl.ds(pl.multiple_of(core * tile, tile), tile)
    head_ref[mine, :] = own_ref[:, lanes]
    head_ref[theirs, :] = core_far[:, lanes]


def bottom(moist, chip_pair, own, core_far, chip_far, both_far):
    rows, half = own.shape
    return pl.pallas_call(
        bottom_kernel,
        in_specs=[ANY] + [VMEM] * 5,
        out_specs=[ANY, VMEM],
        out_shape=[
            jax.ShapeDtypeStruct(moist.shape, moist.dtype),
            jax.ShapeDtypeStruct((2 * rows, half // 2), jnp.float32),
        ],
        input_output_aliases={0: 0},
        scratch_shapes=[pltpu.VMEM(moist.shape[1:], jnp.float32), pltpu.SemaphoreType.DMA],
        compiler_params=params(12),
        cost_estimate=cost(10 * own.size, 40 * own.size),
        name="bottom",
    )(moist, chip_pair, own, core_far, chip_far, both_far)


def gate_kernel(*refs):
    del refs


def gate(value, *first):
    return pl.pallas_call(
        gate_kernel,
        in_specs=[ANY] * (1 + len(first)),
        out_specs=ANY,
        out_shape=jax.ShapeDtypeStruct(value.shape, value.dtype),
        input_output_aliases={0: 0},
        compiler_params=params(1),
        cost_estimate=cost(1, 1),
        name="gate",
    )(value, *first)


def core_swap(value):
    return lax.ppermute(value, "depth", [(i, i ^ 1) for i in range(lax.axis_size("depth"))])


def chip_swap(value):
    return lax.ppermute(value, "depth", [(i, i ^ 2) for i in range(lax.axis_size("depth"))])


def middle_swap(value):
    return lax.ppermute(value, "depth", [(1, 2), (2, 1)])


def strip_swap(value, chips=0):
    depth, strips = lax.axis_size("depth"), lax.axis_size("strips")
    pairs = []
    for d in range(1, depth, 2):
        for s in range(strips):
            lower, upper = d * strips + s, ((d - 1) ^ chips) * strips + (s + 1) % strips
            pairs += [(lower, upper), (upper, lower)]
    return lax.ppermute(value, ("depth", "strips"), pairs)


def shards(pressure, texture, active, rain, k_sat, alpha, theta_sat, head_old, cell_code, section):
    river = jnp.where(
        cell_code == 1,
        jnp.float32(river_cond),
        jnp.where(cell_code == 2, jnp.float32(fixed_cond), jnp.float32(0.0)),
    )
    own = jnp.stack([head_old, river, river * section])
    other = core_swap(own)
    tables = (k_sat[None], alpha[None], theta_sat[None])
    chip_pair = face(tables, pressure, texture, active)
    chip_far = middle_swap(chip_pair)
    moist, keep, send, core_pair = soil(tables, pressure, texture, active)
    recv = core_swap(gate(send, chip_far, other))
    message = pack(keep, recv, own, other)
    far = chip_swap(message)
    side, cross = rim(keep, recv, own, other, message)
    side, cross = strip_swap(side), strip_swap(cross, 2)
    core_far = core_swap(gate(core_pair, message))
    moist = faces(moist, core_pair, chip_pair, core_far, chip_far, rain)
    heads = sweeps(keep, recv, own, other, far, side, cross, moist)
    heads_chip = chip_swap(heads)
    heads_core = core_swap(heads)
    heads_both = core_swap(heads_chip)
    return bottom(moist, chip_pair, heads, heads_core, heads_chip, heads_both)


def solution(mesh):
    in_specs = (
        P("depth", "strips", None),
        P("depth", "strips", None),
        P("depth", "strips", None),
        P("strips", None),
        P(),
        P(),
        P(),
        P("strips", "depth"),
        P("strips", "depth"),
        P("strips", "depth"),
    )
    out_specs = (P("depth", "strips", None), P("strips", "depth"))
    return jax.shard_map(shards, mesh=mesh, in_specs=in_specs, out_specs=out_specs, check_vma=False)
```

time: 58.4 us -> 47.4 us (0.81)
  the two profiles are of different devices: /device:TPU:0 before, /device:TPU:31 now
where the time goes in v2:
time: 47.4 us; the launch traced here: 47.2 us
  Pallas kernels  19.8 us (42%)
  starting transfers between devices  15.5 us (33%)
  waiting for transfers between devices  10.8 us (23%)
  between operations  0.77 us (2%)
    pallas_call x1, Pallas kernels, soil(): pl.pallas_call(soil_kernel, grid=(nrows // rows,), in_specs=[whole, whole...  10.5 us
    ppermute x5, starting transfers between devices, core_swap(): lax.ppermute(value, 'depth', [(i, i ^ 1) for i in range(lax.axis_size('de...  9.09 us
    ppermute x2, waiting for transfers between devices, chip_swap(): lax.ppermute(value, 'depth', [(i, i ^ 2) for i in range(lax.axis_size('de...  6.96 us
    ppermute x2, starting transfers between devices, strip_swap(): return lax.ppermute(value, ('depth', 'strips'), pairs)  5.63 us
    pallas_call x1, Pallas kernels, face(): pl.pallas_call(face_kernel, grid=(1,), in_specs=[pl.BlockSpec(t.shape, la...  3.13 us
    ppermute x5, waiting for transfers between devices, core_swap(): lax.ppermute(value, 'depth', [(i, i ^ 1) for i in range(lax.axis_size('de...  2.94 us
    pallas_call x1, Pallas kernels, bottom(): pl.pallas_call(bottom_kernel, in_specs=[ANY] + [VMEM] * 5, out_specs=[ANY...  2.63 us
    pallas_call x1, Pallas kernels, faces(): pl.pallas_call(faces_kernel, in_specs=[ANY] + [VMEM] * 5, out_specs=ANY,...  2.32 us
  transfers between devices with their start and end apart: 10, of which 5 were waited for; matrix products, arithmetic and copies ran while one was open for 0% of the time, Pallas kernels for 27%

profile of v2, /device:TPU:31, one launch (start us, length us, event | category | flops | bytes accessed | tf_op | source)
XLA Modules:
  0.0 47.2 jit_solution(17777937949075097602)
XLA Ops:
  0.6 0.0 copy-start.1
  0.6 0.0 copy-start.2
  0.7 0.0 copy-start.3
  0.7 3.1 %face.1.chip_ref.chip_pair = f32[2,128,1024]{2,1,0:T(8,128)S(1)} custom-call(f32[1,12]{1,0:T(1,128)} %bitcast.9, f32[1,12]{1,0:T(1,128)} %bitcast.11, f32[1,12]{1,0:T(1,128)} %bitcast.13, f32[8,128,1024]{2,1,0:T(8,128)} %psi_hbm.1, s32[8,128,1024]{2,1,0:T(8,128)} %tex_hbm.1, s32[8,128,1024]{2,1,0:T(8,128)} %act_hbm.1), custom_call_target="tpu_custom_call" | custom-call | flops 2621440 | bytes 2621440 | tf_op jit(solution)/shard_map/face/pallas_call | solution.py:105
  3.8 0.7 %collective-permute-start = (f32[2,128,1024]{2,1,0:T(8,128)S(1)}, f32[2,128,1024]{2,1,0:T(8,128)S(1)}, u32[]{:S(2)}, u32[]{:S(2)}) collective-permute-start(f32[2,128,1024]{2,1,0:T(8,128)S(1)} %face.1.chip_ref.chip_pair), channel_id=1, source_target_pairs={{8,16},{16,8},{9,17},{17,9},{10,18},{18,10},{11,19},{19,11},{12,20... | collective-permute-start | bytes 3145736 | tf_op jit(solution)/shard_map/ppermute | solution.py:581
  4.5 0.0 copy-done.1
  4.6 0.0 copy-done.2
  4.7 0.0 copy-done.3
  4.7 1.9 %collective-permute-start.1 = (f32[3,128,256]{2,1,0:T(8,128)S(1)}, f32[3,128,256]{2,1,0:T(8,128)S(1)}, u32[]{:S(2)}, u32[]{:S(2)}) collective-permute-start(f32[3,128,256]{2,1,0:T(8,128)S(1)} %pad_maximum_fusion.own_ref), channel_id=1, source_target_pairs={{0,8},{8,0},{16,24},{24,16},{1,9},{9,1},{17,25},{25,17},{2,10},{10... | collective-permute-start | bytes 1179656 | tf_op jit(solution)/shard_map/ppermute | solution.py:573
  6.6 10.5 %soil.1 = (f32[8,128,1024]{2,1,0:T(8,128)}, f32[9,3,8,1024]{3,2,1,0:T(8,128)S(1)}, f32[9,3,8,1024]{3,2,1,0:T(8,128)S(1)}, f32[2,128,1024]{2,1,0:T(8,128)S(1)}) custom-call(f32[1,12]{1,0:T(1,128)} %bitcast.10, f32[1,12]{1,0:T(1,128)} %bitcast.12, f32[1,12]{1,0:T(1,128)} %bitcast.14, f32[8,128,1024]{2,1,0:T(8,128)} %psi_hbm.1, s32[8,128,1024]{2,1,0:T(8,128)} %tex_hbm.1, ...), custom_call_target="tpu_custom_call" | custom-call | flops 62914560 | bytes 20971520 | tf_op jit(solution)/shard_map/soil/pallas_call | solution.py:215
  17.2 0.0 collective-permute-done.1.refs_2_.other_ref
  17.2 0.0 collective-permute-done.refs_1_.chip_far
  17.2 3.4 %collective-permute-start.2 = (f32[9,3,8,1024]{3,2,1,0:T(8,128)S(1)}, f32[9,3,8,1024]{3,2,1,0:T(8,128)S(1)}, u32[]{:S(2)}, u32[]{:S(2)}) collective-permute-start(f32[9,3,8,1024]{3,2,1,0:T(8,128)S(1)} %gate.2), channel_id=1, source_target_pairs={{0,8},{8,0},{16,24},{24,16},{1,9},{9,1},{17,25},{25,17},{2,10},{10... | collective-permute-start | bytes 2654216 | tf_op jit(solution)/shard_map/ppermute | solution.py:573
  20.6 0.1 copy.17.refs_0_
  20.7 1.9 %collective-permute-done.2.recv_ref = f32[9,3,8,1024]{3,2,1,0:T(8,128)S(1)} collective-permute-done((f32[9,3,8,1024]{3,2,1,0:T(8,128)S(1)}, f32[9,3,8,1024]{3,2,1,0:T(8,128)S(1)}, u32[]{:S(2)}, u32[]{:S(2)}) %collective-permute-start.2) | collective-permute-done | bytes 884768 | tf_op jit(solution)/shard_map/ppermute | solution.py:573
  22.6 0.0 copy-start
  22.7 0.2 pack.1.refs_1_.first
  22.9 0.4 collective-permute-start.3
  23.3 0.0 collective-permute-start.4
  23.3 0.1 rim.1
  23.4 0.2 collective-permute-start.5
  23.6 5.4 %collective-permute-start.6 = (f32[4,8,512]{2,1,0:T(8,128)S(1)}, f32[4,8,512]{2,1,0:T(8,128)S(1)}, u32[]{:S(2)}, u32[]{:S(2)}) collective-permute-start(f32[4,8,512]{2,1,0:T(8,128)S(1)} %get-tuple-element.13), channel_id=1, source_target_pairs={{8,17},{17,8},{9,18},{18,9},{10,19},{19,10},{11,20},{20,11},{12,21... | collective-permute-start | bytes 196616 | tf_op jit(solution)/shard_map/ppermute | solution.py:591
  29.0 0.0 collective-permute-done.3.core_far
  29.0 0.0 copy-done
  29.0 2.3 %faces.1.first.moist_in = f32[8,128,1024]{2,1,0:T(8,128)} custom-call(f32[8,128,1024]{2,1,0:T(8,128)} %get-tuple-element.8.moist_in, f32[2,128,1024]{2,1,0:T(8,128)S(1)} %get-tuple-element.9.core_ref, f32[2,128,1024]{2,1,0:T(8,128)S(1)} %face.1.chip_ref.chip_pair, ...), custom_call_target="tpu_custom_call", output_to_operand_aliasing={{}: (0, {})} | custom-call | flops 2621440 | bytes 4194304 | tf_op jit(solution)/shard_map/faces/pallas_call | solution.py:490
  31.4 0.9 %collective-permute-done.6.cross_ref = f32[4,8,512]{2,1,0:T(8,128)S(1)} collective-permute-done((f32[4,8,512]{2,1,0:T(8,128)S(1)}, f32[4,8,512]{2,1,0:T(8,128)S(1)}, u32[]{:S(2)}, u32[]{:S(2)}) %collective-permute-start.6) | collective-permute-done | bytes 65568 | tf_op jit(solution)/shard_map/ppermute | solution.py:591
  32.3 0.0 collective-permute-done.5.side_ref
  32.3 4.4 %collective-permute-done.4.far_ref = f32[28,8,512]{2,1,0:T(8,128)S(1)} collective-permute-done((f32[28,8,512]{2,1,0:T(8,128)S(1)}, f32[28,8,512]{2,1,0:T(8,128)S(1)}, u32[]{:S(2)}, u32[]{:S(2)}) %collective-permute-start.4) | collective-permute-done | bytes 458784 | tf_op jit(solution)/shard_map/ppermute | solution.py:577
  36.7 0.9 %sweeps.1.own_ref = f32[64,512]{1,0:T(8,128)S(1)} custom-call(f32[9,3,8,1024]{3,2,1,0:T(8,128)S(1)} %get-tuple-element.10.keep_ref, f32[9,3,8,1024]{3,2,1,0:T(8,128)S(1)} %collective-permute-done.2.recv_ref, f32[3,128,256]{2,1,0:T(8,128)S(1)} %pad_maximum_fusion.own_ref, f32[3,128,256]{2,1,0:T(8,128)S(1)} %collective-permute-done.1.refs_2_.other_ref, ...), custom_call_target="tpu_custom_call" | custom-call | flops 4423680 | bytes 2654208 | tf_op jit(solution)/shard_map/sweeps/pallas_call | solution.py:429
  37.6 0.1 collective-permute-start.8
  37.7 1.2 %collective-permute-start.7 = (f32[64,512]{1,0:T(8,128)S(1)}, f32[64,512]{1,0:T(8,128)S(1)}, u32[]{:S(2)}, u32[]{:S(2)}) collective-permute-start(f32[64,512]{1,0:T(8,128)S(1)} %sweeps.1.own_ref), channel_id=1, source_target_pairs={{0,8},{8,0},{16,24},{24,16},{1,9},{9,1},{17,25},{25,17},{2,10},{10... | collective-permute-start | bytes 393224 | tf_op jit(solution)/shard_map/ppermute | solution.py:573
  38.9 2.6 %collective-permute-done.8.chip_far = f32[64,512]{1,0:T(8,128)S(1)} collective-permute-done((f32[64,512]{1,0:T(8,128)S(1)}, f32[64,512]{1,0:T(8,128)S(1)}, u32[]{:S(2)}, u32[]{:S(2)}) %collective-permute-start.8) | collective-permute-done | bytes 131104 | tf_op jit(solution)/shard_map/ppermute | solution.py:577
  41.5 2.1 %collective-permute-start.9 = (f32[64,512]{1,0:T(8,128)S(1)}, f32[64,512]{1,0:T(8,128)S(1)}, u32[]{:S(2)}, u32[]{:S(2)}) collective-permute-start(f32[64,512]{1,0:T(8,128)S(1)} %collective-permute-done.8.chip_far), channel_id=1, source_target_pairs={{0,8},{8,0},{16,24},{24,16},{1,9},{9,1},{17,25},{25,17},{2,10},{10... | collective-permute-start | bytes 393224 | tf_op jit(solution)/shard_map/ppermute | solution.py:573
  43.6 0.0 collective-permute-done.7.core_far
  43.6 1.0 %collective-permute-done.9.both_far = f32[64,512]{1,0:T(8,128)S(1)} collective-permute-done((f32[64,512]{1,0:T(8,128)S(1)}, f32[64,512]{1,0:T(8,128)S(1)}, u32[]{:S(2)}, u32[]{:S(2)}) %collective-permute-start.9) | collective-permute-done | bytes 131104 | tf_op jit(solution)/shard_map/ppermute | solution.py:573
  44.6 2.6 %bottom.1 = (f32[8,128,1024]{2,1,0:T(8,128)}, f32[128,256]{1,0:T(8,128)}) custom-call(f32[8,128,1024]{2,1,0:T(8,128)} %faces.1.first.moist_in, f32[2,128,1024]{2,1,0:T(8,128)S(1)} %face.1.chip_ref.chip_pair, f32[64,512]{1,0:T(8,128)S(1)} %sweeps.1.own_ref, f32[64,512]{1,0:T(8,128)S(1)} %collective-permute-done.7.core_far, ...), custom_call_target="tpu_custom_call", output_to_operand_aliasing={{0}: (0, {})} | custom-call | flops 327680 | bytes 1310720 | tf_op jit(solution)/shard_map/bottom/pallas_call | solution.py:539
  (5 shorter events, 0.1 us)
Async XLA Ops:
  0.6 3.9 %copy-start.1 = (s32[128,256]{1,0:T(8,128)S(1)}, s32[128,256]{1,0:T(8,128)}, u32[]{:S(2)}) copy-start(s32[128,256]{1,0:T(8,128)} %param.18) | copy-start | bytes 393220
  0.6 4.0 %copy-start.2 = (f32[128,256]{1,0:T(8,128)S(1)}, f32[128,256]{1,0:T(8,128)}, u32[]{:S(2)}) copy-start(f32[128,256]{1,0:T(8,128)} %param.19) | copy-start | bytes 393220
  0.7 4.0 %copy-start.3 = (f32[128,256]{1,0:T(8,128)S(1)}, f32[128,256]{1,0:T(8,128)}, u32[]{:S(2)}) copy-start(f32[128,256]{1,0:T(8,128)} %param.17) | copy-start | bytes 393220
  3.8 13.4 %collective-permute-start = (f32[2,128,1024]{2,1,0:T(8,128)S(1)}, f32[2,128,1024]{2,1,0:T(8,128)S(1)}, u32[]{:S(2)}, u32[]{:S(2)}) collective-permute-start(f32[2,128,1024]{2,1,0:T(8,128)S(1)} %face.1.chip_ref.chip_pair), channel_id=1, source_target_pairs={{8,16},{16,8},{9,17},{17,9},{10,18},{18,10},{11,19},{19,11},{12,20... | collective-permute-start | bytes 3145736 | tf_op jit(solution)/shard_map/ppermute | solution.py:581
  4.7 12.5 %collective-permute-start.1 = (f32[3,128,256]{2,1,0:T(8,128)S(1)}, f32[3,128,256]{2,1,0:T(8,128)S(1)}, u32[]{:S(2)}, u32[]{:S(2)}) collective-permute-start(f32[3,128,256]{2,1,0:T(8,128)S(1)} %pad_maximum_fusion.own_ref), channel_id=1, source_target_pairs={{0,8},{8,0},{16,24},{24,16},{1,9},{9,1},{17,25},{25,17},{2,10},{10... | collective-permute-start | bytes 1179656 | tf_op jit(solution)/shard_map/ppermute | solution.py:573
  17.2 5.5 %collective-permute-start.2 = (f32[9,3,8,1024]{3,2,1,0:T(8,128)S(1)}, f32[9,3,8,1024]{3,2,1,0:T(8,128)S(1)}, u32[]{:S(2)}, u32[]{:S(2)}) collective-permute-start(f32[9,3,8,1024]{3,2,1,0:T(8,128)S(1)} %gate.2), channel_id=1, source_target_pairs={{0,8},{8,0},{16,24},{24,16},{1,9},{9,1},{17,25},{25,17},{2,10},{10... | collective-permute-start | bytes 2654216 | tf_op jit(solution)/shard_map/ppermute | solution.py:573
  22.6 6.4 %copy-start = (f32[128,1024]{1,0:T(8,128)S(1)}, f32[128,1024]{1,0:T(8,128)}, u32[]{:S(2)}) copy-start(f32[128,1024]{1,0:T(8,128)} %rain_ref.1) | copy-start | bytes 1572868
  22.9 6.2 %collective-permute-start.3 = (f32[2,128,1024]{2,1,0:T(8,128)S(1)}, f32[2,128,1024]{2,1,0:T(8,128)S(1)}, u32[]{:S(2)}, u32[]{:S(2)}) collective-permute-start(f32[2,128,1024]{2,1,0:T(8,128)S(1)} %gate.3), channel_id=1, source_target_pairs={{0,8},{8,0},{16,24},{24,16},{1,9},{9,1},{17,25},{25,17},{2,10},{10... | collective-permute-start | bytes 3145736 | tf_op jit(solution)/shard_map/ppermute | solution.py:573
  23.3 13.4 %collective-permute-start.4 = (f32[28,8,512]{2,1,0:T(8,128)S(1)}, f32[28,8,512]{2,1,0:T(8,128)S(1)}, u32[]{:S(2)}, u32[]{:S(2)}) collective-permute-start(f32[28,8,512]{2,1,0:T(8,128)S(1)} %pack.1.refs_1_.first), channel_id=1, source_target_pairs={{0,16},{8,24},{16,0},{24,8},{1,17},{9,25},{17,1},{25,9},{2,18},{10... | collective-permute-start | bytes 1376264 | tf_op jit(solution)/shard_map/ppermute | solution.py:577
  23.4 8.9 %collective-permute-start.5 = (f32[7,8,512]{2,1,0:T(8,128)S(1)}, f32[7,8,512]{2,1,0:T(8,128)S(1)}, u32[]{:S(2)}, u32[]{:S(2)}) collective-permute-start(f32[7,8,512]{2,1,0:T(8,128)S(1)} %get-tuple-element.12), channel_id=1, source_target_pairs={{8,1},{1,8},{9,2},{2,9},{10,3},{3,10},{11,4},{4,11},{12,5},{5,12},... | collective-permute-start | bytes 344072 | tf_op jit(solution)/shard_map/ppermute | solution.py:591
  23.6 8.7 %collective-permute-start.6 = (f32[4,8,512]{2,1,0:T(8,128)S(1)}, f32[4,8,512]{2,1,0:T(8,128)S(1)}, u32[]{:S(2)}, u32[]{:S(2)}) collective-permute-start(f32[4,8,512]{2,1,0:T(8,128)S(1)} %get-tuple-element.13), channel_id=1, source_target_pairs={{8,17},{17,8},{9,18},{18,9},{10,19},{19,10},{11,20},{20,11},{12,21... | collective-permute-start | bytes 196616 | tf_op jit(solution)/shard_map/ppermute | solution.py:591
  37.6 3.9 %collective-permute-start.8 = (f32[64,512]{1,0:T(8,128)S(1)}, f32[64,512]{1,0:T(8,128)S(1)}, u32[]{:S(2)}, u32[]{:S(2)}) collective-permute-start(f32[64,512]{1,0:T(8,128)S(1)} %sweeps.1.own_ref), channel_id=1, source_target_pairs={{0,16},{8,24},{16,0},{24,8},{1,17},{9,25},{17,1},{25,9},{2,18},{10... | collective-permute-start | bytes 393224 | tf_op jit(solution)/shard_map/ppermute | solution.py:577
  37.7 5.9 %collective-permute-start.7 = (f32[64,512]{1,0:T(8,128)S(1)}, f32[64,512]{1,0:T(8,128)S(1)}, u32[]{:S(2)}, u32[]{:S(2)}) collective-permute-start(f32[64,512]{1,0:T(8,128)S(1)} %sweeps.1.own_ref), channel_id=1, source_target_pairs={{0,8},{8,0},{16,24},{24,16},{1,9},{9,1},{17,25},{25,17},{2,10},{10... | collective-permute-start | bytes 393224 | tf_op jit(solution)/shard_map/ppermute | solution.py:573
  41.5 3.1 %collective-permute-start.9 = (f32[64,512]{1,0:T(8,128)S(1)}, f32[64,512]{1,0:T(8,128)S(1)}, u32[]{:S(2)}, u32[]{:S(2)}) collective-permute-start(f32[64,512]{1,0:T(8,128)S(1)} %collective-permute-done.8.chip_far), channel_id=1, source_target_pairs={{0,8},{8,0},{16,24},{24,16},{1,9},{9,1},{17,25},{25,17},{2,10},{10... | collective-permute-start | bytes 393224 | tf_op jit(solution)/shard_map/ppermute | solution.py:573

commit v3 on v2

--- a/solution.py
+++ b/solution.py
@@ -24,6 +24,7 @@
 
 VMEM = pl.BlockSpec(memory_space=pltpu.VMEM)
 ANY = pl.BlockSpec(memory_space=pl.ANY)
+HBM = pl.BlockSpec(memory_space=pltpu.HBM)
 
 
 def params(mib):
@@ -59,40 +60,43 @@
         tab[i, :, :classes] = jnp.broadcast_to(ref[...] * scale, (SUB, classes))
 
 
-def face_kernel(sat_ref, alpha_ref, theta_ref, psi_hbm, tex_hbm, act_hbm, out_ref, kinds, acts, tab, sems):
+def face_kernel(
+    sat_hbm, alpha_hbm, psi_hbm, tex_hbm, act_hbm, out_ref, kinds, acts, given, tab, sems
+):
     _, core = place()
     layer = core * (psi_hbm.shape[0] - 1)
-    nrows, cols = psi_hbm.shape[1:]
-    chunk = nrows // 4
-
-    def copies(i):
-        rows = pl.ds(i * chunk, chunk)
-        return [
-            pltpu.make_async_copy(src.at[layer, rows], dst.at[rows], sems.at[i, k])
-            for k, (src, dst) in enumerate(
-                ((psi_hbm, out_ref.at[0]), (tex_hbm, kinds), (act_hbm, acts))
+    cols = psi_hbm.shape[2]
+    classes = sat_hbm.shape[1]
+    copies = [
+        pltpu.make_async_copy(src, dst, sems.at[i])
+        for i, (src, dst) in enumerate(
+            (
+                (sat_hbm, given.at[0]),
+                (alpha_hbm, given.at[1]),
+                (psi_hbm.at[layer], out_ref.at[0]),
+                (tex_hbm.at[layer], kinds),
+                (act_hbm.at[layer], acts),
             )
-        ]
-
-    for i in range(4):
-        for c in copies(i):
-            c.start()
-    fill_tables(tab, sat_ref, alpha_ref, theta_ref)
-    for i in range(4):
-        for c in copies(i):
-            c.wait()
-
-        def columns(q, carry):
-            lanes = pl.ds(pl.multiple_of(q * LANE, LANE), LANE)
-            for r in range(i * chunk, (i + 1) * chunk, SUB):
-                rws = slice(r, r + SUB)
-                kind = kinds[rws, lanes]
-                wet = jnp.exp2(gathered(tab[1], kind) * jnp.minimum(out_ref[0, rws, lanes], 0.0))
-                active = acts[rws, lanes].astype(jnp.float32)
-                out_ref[1, rws, lanes] = gathered(tab[0], kind) * active * (wet * wet)
-            return carry
-
-        lax.fori_loop(0, cols // LANE, columns, 0, unroll=4)
+        )
+    ]
+    for c in copies:
+        c.start()
+    for c in copies:
+        c.wait()
+    for i, scale in enumerate((1.0, 0.5 * math.log2(math.e))):
+        tab[i, :, :classes] = jnp.broadcast_to(given[i] * scale, (SUB, classes))
+
+    def columns(q, carry):
+        lanes = pl.ds(pl.multiple_of(q * LANE, LANE), LANE)
+        for r in range(0, kinds.shape[0], SUB):
+            rws = slice(r, r + SUB)
+            kind = kinds[rws, lanes]
+            wet = jnp.exp2(gathered(tab[1], kind) * jnp.minimum(out_ref[0, rws, lanes], 0.0))
+            active = acts[rws, lanes].astype(jnp.float32)
+            out_ref[1, rws, lanes] = gathered(tab[0], kind) * active * (wet * wet)
+        return carry
+
+    lax.fori_loop(0, cols // LANE, columns, 0, unroll=4)
 
 
 def in_hbm(*arrays):
@@ -104,21 +108,20 @@
     size = nrows * cols
     return pl.pallas_call(
         face_kernel,
-        grid=(1,),
-        in_specs=[pl.BlockSpec(t.shape, lambda j: (0, 0)) for t in tables]
-        + [pl.BlockSpec(memory_space=pltpu.HBM)] * 3,
-        out_specs=pl.BlockSpec((2, nrows, cols), lambda j: (0, 0, 0)),
+        in_specs=[HBM] * 5,
+        out_specs=VMEM,
         out_shape=jax.ShapeDtypeStruct((2, nrows, cols), jnp.float32),
         scratch_shapes=[
             pltpu.VMEM((nrows, cols), jnp.int32),
             pltpu.VMEM((nrows, cols), jnp.int32),
-            pltpu.VMEM((3, SUB, LANE), jnp.float32),
-            pltpu.SemaphoreType.DMA((4, 3)),
+            pltpu.VMEM((2,) + tables[0].shape, jnp.float32),
+            pltpu.VMEM((2, SUB, LANE), jnp.float32),
+            pltpu.SemaphoreType.DMA((5,)),
         ],
         compiler_params=params(8),
         cost_estimate=cost(20 * size, 20 * size, size),
         name="face",
-    )(*in_hbm(*tables, pressure, texture, active))
+    )(*in_hbm(*tables[:2], pressure, texture, active))
 
 
 def soil_kernel(
@@ -257,6 +260,42 @@
     return pltpu.roll(tile, LANE - shift(array, block), 1)
 
 
+def nearest(block, core):
+    return jnp.where(core == 0, block[:SWEEPS], block[SUB - SWEEPS :])
+
+
+def spread(rows, core):
+    zeros = jnp.zeros((SUB - SWEEPS, rows.shape[1]), rows.dtype)
+    return jnp.where(core == 0, jnp.concatenate([rows, zeros], 0), jnp.concatenate([zeros, rows], 0))
+
+
+def put_rows(ref, plane, pieces):
+    used = sum(piece.shape[0] for piece in pieces)
+    spare = jnp.zeros((2 * SUB - used, pieces[0].shape[1]), jnp.float32)
+    rows = jnp.concatenate([*pieces, spare], 0)
+    ref[plane] = rows[:SUB]
+    ref[plane + 1] = rows[SUB:]
+
+
+def get_rows(ref, plane, counts):
+    rows = jnp.concatenate([ref[plane], ref[plane + 1]], 0)
+    out, at = [], 0
+    for count in counts:
+        out.append(rows[at : at + count])
+        at += count
+    return out
+
+
+def fold(tiles):
+    mid = SUB // 2
+    return jnp.concatenate([part for tile in tiles for part in (tile[:mid], tile[mid:])], 1)
+
+
+def unfold(rows):
+    parts = [rows[:, i : i + LANE] for i in range(0, rows.shape[1], LANE)]
+    return [jnp.concatenate(parts[i : i + 2], 0) for i in range(0, len(parts), 2)]
+
+
 def half_lanes(which, half):
     return pl.ds(pl.multiple_of(which * half, half), half)
 
@@ -291,29 +330,32 @@
     half = cols // 2
     away = half_lanes(1 - chip, half)
     slab = slab_lanes(chip, half)
+    main = 3 * (blocks - 1)
     tiles = [None] * -(-blocks // SHARE)
-    for b in range(blocks):
-        out_ref[3 * b : 3 * b + 3] = keep_ref[b, :, :, away] + recv_ref[b, :, :, away]
+    for j in range(blocks):
+        b = j + core if j < blocks - 1 else (1 - core) * (blocks - 1)
+        sums = [keep_ref[b, a, :, away] + recv_ref[b, a, :, away] for a in range(3)]
+        if j < blocks - 1:
+            for a in range(3):
+                out_ref[3 * j + a] = sums[a]
+        else:
+            rows = [nearest(v, core) for v in sums]
         pieces = [keep_ref[b, a, :, slab] + recv_ref[b, a, :, slab] for a in range(3)]
         pieces += edge_inputs(own_ref, other_ref, chip, core, first_row(core, blocks, b))
-        piece = packed(pieces, chip, b % SHARE)
-        i = b // SHARE
+        piece = packed(pieces, chip, j % SHARE)
+        i = j // SHARE
         tiles[i] = piece if tiles[i] is None else tiles[i] + piece
-    per = half // LANE
-    for i, tile in enumerate(tiles):
-        out_ref[3 * blocks + i // per, :, (i % per) * LANE : (i % per + 1) * LANE] = tile
+    put_rows(out_ref, main, [*rows, fold(tiles)])
 
 
 def pack(keep, recv, own, other):
     blocks, _, _, cols = keep.shape
     half = cols // 2
-    tiles = -(-blocks // SHARE)
-    planes = 3 * blocks - (-tiles // (half // LANE))
     return pl.pallas_call(
         pack_kernel,
         in_specs=[VMEM] * 4,
         out_specs=VMEM,
-        out_shape=jax.ShapeDtypeStruct((planes, SUB, half), jnp.float32),
+        out_shape=jax.ShapeDtypeStruct((3 * blocks - 1, SUB, half), jnp.float32),
         compiler_params=params(8),
         cost_estimate=cost(keep.size, 12 * keep.size),
         name="pack",
@@ -330,7 +372,7 @@
     row = first_row(core, blocks, b)
     near, away = half_lanes(chip, half), half_lanes(1 - chip, half)
     side_ref[:3] = keep_ref[b, :, :, near] + recv_ref[b, :, :, near]
-    cross_ref[:3] = keep_ref[b, :, :, away] + recv_ref[b, :, :, away]
+    rows = [nearest(keep_ref[b, a, :, away] + recv_ref[b, a, :, away], core) for a in range(3)]
     for which in range(2):
         for a in range(3):
             side_ref[3 + a, :, which * tile : (which + 1) * tile] = tile_rows(
@@ -342,7 +384,9 @@
 
     side_ref[6, :, :LANE] = packed(sums(slab_lanes(1 - chip, half)), 1 - chip)
     inputs = edge_inputs(own_ref, other_ref, chip, core, row)
-    cross_ref[3, :, :LANE] = packed(sums(slab_lanes(chip, half)) + inputs, chip)
+    halo = nearest(packed(sums(slab_lanes(chip, half)) + inputs, chip), core)
+    spare = jnp.zeros((SWEEPS, half - LANE), jnp.float32)
+    put_rows(cross_ref, 0, [*rows, jnp.concatenate([halo, spare], 1)])
 
 
 def rim(keep, recv, own, other, first):
@@ -351,46 +395,51 @@
         rim_kernel,
         in_specs=[VMEM] * 4 + [ANY],
         out_specs=[VMEM] * 2,
-        out_shape=[jax.ShapeDtypeStruct((n, SUB, half), jnp.float32) for n in (7, 4)],
+        out_shape=[jax.ShapeDtypeStruct((n, SUB, half), jnp.float32) for n in (7, 2)],
         compiler_params=params(8),
         cost_estimate=cost(keep.size // 8, keep.size),
         name="rim",
     )(keep, recv, own, other, first)
 
 
-def sweep_kernel(keep_ref, recv_ref, own_ref, other_ref, far_ref, side_ref, cross_ref, first, out_ref, work):
-    del first
+def sweep_kernel(keep_ref, recv_ref, own_ref, other_ref, far_ref, side_ref, cross_ref, out_ref, work):
     chip, core = place()
     strip = lax.axis_index("strips")
     blocks, _, _, cols = keep_ref.shape
     half = cols // 2
     tile = half // 2
-    per = half // LANE
+    main = 3 * (blocks - 1)
 
     def cells(at, lanes, sums, inputs):
         trans = sums[0] * layer_thick
         store = spec_yield + sums[1] * layer_thick
         old, river, inflow = inputs
-        rows = slice(at * SUB, (at + 1) * SUB)
+        rows = pl.ds(pl.multiple_of(at * SUB, SUB), SUB)
         work[0, rows, lanes] = trans
         work[1, rows, lanes] = store + river
         work[2, rows, lanes] = store * old + leak_rate * layer_thick * sums[2] + inflow
         work[3, rows, lanes] = old
 
     def halo(at, sums, inputs):
-        cells(at, slice(half, half + LANE), [on_edge(v, 1 - chip) for v in sums], [on_edge(v, 1 - chip) for v in inputs])
+        sums, inputs = ([on_edge(v, 1 - chip) for v in values] for values in (sums, inputs))
+        cells(at, slice(half, half + LANE), sums, inputs)
 
     near, slab = half_lanes(chip, half), slab_lanes(1 - chip, half)
-    for b in range(blocks):
-        sums = [keep_ref[b, a, :, near] + recv_ref[b, a, :, near] + far_ref[3 * b + a] for a in range(3)]
+    *beyond, tiles = get_rows(far_ref, main, (SWEEPS, SWEEPS, SWEEPS, SUB // 2))
+    tiles = unfold(tiles)
+    for j in range(blocks):
+        b = j + core if j < blocks - 1 else (1 - core) * (blocks - 1)
+        if j < blocks - 1:
+            far = [far_ref[3 * j + a] for a in range(3)]
+        else:
+            far = [spread(v, core) for v in beyond]
+        sums = [keep_ref[b, a, :, near] + recv_ref[b, a, :, near] + far[a] for a in range(3)]
         first_at = first_row(core, blocks, b)
         for which in range(2):
             lanes = slice(which * tile, (which + 1) * tile)
             inputs = [tile_rows(own_ref, other_ref, core, which, a, first_at, slice(0, tile)) for a in range(3)]
             cells(b, lanes, [s[:, lanes] for s in sums], inputs)
-        i = b // SHARE
-        far = far_ref[3 * blocks + i // per, :, (i % per) * LANE : (i % per + 1) * LANE]
-        far = [unpacked(far, a, b % SHARE) for a in range(6)]
+        far = [unpacked(tiles[j // SHARE], a, j % SHARE) for a in range(6)]
         sums = [keep_ref[b, a, :, slab] + recv_ref[b, a, :, slab] + far[a] for a in range(3)]
         halo(b, sums, far[3:])
     outside = ((core == 0) & (strip == 0)) | ((core == 1) & (strip == lax.axis_size("strips") - 1))
@@ -398,9 +447,10 @@
     def inside(value):
         return jnp.where(outside, 0.0, value)
 
-    sums = [inside(side_ref[a] + cross_ref[a]) for a in range(3)]
+    *cross, corner = [spread(v, 1 - core) for v in get_rows(cross_ref, 0, (SWEEPS,) * 4)]
+    sums = [inside(side_ref[a] + cross[a]) for a in range(3)]
     cells(blocks, slice(0, half), sums, [inside(side_ref[3 + a]) for a in range(3)])
-    side, cross = side_ref[6, :, :LANE], cross_ref[3, :, :LANE]
+    side, cross = side_ref[6, :, :LANE], corner[:, :LANE]
     sums = [inside(unpacked(side, a) + unpacked(cross, a)) for a in range(3)]
     halo(blocks, sums, [inside(unpacked(cross, a)) for a in range(3, 6)])
 
@@ -423,35 +473,37 @@
     out_ref[...] = work[0, pl.ds(pl.multiple_of(core * SUB, SUB), out_ref.shape[0]), :half]
 
 
-def sweeps(keep, recv, own, other, far, side, cross, first):
+def sweeps(keep, recv, own, other, far, side, cross):
     blocks = keep.shape[0]
     half = keep.shape[3] // 2
     return pl.pallas_call(
         sweep_kernel,
-        in_specs=[VMEM] * 7 + [pl.BlockSpec(memory_space=pltpu.HBM)],
+        in_specs=[VMEM] * 7,
         out_specs=VMEM,
         out_shape=jax.ShapeDtypeStruct(((blocks - 1) * SUB, half), jnp.float32),
         scratch_shapes=[pltpu.VMEM((4, (blocks + 1) * SUB, half + LANE), jnp.float32)],
         compiler_params=params(12),
         cost_estimate=cost(20 * keep.size, 12 * keep.size),
         name="sweeps",
-    )(keep, recv, own, other, far, side, cross, *in_hbm(first))
-
-
-def faces_kernel(moist_in, core_ref, chip_ref, core_far, chip_far, rain_ref, moist_out, ends, sems):
+    )(keep, recv, own, other, far, side, cross)
+
+
+def faces_kernel(moist_in, core_ref, chip_ref, core_far, chip_far, rain_ref, moist_out, tail_ref, ends, sems):
     del moist_in
     chip, core = place()
     layers = moist_out.shape[0]
-    loads = [
-        pltpu.make_async_copy(moist_out.at[layer], ends.at[i], sems.at[i])
-        for i, layer in enumerate((0, layers - 1))
+    copies = [
+        (moist_out.at[layer], ends.at[i], sems.at[i]) for i, layer in enumerate((0, layers - 1))
     ]
+    loads = [pltpu.make_async_copy(src, dst, sem) for src, dst, sem in copies]
+    stores = [pltpu.make_async_copy(dst, src, sem) for src, dst, sem in copies]
     for c in loads:
         c.start()
     for c in loads:
         c.wait()
     gain = soil_step / layer_thick
     face = 0.5 * gain
+    last = (core == 1) & (chip == 1)
 
     def flux(upper, lower):
         return (upper[1] + lower[1]) * ((upper[0] - lower[0]) * (face / layer_thick) + face)
@@ -476,22 +528,31 @@
     def _():
         ends[1] = ends[1] - flux(chip_ref, chip_far)
 
-    stores = [
-        pltpu.make_async_copy(ends.at[i], moist_out.at[layer], sems.at[i])
-        for i, layer in enumerate((0, layers - 1))
-    ]
-    for c in stores:
-        c.start()
-    for c in stores:
-        c.wait()
+    stores[0].start()
+
+    @pl.when(last)
+    def _():
+        slope = chip_ref[1] * (gain / (0.5 * layer_thick))
+        tail_ref[0] = ends[1] - (chip_ref[0] * slope + gain * chip_ref[1])
+        tail_ref[1] = slope
+
+    @pl.when(jnp.logical_not(last))
+    def _():
+        stores[1].start()
+        stores[1].wait()
+
+    stores[0].wait()
 
 
 def faces(moist, core_pair, chip_pair, core_far, chip_far, rain):
     return pl.pallas_call(
         faces_kernel,
         in_specs=[ANY] + [VMEM] * 5,
-        out_specs=ANY,
-        out_shape=jax.ShapeDtypeStruct(moist.shape, moist.dtype),
+        out_specs=[ANY, VMEM],
+        out_shape=[
+            jax.ShapeDtypeStruct(moist.shape, moist.dtype),
+            jax.ShapeDtypeStruct((2,) + moist.shape[1:], moist.dtype),
+        ],
         input_output_aliases={0: 0},
         scratch_shapes=[pltpu.VMEM((2,) + moist.shape[1:], jnp.float32), pltpu.SemaphoreType.DMA((2,))],
         compiler_params=params(12),
@@ -500,9 +561,7 @@
     )(moist, core_pair, chip_pair, core_far, chip_far, rain)
 
 
-def bottom_kernel(
-    moist_in, chip_pair, own_ref, core_far, chip_far, both_far, moist_out, head_ref, last, sem
-):
+def bottom_kernel(moist_in, tail_ref, own_ref, core_far, chip_far, both_far, moist_out, head_ref, last, sems):
     del moist_in
     chip, core = place()
     layers = moist_out.shape[0]
@@ -513,28 +572,24 @@
 
     @pl.when((core == 1) & (chip == 1))
     def _():
-        load = pltpu.make_async_copy(moist_out.at[layers - 1], last, sem)
-        load.start()
-        load.wait()
-        gain = soil_step / layer_thick
-        for ref, where, lanes in (
-            (own_ref, mine, slice(half, 2 * half)),
-            (core_far, theirs, slice(half, 2 * half)),
-            (chip_far, mine, slice(0, half)),
-            (both_far, theirs, slice(0, half)),
-        ):
-            drop = (chip_pair[0, where, lanes] - ref[...]) / (0.5 * layer_thick) + 1.0
-            last[where, lanes] = last[where, lanes] - gain * chip_pair[1, where, lanes] * drop
-        store = pltpu.make_async_copy(last, moist_out.at[layers - 1], sem)
-        store.start()
-        store.wait()
+        copies = []
+        for i, (left, right) in enumerate(((both_far, core_far), (chip_far, own_ref))):
+            where = slice(i * rows, (i + 1) * rows)
+            for ref, lanes in ((left, slice(0, half)), (right, slice(half, 2 * half))):
+                last[where, lanes] = tail_ref[0, where, lanes] + tail_ref[1, where, lanes] * ref[...]
+            copies.append(
+                pltpu.make_async_copy(last.at[where], moist_out.at[layers - 1, where], sems.at[i])
+            )
+            copies[-1].start()
+        for c in copies:
+            c.wait()
 
     lanes = pl.ds(pl.multiple_of(core * tile, tile), tile)
     head_ref[mine, :] = own_ref[:, lanes]
     head_ref[theirs, :] = core_far[:, lanes]
 
 
-def bottom(moist, chip_pair, own, core_far, chip_far, both_far):
+def bottom(moist, tail, own, core_far, chip_far, both_far):
     rows, half = own.shape
     return pl.pallas_call(
         bottom_kernel,
@@ -545,28 +600,49 @@
             jax.ShapeDtypeStruct((2 * rows, half // 2), jnp.float32),
         ],
         input_output_aliases={0: 0},
-        scratch_shapes=[pltpu.VMEM(moist.shape[1:], jnp.float32), pltpu.SemaphoreType.DMA],
+        scratch_shapes=[pltpu.VMEM(moist.shape[1:], jnp.float32), pltpu.SemaphoreType.DMA((2,))],
         compiler_params=params(12),
         cost_estimate=cost(10 * own.size, 40 * own.size),
         name="bottom",
-    )(moist, chip_pair, own, core_far, chip_far, both_far)
+    )(moist, tail, own, core_far, chip_far, both_far)
+
+
+def inputs_kernel(old_ref, code_ref, section_ref, first, out_ref):
+    del first
+    code = code_ref[...]
+    river = jnp.where(code == 1, river_cond, jnp.where(code == 2, fixed_cond, 0.0))
+    out_ref[0] = old_ref[...]
+    out_ref[1] = river
+    out_ref[2] = river * section_ref[...]
+
+
+def inputs(head_old, cell_code, section, first):
+    return pl.pallas_call(
+        inputs_kernel,
+        in_specs=[VMEM] * 3 + [ANY],
+        out_specs=VMEM,
+        out_shape=jax.ShapeDtypeStruct((3,) + head_old.shape, jnp.float32),
+        compiler_params=params(4),
+        cost_estimate=cost(4 * head_old.size, 24 * head_old.size),
+        name="inputs",
+    )(head_old, cell_code, section, first)
 
 
 def gate_kernel(*refs):
     del refs
 
 
-def gate(value, *first):
+def gate(value, *first, stored=()):
     return pl.pallas_call(
         gate_kernel,
-        in_specs=[ANY] * (1 + len(first)),
+        in_specs=[ANY] * (1 + len(first)) + [HBM] * len(stored),
         out_specs=ANY,
         out_shape=jax.ShapeDtypeStruct(value.shape, value.dtype),
         input_output_aliases={0: 0},
         compiler_params=params(1),
         cost_estimate=cost(1, 1),
         name="gate",
-    )(value, *first)
+    )(value, *first, *in_hbm(*stored))
 
 
 def core_swap(value):
@@ -592,29 +668,24 @@
 
 
 def shards(pressure, texture, active, rain, k_sat, alpha, theta_sat, head_old, cell_code, section):
-    river = jnp.where(
-        cell_code == 1,
-        jnp.float32(river_cond),
-        jnp.where(cell_code == 2, jnp.float32(fixed_cond), jnp.float32(0.0)),
-    )
-    own = jnp.stack([head_old, river, river * section])
-    other = core_swap(own)
     tables = (k_sat[None], alpha[None], theta_sat[None])
     chip_pair = face(tables, pressure, texture, active)
     chip_far = middle_swap(chip_pair)
+    own = inputs(head_old, cell_code, section, chip_pair)
+    other = core_swap(own)
     moist, keep, send, core_pair = soil(tables, pressure, texture, active)
-    recv = core_swap(gate(send, chip_far, other))
+    recv = core_swap(gate(send, other))
+    keep = gate(keep, chip_far)
     message = pack(keep, recv, own, other)
     far = chip_swap(message)
     side, cross = rim(keep, recv, own, other, message)
-    side, cross = strip_swap(side), strip_swap(cross, 2)
-    core_far = core_swap(gate(core_pair, message))
-    moist = faces(moist, core_pair, chip_pair, core_far, chip_far, rain)
-    heads = sweeps(keep, recv, own, other, far, side, cross, moist)
-    heads_chip = chip_swap(heads)
+    heads = sweeps(keep, recv, own, other, far, strip_swap(side), strip_swap(cross, 2))
+    core_far = core_swap(gate(core_pair, side))
+    moist, tail = faces(moist, core_pair, chip_pair, core_far, chip_far, rain)
+    heads_chip = gate(chip_swap(heads), stored=(moist,))
     heads_core = core_swap(heads)
     heads_both = core_swap(heads_chip)
-    return bottom(moist, chip_pair, heads, heads_core, heads_chip, heads_both)
+    return bottom(moist, tail, heads, heads_core, heads_chip, heads_both)
 
 
 def solution(mesh):

time: 47.4 us -> 42.5 us (0.90)
  the two profiles are of different devices: /device:TPU:31 before, /device:TPU:0 now
where the time goes in v3:
time: 42.5 us; the launch traced here: 42.3 us
  Pallas kernels  17.3 us (41%)
  starting transfers between devices  13 us (31%)
  waiting for transfers between devices  11.2 us (26%)
  between operations  0.75 us (2%)
    pallas_call x1, Pallas kernels, soil(): pl.pallas_call(soil_kernel, grid=(nrows // rows,), in_specs=[whole, whole...  10.6 us
    ppermute x2, waiting for transfers between devices, strip_swap(): return lax.ppermute(value, ('depth', 'strips'), pairs)  6.55 us
    ppermute x5, starting transfers between devices, core_swap(): lax.ppermute(value, 'depth', [(i, i ^ 1) for i in range(lax.axis_size('de...  4.86 us
    ppermute x2, starting transfers between devices, strip_swap(): return lax.ppermute(value, ('depth', 'strips'), pairs)  4.79 us
    ppermute x5, waiting for transfers between devices, core_swap(): lax.ppermute(value, 'depth', [(i, i ^ 1) for i in range(lax.axis_size('de...  3.4 us
    ppermute x2, starting transfers between devices, chip_swap(): lax.ppermute(value, 'depth', [(i, i ^ 2) for i in range(lax.axis_size('de...  2.61 us
    pallas_call x1, Pallas kernels, faces(): pl.pallas_call(faces_kernel, in_specs=[ANY] + [VMEM] * 5, out_specs=[ANY,...  2.4 us
    pallas_call x1, Pallas kernels, face(): pl.pallas_call(face_kernel, in_specs=[HBM] * 5, out_specs=VMEM, out_shape...  2.3 us
  transfers between devices with their start and end apart: 10, of which 5 were waited for; matrix products, arithmetic and copies ran while one was open for 0% of the time, Pallas kernels for 33%

profile of v3, /device:TPU:0, one launch (start us, length us, event | category | flops | bytes accessed | tf_op | source)
XLA Modules:
  0.0 42.3 jit_solution(2211545551657461651)
XLA Ops:
  0.6 0.0 copy-start.1
  0.6 0.0 copy-start.2
  0.7 0.0 copy-start.3
  0.7 2.3 %face.1.first.chip_ref = f32[2,128,1024]{2,1,0:T(8,128)S(1)} custom-call(f32[1,12]{1,0:T(1,128)} %bitcast.3, f32[1,12]{1,0:T(1,128)} %bitcast.5, f32[8,128,1024]{2,1,0:T(8,128)} %psi_hbm.1, s32[8,128,1024]{2,1,0:T(8,128)} %tex_hbm.1, s32[8,128,1024]{2,1,0:T(8,128)} %act_hbm.1), custom_call_target="tpu_custom_call" | custom-call | flops 2621440 | bytes 2621440 | tf_op jit(solution)/shard_map/face/pallas_call | solution.py:109
  3.0 0.0 copy-done.1
  3.0 0.0 copy-done.2
  3.0 0.0 copy-done.3
  3.0 0.5 %collective-permute-start.1 = (f32[3,128,256]{2,1,0:T(8,128)S(1)}, f32[3,128,256]{2,1,0:T(8,128)S(1)}, u32[]{:S(2)}, u32[]{:S(2)}) collective-permute-start(f32[3,128,256]{2,1,0:T(8,128)S(1)} %inputs.1.own_ref), channel_id=1, source_target_pairs={{0,8},{8,0},{16,24},{24,16},{1,9},{9,1},{17,25},{25,17},{2,10},{10... | collective-permute-start | bytes 1179656 | tf_op jit(solution)/shard_map/ppermute | solution.py:649
  3.6 0.7 %collective-permute-start = (f32[2,128,1024]{2,1,0:T(8,128)S(1)}, f32[2,128,1024]{2,1,0:T(8,128)S(1)}, u32[]{:S(2)}, u32[]{:S(2)}) collective-permute-start(f32[2,128,1024]{2,1,0:T(8,128)S(1)} %face.1.first.chip_ref), channel_id=1, source_target_pairs={{8,16},{16,8},{9,17},{17,9},{10,18},{18,10},{11,19},{19,11},{12,20... | collective-permute-start | bytes 3145736 | tf_op jit(solution)/shard_map/ppermute | solution.py:657
  4.3 10.6 %soil.1 = (f32[8,128,1024]{2,1,0:T(8,128)}, f32[9,3,8,1024]{3,2,1,0:T(8,128)S(1)}, f32[9,3,8,1024]{3,2,1,0:T(8,128)S(1)}, f32[2,128,1024]{2,1,0:T(8,128)S(1)}) custom-call(f32[1,12]{1,0:T(1,128)} %bitcast.4, f32[1,12]{1,0:T(1,128)} %bitcast.6, f32[1,12]{1,0:T(1,128)} %bitcast.7, f32[8,128,1024]{2,1,0:T(8,128)} %psi_hbm.1, s32[8,128,1024]{2,1,0:T(8,128)} %tex_hbm.1, ...), custom_call_target="tpu_custom_call" | custom-call | flops 62914560 | bytes 20971520 | tf_op jit(solution)/shard_map/soil/pallas_call | solution.py:218
  14.9 0.0 collective-permute-done.1.refs_1_.other_ref
  14.9 3.9 %collective-permute-start.2 = (f32[9,3,8,1024]{3,2,1,0:T(8,128)S(1)}, f32[9,3,8,1024]{3,2,1,0:T(8,128)S(1)}, u32[]{:S(2)}, u32[]{:S(2)}) collective-permute-start(f32[9,3,8,1024]{3,2,1,0:T(8,128)S(1)} %gate.5), channel_id=1, source_target_pairs={{0,8},{8,0},{16,24},{24,16},{1,9},{9,1},{17,25},{25,17},{2,10},{10... | collective-permute-start | bytes 2654216 | tf_op jit(solution)/shard_map/ppermute | solution.py:649
  18.7 0.0 collective-permute-done.refs_1_.chip_far
  18.8 2.0 %collective-permute-done.2.recv_ref = f32[9,3,8,1024]{3,2,1,0:T(8,128)S(1)} collective-permute-done((f32[9,3,8,1024]{3,2,1,0:T(8,128)S(1)}, f32[9,3,8,1024]{3,2,1,0:T(8,128)S(1)}, u32[]{:S(2)}, u32[]{:S(2)}) %collective-permute-start.2) | collective-permute-done | bytes 884768 | tf_op jit(solution)/shard_map/ppermute | solution.py:649
  20.8 0.2 pack.1.first
  21.0 0.1 copy.20.refs_0_
  21.1 0.0 copy-start
  21.1 0.1 rim.1
  21.2 0.4 %collective-permute-start.3 = (f32[2,128,1024]{2,1,0:T(8,128)S(1)}, f32[2,128,1024]{2,1,0:T(8,128)S(1)}, u32[]{:S(2)}, u32[]{:S(2)}) collective-permute-start(f32[2,128,1024]{2,1,0:T(8,128)S(1)} %gate.6), channel_id=1, source_target_pairs={{0,8},{8,0},{16,24},{24,16},{1,9},{9,1},{17,25},{25,17},{2,10},{10... | collective-permute-start | bytes 3145736 | tf_op jit(solution)/shard_map/ppermute | solution.py:649
  21.6 1.1 %collective-permute-start.4 = (f32[26,8,512]{2,1,0:T(8,128)S(1)}, f32[26,8,512]{2,1,0:T(8,128)S(1)}, u32[]{:S(2)}, u32[]{:S(2)}) collective-permute-start(f32[26,8,512]{2,1,0:T(8,128)S(1)} %pack.1.first), channel_id=1, source_target_pairs={{0,16},{8,24},{16,0},{24,8},{1,17},{9,25},{17,1},{25,9},{2,18},{10... | collective-permute-start | bytes 1277960 | tf_op jit(solution)/shard_map/ppermute | solution.py:653
  22.7 4.3 %collective-permute-start.5 = (f32[7,8,512]{2,1,0:T(8,128)S(1)}, f32[7,8,512]{2,1,0:T(8,128)S(1)}, u32[]{:S(2)}, u32[]{:S(2)}) collective-permute-start(f32[7,8,512]{2,1,0:T(8,128)S(1)} %get-tuple-element.14.refs_1_), channel_id=1, source_target_pairs={{8,1},{1,8},{9,2},{2,9},{10,3},{3,10},{11,4},{4,11},{12,5},{5,12},... | collective-permute-start | bytes 344072 | tf_op jit(solution)/shard_map/ppermute | solution.py:667
  27.0 0.5 %collective-permute-start.6 = (f32[2,8,512]{2,1,0:T(8,128)S(1)}, f32[2,8,512]{2,1,0:T(8,128)S(1)}, u32[]{:S(2)}, u32[]{:S(2)}) collective-permute-start(f32[2,8,512]{2,1,0:T(8,128)S(1)} %get-tuple-element.17), channel_id=1, source_target_pairs={{8,17},{17,8},{9,18},{18,9},{10,19},{19,10},{11,20},{20,11},{12,21... | collective-permute-start | bytes 98312 | tf_op jit(solution)/shard_map/ppermute | solution.py:667
  27.5 6.5 %collective-permute-done.6.cross_ref = f32[2,8,512]{2,1,0:T(8,128)S(1)} collective-permute-done((f32[2,8,512]{2,1,0:T(8,128)S(1)}, f32[2,8,512]{2,1,0:T(8,128)S(1)}, u32[]{:S(2)}, u32[]{:S(2)}) %collective-permute-start.6) | collective-permute-done | bytes 32800 | tf_op jit(solution)/shard_map/ppermute | solution.py:667
  34.1 0.0 collective-permute-done.5.side_ref
  34.1 0.1 collective-permute-done.4.far_ref
  34.2 1.1 %sweeps.1.own_ref = f32[64,512]{1,0:T(8,128)S(1)} custom-call(f32[9,3,8,1024]{3,2,1,0:T(8,128)S(1)} %gate.4.keep_ref, f32[9,3,8,1024]{3,2,1,0:T(8,128)S(1)} %collective-permute-done.2.recv_ref, f32[3,128,256]{2,1,0:T(8,128)S(1)} %inputs.1.own_ref, f32[3,128,256]{2,1,0:T(8,128)S(1)} %collective-permute-done.1.refs_1_.other_ref, ...), custom_call_target="tpu_custom_call" | custom-call | flops 4423680 | bytes 2654208 | tf_op jit(solution)/shard_map/sweeps/pallas_call | solution.py:479
  35.3 1.5 %collective-permute-start.8 = (f32[64,512]{1,0:T(8,128)S(1)}, f32[64,512]{1,0:T(8,128)S(1)}, u32[]{:S(2)}, u32[]{:S(2)}) collective-permute-start(f32[64,512]{1,0:T(8,128)S(1)} %sweeps.1.own_ref), channel_id=1, source_target_pairs={{0,16},{8,24},{16,0},{24,8},{1,17},{9,25},{17,1},{25,9},{2,18},{10... | collective-permute-start | bytes 393224 | tf_op jit(solution)/shard_map/ppermute | solution.py:653
  36.8 0.0 collective-permute-start.7
  36.8 0.0 collective-permute-done.3.core_far
  36.8 0.0 copy-done
  36.8 2.4 %faces.1 = (f32[8,128,1024]{2,1,0:T(8,128)}, f32[2,128,1024]{2,1,0:T(8,128)S(1)}) custom-call(f32[8,128,1024]{2,1,0:T(8,128)} %get-tuple-element.10.moist_in, f32[2,128,1024]{2,1,0:T(8,128)S(1)} %get-tuple-element.11.core_ref, f32[2,128,1024]{2,1,0:T(8,128)S(1)} %face.1.first.chip_ref, ...), custom_call_target="tpu_custom_call", output_to_operand_aliasing={{0}: (0, {})} | custom-call | flops 2621440 | bytes 4194304 | tf_op jit(solution)/shard_map/faces/pallas_call | solution.py:548
  39.2 1.1 %collective-permute-done.8.refs_0_ = f32[64,512]{1,0:T(8,128)S(1)} collective-permute-done((f32[64,512]{1,0:T(8,128)S(1)}, f32[64,512]{1,0:T(8,128)S(1)}, u32[]{:S(2)}, u32[]{:S(2)}) %collective-permute-start.8) | collective-permute-done | bytes 131104 | tf_op jit(solution)/shard_map/ppermute | solution.py:653
  40.3 0.0 collective-permute-start.9
  40.3 0.0 collective-permute-done.7.core_far
  40.3 1.3 %collective-permute-done.9.both_far = f32[64,512]{1,0:T(8,128)S(1)} collective-permute-done((f32[64,512]{1,0:T(8,128)S(1)}, f32[64,512]{1,0:T(8,128)S(1)}, u32[]{:S(2)}, u32[]{:S(2)}) %collective-permute-start.9) | collective-permute-done | bytes 131104 | tf_op jit(solution)/shard_map/ppermute | solution.py:649
  41.7 0.7 %bottom.1 = (f32[8,128,1024]{2,1,0:T(8,128)}, f32[128,256]{1,0:T(8,128)}) custom-call(f32[8,128,1024]{2,1,0:T(8,128)} %get-tuple-element.15.refs_1_.moist_in, f32[2,128,1024]{2,1,0:T(8,128)S(1)} %get-tuple-element.16.tail_ref, f32[64,512]{1,0:T(8,128)S(1)} %sweeps.1.own_ref, ...), custom_call_target="tpu_custom_call", output_to_operand_aliasing={{0}: (0, {})} | custom-call | flops 327680 | bytes 1310720 | tf_op jit(solution)/shard_map/bottom/pallas_call | solution.py:594
  (5 shorter events, 0.0 us)
Async XLA Ops:
  0.6 2.3 %copy-start.1 = (f32[128,256]{1,0:T(8,128)S(1)}, f32[128,256]{1,0:T(8,128)}, u32[]{:S(2)}) copy-start(f32[128,256]{1,0:T(8,128)} %old_ref.1) | copy-start | bytes 393220
  0.6 2.3 %copy-start.2 = (s32[128,256]{1,0:T(8,128)S(1)}, s32[128,256]{1,0:T(8,128)}, u32[]{:S(2)}) copy-start(s32[128,256]{1,0:T(8,128)} %code_ref.1) | copy-start | bytes 393220
  0.7 2.3 %copy-start.3 = (f32[128,256]{1,0:T(8,128)S(1)}, f32[128,256]{1,0:T(8,128)}, u32[]{:S(2)}) copy-start(f32[128,256]{1,0:T(8,128)} %section_ref.1) | copy-start | bytes 393220
  3.0 11.8 %collective-permute-start.1 = (f32[3,128,256]{2,1,0:T(8,128)S(1)}, f32[3,128,256]{2,1,0:T(8,128)S(1)}, u32[]{:S(2)}, u32[]{:S(2)}) collective-permute-start(f32[3,128,256]{2,1,0:T(8,128)S(1)} %inputs.1.own_ref), channel_id=1, source_target_pairs={{0,8},{8,0},{16,24},{24,16},{1,9},{9,1},{17,25},{25,17},{2,10},{10... | collective-permute-start | bytes 1179656 | tf_op jit(solution)/shard_map/ppermute | solution.py:649
  3.6 15.2 %collective-permute-start = (f32[2,128,1024]{2,1,0:T(8,128)S(1)}, f32[2,128,1024]{2,1,0:T(8,128)S(1)}, u32[]{:S(2)}, u32[]{:S(2)}) collective-permute-start(f32[2,128,1024]{2,1,0:T(8,128)S(1)} %face.1.first.chip_ref), channel_id=1, source_target_pairs={{8,16},{16,8},{9,17},{17,9},{10,18},{18,10},{11,19},{19,11},{12,20... | collective-permute-start | bytes 3145736 | tf_op jit(solution)/shard_map/ppermute | solution.py:657
  14.9 5.9 %collective-permute-start.2 = (f32[9,3,8,1024]{3,2,1,0:T(8,128)S(1)}, f32[9,3,8,1024]{3,2,1,0:T(8,128)S(1)}, u32[]{:S(2)}, u32[]{:S(2)}) collective-permute-start(f32[9,3,8,1024]{3,2,1,0:T(8,128)S(1)} %gate.5), channel_id=1, source_target_pairs={{0,8},{8,0},{16,24},{24,16},{1,9},{9,1},{17,25},{25,17},{2,10},{10... | collective-permute-start | bytes 2654216 | tf_op jit(solution)/shard_map/ppermute | solution.py:649
  21.1 15.7 %copy-start = (f32[128,1024]{1,0:T(8,128)S(1)}, f32[128,1024]{1,0:T(8,128)}, u32[]{:S(2)}) copy-start(f32[128,1024]{1,0:T(8,128)} %rain_ref.1) | copy-start | bytes 1572868
  21.2 15.6 %collective-permute-start.3 = (f32[2,128,1024]{2,1,0:T(8,128)S(1)}, f32[2,128,1024]{2,1,0:T(8,128)S(1)}, u32[]{:S(2)}, u32[]{:S(2)}) collective-permute-start(f32[2,128,1024]{2,1,0:T(8,128)S(1)} %gate.6), channel_id=1, source_target_pairs={{0,8},{8,0},{16,24},{24,16},{1,9},{9,1},{17,25},{25,17},{2,10},{10... | collective-permute-start | bytes 3145736 | tf_op jit(solution)/shard_map/ppermute | solution.py:649
  21.6 12.6 %collective-permute-start.4 = (f32[26,8,512]{2,1,0:T(8,128)S(1)}, f32[26,8,512]{2,1,0:T(8,128)S(1)}, u32[]{:S(2)}, u32[]{:S(2)}) collective-permute-start(f32[26,8,512]{2,1,0:T(8,128)S(1)} %pack.1.first), channel_id=1, source_target_pairs={{0,16},{8,24},{16,0},{24,8},{1,17},{9,25},{17,1},{25,9},{2,18},{10... | collective-permute-start | bytes 1277960 | tf_op jit(solution)/shard_map/ppermute | solution.py:653
  22.7 11.3 %collective-permute-start.5 = (f32[7,8,512]{2,1,0:T(8,128)S(1)}, f32[7,8,512]{2,1,0:T(8,128)S(1)}, u32[]{:S(2)}, u32[]{:S(2)}) collective-permute-start(f32[7,8,512]{2,1,0:T(8,128)S(1)} %get-tuple-element.14.refs_1_), channel_id=1, source_target_pairs={{8,1},{1,8},{9,2},{2,9},{10,3},{3,10},{11,4},{4,11},{12,5},{5,12},... | collective-permute-start | bytes 344072 | tf_op jit(solution)/shard_map/ppermute | solution.py:667
  27.0 7.0 %collective-permute-start.6 = (f32[2,8,512]{2,1,0:T(8,128)S(1)}, f32[2,8,512]{2,1,0:T(8,128)S(1)}, u32[]{:S(2)}, u32[]{:S(2)}) collective-permute-start(f32[2,8,512]{2,1,0:T(8,128)S(1)} %get-tuple-element.17), channel_id=1, source_target_pairs={{8,17},{17,8},{9,18},{18,9},{10,19},{19,10},{11,20},{20,11},{12,21... | collective-permute-start | bytes 98312 | tf_op jit(solution)/shard_map/ppermute | solution.py:667
  35.3 5.0 %collective-permute-start.8 = (f32[64,512]{1,0:T(8,128)S(1)}, f32[64,512]{1,0:T(8,128)S(1)}, u32[]{:S(2)}, u32[]{:S(2)}) collective-permute-start(f32[64,512]{1,0:T(8,128)S(1)} %sweeps.1.own_ref), channel_id=1, source_target_pairs={{0,16},{8,24},{16,0},{24,8},{1,17},{9,25},{17,1},{25,9},{2,18},{10... | collective-permute-start | bytes 393224 | tf_op jit(solution)/shard_map/ppermute | solution.py:653
  36.8 3.5 %collective-permute-start.7 = (f32[64,512]{1,0:T(8,128)S(1)}, f32[64,512]{1,0:T(8,128)S(1)}, u32[]{:S(2)}, u32[]{:S(2)}) collective-permute-start(f32[64,512]{1,0:T(8,128)S(1)} %sweeps.1.own_ref), channel_id=1, source_target_pairs={{0,8},{8,0},{16,24},{24,16},{1,9},{9,1},{17,25},{25,17},{2,10},{10... | collective-permute-start | bytes 393224 | tf_op jit(solution)/shard_map/ppermute | solution.py:649
  40.3 1.3 %collective-permute-start.9 = (f32[64,512]{1,0:T(8,128)S(1)}, f32[64,512]{1,0:T(8,128)S(1)}, u32[]{:S(2)}, u32[]{:S(2)}) collective-permute-start(f32[64,512]{1,0:T(8,128)S(1)} %gate.7.chip_far), channel_id=1, source_target_pairs={{0,8},{8,0},{16,24},{24,16},{1,9},{9,1},{17,25},{25,17},{2,10},{10... | collective-permute-start | bytes 393224 | tf_op jit(solution)/shard_map/ppermute | solution.py:649

commit v4 on v3

--- a/solution.py
+++ b/solution.py
@@ -63,8 +63,8 @@
 def face_kernel(
     sat_hbm, alpha_hbm, psi_hbm, tex_hbm, act_hbm, out_ref, kinds, acts, given, tab, sems
 ):
-    _, core = place()
-    layer = core * (psi_hbm.shape[0] - 1)
+    chip, _ = place()
+    layer = (1 - chip) * (psi_hbm.shape[0] - 1)
     cols = psi_hbm.shape[2]
     classes = sat_hbm.shape[1]
     copies = [
@@ -126,7 +126,7 @@
 
 def soil_kernel(
     sat_ref, alpha_ref, theta_ref, psi_ref, tex_ref, act_ref,
-    moist_ref, keep_ref, send_ref, core_ref, tab, part,
+    moist_ref, keep_ref, send_ref, core_ref, rest_ref, tab, part,
 ):
     step = pl.program_id(0)
     _, core = place()
@@ -142,6 +142,7 @@
     nbits = max(1, (classes - 1).bit_length())
     face = 0.5 * soil_step / layer_thick
     core_layer = (1 - core) * (layers - 1)
+    rest_layer = core * (layers - 1)
 
     def columns(q, carry):
         lanes = pl.ds(pl.multiple_of(q * LANE, LANE), LANE)
@@ -174,9 +175,11 @@
             part[r // SUB, 2, :, lanes] = charge
             core_ref[0, rws, lanes] = psi_ref[core_layer, rws, lanes]
             core_ref[1, rws, lanes] = jnp.where(core == 0, cond, first)
+            rest_ref[0, rws, lanes] = psi_ref[rest_layer, rws, lanes]
+            rest_ref[1, rws, lanes] = jnp.where(core == 0, first, cond)
         return carry
 
-    lax.fori_loop(0, cols // LANE, columns, 0, unroll=4)
+    lax.fori_loop(0, cols // LANE, columns, 0, unroll=8)
 
     blocks = rows // SUB
     half = keep_ref.shape[0] - 1
@@ -219,8 +222,8 @@
         soil_kernel,
         grid=(nrows // rows,),
         in_specs=[whole, whole, whole, block, block, block],
-        out_specs=[block, msg_spec, msg_spec, pair],
-        out_shape=[jax.ShapeDtypeStruct((layers, nrows, cols), jnp.float32), msg, msg, layer2],
+        out_specs=[block, msg_spec, msg_spec, pair, pair],
+        out_shape=[jax.ShapeDtypeStruct((layers, nrows, cols), jnp.float32), msg, msg, layer2, layer2],
         scratch_shapes=[
             pltpu.VMEM((3, SUB, LANE), jnp.float32),
             pltpu.VMEM((rows // SUB, 3, SUB, cols), jnp.float32),
@@ -362,8 +365,8 @@
     )(keep, recv, own, other)
 
 
-def rim_kernel(keep_ref, recv_ref, own_ref, other_ref, first, side_ref, cross_ref):
-    del first
+def rim_kernel(keep_ref, recv_ref, own_ref, other_ref, first, second, side_ref, cross_ref):
+    del first, second
     chip, core = place()
     blocks, _, _, cols = keep_ref.shape
     half = cols // 2
@@ -389,17 +392,17 @@
     put_rows(cross_ref, 0, [*rows, jnp.concatenate([halo, spare], 1)])
 
 
-def rim(keep, recv, own, other, first):
+def rim(keep, recv, own, other, *first):
     half = keep.shape[3] // 2
     return pl.pallas_call(
         rim_kernel,
-        in_specs=[VMEM] * 4 + [ANY],
+        in_specs=[VMEM] * 4 + [ANY] * 2,
         out_specs=[VMEM] * 2,
         out_shape=[jax.ShapeDtypeStruct((n, SUB, half), jnp.float32) for n in (7, 2)],
         compiler_params=params(8),
         cost_estimate=cost(keep.size // 8, keep.size),
         name="rim",
-    )(keep, recv, own, other, first)
+    )(keep, recv, own, other, *first)
 
 
 def sweep_kernel(keep_ref, recv_ref, own_ref, other_ref, far_ref, side_ref, cross_ref, out_ref, work):
@@ -488,7 +491,32 @@
     )(keep, recv, own, other, far, side, cross)
 
 
-def faces_kernel(moist_in, core_ref, chip_ref, core_far, chip_far, rain_ref, moist_out, tail_ref, ends, sems):
+def pass_on_kernel(core_ref, ring_ref, first, out_ref):
+    del first
+    chip, core = place()
+
+    @pl.when(chip == core)
+    def _():
+        out_ref[...] = ring_ref[...]
+
+    @pl.when(chip != core)
+    def _():
+        out_ref[...] = core_ref[...]
+
+
+def pass_on(core_pair, ring, first):
+    return pl.pallas_call(
+        pass_on_kernel,
+        in_specs=[VMEM] * 2 + [ANY],
+        out_specs=VMEM,
+        out_shape=jax.ShapeDtypeStruct(ring.shape, ring.dtype),
+        compiler_params=params(8),
+        cost_estimate=cost(ring.size, 8 * ring.size),
+        name="pass_on",
+    )(core_pair, ring, first)
+
+
+def faces_kernel(moist_in, core_ref, rest_ref, ring_ref, got_ref, rain_ref, moist_out, tail_ref, ends, sems):
     del moist_in
     chip, core = place()
     layers = moist_out.shape[0]
@@ -508,32 +536,31 @@
     def flux(upper, lower):
         return (upper[1] + lower[1]) * ((upper[0] - lower[0]) * (face / layer_thick) + face)
 
-    @pl.when(core == 0)
-    def _():
-        ends[1] = ends[1] - flux(core_ref, core_far)
-
-    @pl.when(core == 1)
-    def _():
-        ends[0] = ends[0] + flux(core_far, core_ref)
-
     @pl.when((core == 0) & (chip == 0))
     def _():
         ends[0] = ends[0] + gain * rain_ref[...]
+        ends[1] = ends[1] - flux(core_ref, got_ref)
+
+    @pl.when((core == 1) & (chip == 0))
+    def _():
+        ends[0] = ends[0] + flux(ring_ref, core_ref)
+        ends[1] = ends[1] - flux(rest_ref, got_ref)
 
     @pl.when((core == 0) & (chip == 1))
     def _():
-        ends[0] = ends[0] + flux(chip_far, chip_ref)
-
-    @pl.when((core == 1) & (chip == 0))
-    def _():
-        ends[1] = ends[1] - flux(chip_ref, chip_far)
+        ends[0] = ends[0] + flux(got_ref, rest_ref)
+        ends[1] = ends[1] - flux(core_ref, ring_ref)
+
+    @pl.when(last)
+    def _():
+        ends[0] = ends[0] + flux(got_ref, core_ref)
 
     stores[0].start()
 
     @pl.when(last)
     def _():
-        slope = chip_ref[1] * (gain / (0.5 * layer_thick))
-        tail_ref[0] = ends[1] - (chip_ref[0] * slope + gain * chip_ref[1])
+        slope = rest_ref[1] * (gain / (0.5 * layer_thick))
+        tail_ref[0] = ends[1] - (rest_ref[0] * slope + gain * rest_ref[1])
         tail_ref[1] = slope
 
     @pl.when(jnp.logical_not(last))
@@ -544,7 +571,7 @@
     stores[0].wait()
 
 
-def faces(moist, core_pair, chip_pair, core_far, chip_far, rain):
+def faces(moist, core_pair, rest_pair, ring, got, rain):
     return pl.pallas_call(
         faces_kernel,
         in_specs=[ANY] + [VMEM] * 5,
@@ -558,7 +585,7 @@
         compiler_params=params(12),
         cost_estimate=cost(20 * rain.size, 32 * rain.size),
         name="faces",
-    )(moist, core_pair, chip_pair, core_far, chip_far, rain)
+    )(moist, core_pair, rest_pair, ring, got, rain)
 
 
 def bottom_kernel(moist_in, tail_ref, own_ref, core_far, chip_far, both_far, moist_out, head_ref, last, sems):
@@ -653,8 +680,8 @@
     return lax.ppermute(value, "depth", [(i, i ^ 2) for i in range(lax.axis_size("depth"))])
 
 
-def middle_swap(value):
-    return lax.ppermute(value, "depth", [(1, 2), (2, 1)])
+def ring_shift(value):
+    return lax.ppermute(value, "depth", [(1, 3), (3, 2), (2, 0), (0, 1)])
 
 
 def strip_swap(value, chips=0):
@@ -669,19 +696,18 @@
 
 def shards(pressure, texture, active, rain, k_sat, alpha, theta_sat, head_old, cell_code, section):
     tables = (k_sat[None], alpha[None], theta_sat[None])
-    chip_pair = face(tables, pressure, texture, active)
-    chip_far = middle_swap(chip_pair)
-    own = inputs(head_old, cell_code, section, chip_pair)
+    face_pair = face(tables, pressure, texture, active)
+    ring = ring_shift(face_pair)
+    own = inputs(head_old, cell_code, section, face_pair)
     other = core_swap(own)
-    moist, keep, send, core_pair = soil(tables, pressure, texture, active)
+    moist, keep, send, core_pair, rest_pair = soil(tables, pressure, texture, active)
     recv = core_swap(gate(send, other))
-    keep = gate(keep, chip_far)
     message = pack(keep, recv, own, other)
     far = chip_swap(message)
-    side, cross = rim(keep, recv, own, other, message)
+    side, cross = rim(keep, recv, own, other, message, ring)
     heads = sweeps(keep, recv, own, other, far, strip_swap(side), strip_swap(cross, 2))
-    core_far = core_swap(gate(core_pair, side))
-    moist, tail = faces(moist, core_pair, chip_pair, core_far, chip_far, rain)
+    got = core_swap(pass_on(core_pair, ring, side))
+    moist, tail = faces(moist, core_pair, rest_pair, ring, got, rain)
     heads_chip = gate(chip_swap(heads), stored=(moist,))
     heads_core = core_swap(heads)
     heads_both = core_swap(heads_chip)

time: 42.5 us -> 40.4 us (0.951)
  starting transfers between devices: 13 us -> 10.7 us
    ppermute x5, starting transfers between devices: 4.86 us -> 3.71 us  [core_swap(): lax.ppermute(value, 'depth', [(i, i ^ 1) for i in range(lax.axis_size('de...]
    ppermute x2, waiting for transfers between devices: 1.22 us -> 2.22 us  [chip_swap(): lax.ppermute(value, 'depth', [(i, i ^ 2) for i in range(lax.axis_size('de...]
    ppermute x1, starting transfers between devices: 0.72 us -> 0.06 us  [ring_shift(): return lax.ppermute(value, 'depth', [(1, 3), (3, 2), (2, 0), (0, 1)])]
    ppermute x2, starting transfers between devices: 2.61 us -> 1.98 us  [chip_swap(): lax.ppermute(value, 'depth', [(i, i ^ 2) for i in range(lax.axis_size('de...]
    ppermute x2, waiting for transfers between devices: 6.55 us -> 5.99 us  [strip_swap(): return lax.ppermute(value, ('depth', 'strips'), pairs)]
  transfers between devices with their start and end apart: 10 -> 10, of which waited for: 5 -> 5; matrix products, arithmetic and copies ran while one was open for 0% -> 0% of each run, Pallas kernels for 33% -> 35%
where the time goes in v4:
time: 40.4 us; the launch traced here: 40.2 us
  Pallas kernels  17.1 us (42%)
  waiting for transfers between devices  11.6 us (29%)
  starting transfers between devices  10.7 us (26%)
  between operations  0.74 us (2%)
    pallas_call x1, Pallas kernels, soil(): pl.pallas_call(soil_kernel, grid=(nrows // rows,), in_specs=[whole, whole...  10.2 us
    ppermute x2, waiting for transfers between devices, strip_swap(): return lax.ppermute(value, ('depth', 'strips'), pairs)  5.99 us
    ppermute x2, starting transfers between devices, strip_swap(): return lax.ppermute(value, ('depth', 'strips'), pairs)  4.99 us
    ppermute x5, starting transfers between devices, core_swap(): lax.ppermute(value, 'depth', [(i, i ^ 1) for i in range(lax.axis_size('de...  3.71 us
    ppermute x5, waiting for transfers between devices, core_swap(): lax.ppermute(value, 'depth', [(i, i ^ 1) for i in range(lax.axis_size('de...  3.4 us
    pallas_call x1, Pallas kernels, faces(): pl.pallas_call(faces_kernel, in_specs=[ANY] + [VMEM] * 5, out_specs=[ANY,...  2.39 us
    pallas_call x1, Pallas kernels, face(): pl.pallas_call(face_kernel, in_specs=[HBM] * 5, out_specs=VMEM, out_shape...  2.31 us
    ppermute x2, waiting for transfers between devices, chip_swap(): lax.ppermute(value, 'depth', [(i, i ^ 2) for i in range(lax.axis_size('de...  2.22 us
  transfers between devices with their start and end apart: 10, of which 5 were waited for; matrix products, arithmetic and copies ran while one was open for 0% of the time, Pallas kernels for 35%

profile of v4, /device:TPU:0, one launch (start us, length us, event | category | flops | bytes accessed | tf_op | source)
XLA Modules:
  0.0 40.2 jit_solution(7882284325151694916)
XLA Ops:
  0.6 0.0 copy-start.1
  0.6 0.0 copy-start.2
  0.7 0.0 copy-start.3
  0.7 2.3 %face.1.first = f32[2,128,1024]{2,1,0:T(8,128)S(1)} custom-call(f32[1,12]{1,0:T(1,128)} %bitcast.3, f32[1,12]{1,0:T(1,128)} %bitcast.5, f32[8,128,1024]{2,1,0:T(8,128)} %psi_hbm.1, s32[8,128,1024]{2,1,0:T(8,128)} %tex_hbm.1, s32[8,128,1024]{2,1,0:T(8,128)} %act_hbm.1), custom_call_target="tpu_custom_call" | custom-call | flops 2621440 | bytes 2621440 | tf_op jit(solution)/shard_map/face/pallas_call | solution.py:109
  3.0 0.0 copy-done.1
  3.0 0.0 copy-done.2
  3.0 0.0 copy-done.3
  3.1 0.5 %collective-permute-start.1 = (f32[3,128,256]{2,1,0:T(8,128)S(1)}, f32[3,128,256]{2,1,0:T(8,128)S(1)}, u32[]{:S(2)}, u32[]{:S(2)}) collective-permute-start(f32[3,128,256]{2,1,0:T(8,128)S(1)} %inputs.1.own_ref), channel_id=1, source_target_pairs={{0,8},{8,0},{16,24},{24,16},{1,9},{9,1},{17,25},{25,17},{2,10},{10... | collective-permute-start | bytes 1179656 | tf_op jit(solution)/shard_map/ppermute | solution.py:676
  3.6 0.1 collective-permute-start
  3.6 10.2 %soil.1 = (f32[8,128,1024]{2,1,0:T(8,128)}, f32[9,3,8,1024]{3,2,1,0:T(8,128)S(1)}, f32[9,3,8,1024]{3,2,1,0:T(8,128)S(1)}, f32[2,128,1024]{2,1,0:T(8,128)S(1)}, f32[2,128,1024]{2,1,0:T(8,128)S(1)}) custom-call(f32[1,12]{1,0:T(1,128)} %bitcast.4, f32[1,12]{1,0:T(1,128)} %bitcast.6, f32[1,12]{1,0:T(1,128)} %bitcast.7, f32[8,128,1024]{2,1,0:T(8,128)} %psi_hbm.1, ...), custom_call_target="tpu_custom_call" | custom-call | flops 62914560 | bytes 20971520 | tf_op jit(solution)/shard_map/soil/pallas_call | solution.py:221
  13.9 0.0 collective-permute-done.1.refs_1_.other_ref
  13.9 2.7 %collective-permute-start.2 = (f32[9,3,8,1024]{3,2,1,0:T(8,128)S(1)}, f32[9,3,8,1024]{3,2,1,0:T(8,128)S(1)}, u32[]{:S(2)}, u32[]{:S(2)}) collective-permute-start(f32[9,3,8,1024]{3,2,1,0:T(8,128)S(1)} %gate.2), channel_id=1, source_target_pairs={{0,8},{8,0},{16,24},{24,16},{1,9},{9,1},{17,25},{25,17},{2,10},{10... | collective-permute-start | bytes 2654216 | tf_op jit(solution)/shard_map/ppermute | solution.py:676
  16.6 2.1 %collective-permute-done.2.recv_ref = f32[9,3,8,1024]{3,2,1,0:T(8,128)S(1)} collective-permute-done((f32[9,3,8,1024]{3,2,1,0:T(8,128)S(1)}, f32[9,3,8,1024]{3,2,1,0:T(8,128)S(1)}, u32[]{:S(2)}, u32[]{:S(2)}) %collective-permute-start.2) | collective-permute-done | bytes 884768 | tf_op jit(solution)/shard_map/ppermute | solution.py:676
  18.7 0.2 pack.1.first
  18.9 0.0 collective-permute-done.second.ring_ref
  18.9 0.1 rim.1
  19.0 0.0 copy-start
  19.0 0.1 pass_on.1
  19.1 0.4 %collective-permute-start.3 = (f32[2,128,1024]{2,1,0:T(8,128)S(1)}, f32[2,128,1024]{2,1,0:T(8,128)S(1)}, u32[]{:S(2)}, u32[]{:S(2)}) collective-permute-start(f32[2,128,1024]{2,1,0:T(8,128)S(1)} %pass_on.1), channel_id=1, source_target_pairs={{0,8},{8,0},{16,24},{24,16},{1,9},{9,1},{17,25},{25,17},{2,10},{10... | collective-permute-start | bytes 3145736 | tf_op jit(solution)/shard_map/ppermute | solution.py:676
  19.5 1.0 %collective-permute-start.4 = (f32[26,8,512]{2,1,0:T(8,128)S(1)}, f32[26,8,512]{2,1,0:T(8,128)S(1)}, u32[]{:S(2)}, u32[]{:S(2)}) collective-permute-start(f32[26,8,512]{2,1,0:T(8,128)S(1)} %pack.1.first), channel_id=1, source_target_pairs={{0,16},{8,24},{16,0},{24,8},{1,17},{9,25},{17,1},{25,9},{2,18},{10... | collective-permute-start | bytes 1277960 | tf_op jit(solution)/shard_map/ppermute | solution.py:680
  20.5 3.9 %collective-permute-start.5 = (f32[7,8,512]{2,1,0:T(8,128)S(1)}, f32[7,8,512]{2,1,0:T(8,128)S(1)}, u32[]{:S(2)}, u32[]{:S(2)}) collective-permute-start(f32[7,8,512]{2,1,0:T(8,128)S(1)} %get-tuple-element.16.first), channel_id=1, source_target_pairs={{8,1},{1,8},{9,2},{2,9},{10,3},{3,10},{11,4},{4,11},{12,5},{5,12},... | collective-permute-start | bytes 344072 | tf_op jit(solution)/shard_map/ppermute | solution.py:694
  24.4 1.1 %collective-permute-start.6 = (f32[2,8,512]{2,1,0:T(8,128)S(1)}, f32[2,8,512]{2,1,0:T(8,128)S(1)}, u32[]{:S(2)}, u32[]{:S(2)}) collective-permute-start(f32[2,8,512]{2,1,0:T(8,128)S(1)} %get-tuple-element.19), channel_id=1, source_target_pairs={{8,17},{17,8},{9,18},{18,9},{10,19},{19,10},{11,20},{20,11},{12,21... | collective-permute-start | bytes 98312 | tf_op jit(solution)/shard_map/ppermute | solution.py:694
  25.5 6.0 %collective-permute-done.6.cross_ref = f32[2,8,512]{2,1,0:T(8,128)S(1)} collective-permute-done((f32[2,8,512]{2,1,0:T(8,128)S(1)}, f32[2,8,512]{2,1,0:T(8,128)S(1)}, u32[]{:S(2)}, u32[]{:S(2)}) %collective-permute-start.6) | collective-permute-done | bytes 32800 | tf_op jit(solution)/shard_map/ppermute | solution.py:694
  31.5 0.0 collective-permute-done.5.side_ref
  31.5 0.6 %collective-permute-done.4.far_ref = f32[26,8,512]{2,1,0:T(8,128)S(1)} collective-permute-done((f32[26,8,512]{2,1,0:T(8,128)S(1)}, f32[26,8,512]{2,1,0:T(8,128)S(1)}, u32[]{:S(2)}, u32[]{:S(2)}) %collective-permute-start.4) | collective-permute-done | bytes 426016 | tf_op jit(solution)/shard_map/ppermute | solution.py:680
  32.1 1.1 %sweeps.1.own_ref = f32[64,512]{1,0:T(8,128)S(1)} custom-call(f32[9,3,8,1024]{3,2,1,0:T(8,128)S(1)} %get-tuple-element.14.keep_ref, f32[9,3,8,1024]{3,2,1,0:T(8,128)S(1)} %collective-permute-done.2.recv_ref, f32[3,128,256]{2,1,0:T(8,128)S(1)} %inputs.1.own_ref, f32[3,128,256]{2,1,0:T(8,128)S(1)} %collective-permute-done.1.refs_1_.other_ref, ...), custom_call_target="tpu_custom_call" | custom-call | flops 4423680 | bytes 2654208 | tf_op jit(solution)/shard_map/sweeps/pallas_call | solution.py:482
  33.2 1.0 %collective-permute-start.8 = (f32[64,512]{1,0:T(8,128)S(1)}, f32[64,512]{1,0:T(8,128)S(1)}, u32[]{:S(2)}, u32[]{:S(2)}) collective-permute-start(f32[64,512]{1,0:T(8,128)S(1)} %sweeps.1.own_ref), channel_id=1, source_target_pairs={{0,16},{8,24},{16,0},{24,8},{1,17},{9,25},{17,1},{25,9},{2,18},{10... | collective-permute-start | bytes 393224 | tf_op jit(solution)/shard_map/ppermute | solution.py:680
  34.2 0.0 collective-permute-start.7
  34.2 0.0 collective-permute-done.3.got_ref
  34.2 0.0 copy-done
  34.2 2.4 %faces.1 = (f32[8,128,1024]{2,1,0:T(8,128)}, f32[2,128,1024]{2,1,0:T(8,128)S(1)}) custom-call(f32[8,128,1024]{2,1,0:T(8,128)} %get-tuple-element.11.moist_in, f32[2,128,1024]{2,1,0:T(8,128)S(1)} %get-tuple-element.12.core_ref, f32[2,128,1024]{2,1,0:T(8,128)S(1)} %get-tuple-element.13.rest_ref, ...), custom_call_target="tpu_custom_call", output_to_operand_aliasing={{0}: (0, {})} | custom-call | flops 2621440 | bytes 4194304 | tf_op jit(solution)/shard_map/faces/pallas_call | solution.py:575
  36.6 1.6 %collective-permute-done.8.refs_0_ = f32[64,512]{1,0:T(8,128)S(1)} collective-permute-done((f32[64,512]{1,0:T(8,128)S(1)}, f32[64,512]{1,0:T(8,128)S(1)}, u32[]{:S(2)}, u32[]{:S(2)}) %collective-permute-start.8) | collective-permute-done | bytes 131104 | tf_op jit(solution)/shard_map/ppermute | solution.py:680
  38.2 0.0 collective-permute-start.9
  38.2 0.0 collective-permute-done.7.core_far
  38.2 1.3 %collective-permute-done.9.both_far = f32[64,512]{1,0:T(8,128)S(1)} collective-permute-done((f32[64,512]{1,0:T(8,128)S(1)}, f32[64,512]{1,0:T(8,128)S(1)}, u32[]{:S(2)}, u32[]{:S(2)}) %collective-permute-start.9) | collective-permute-done | bytes 131104 | tf_op jit(solution)/shard_map/ppermute | solution.py:676
  39.6 0.7 %bottom.1 = (f32[8,128,1024]{2,1,0:T(8,128)}, f32[128,256]{1,0:T(8,128)}) custom-call(f32[8,128,1024]{2,1,0:T(8,128)} %get-tuple-element.17.refs_1_.moist_in, f32[2,128,1024]{2,1,0:T(8,128)S(1)} %get-tuple-element.18.tail_ref, f32[64,512]{1,0:T(8,128)S(1)} %sweeps.1.own_ref, ...), custom_call_target="tpu_custom_call", output_to_operand_aliasing={{0}: (0, {})} | custom-call | flops 327680 | bytes 1310720 | tf_op jit(solution)/shard_map/bottom/pallas_call | solution.py:621
  (3 shorter events, 0.0 us)
Async XLA Ops:
  0.6 2.3 %copy-start.1 = (f32[128,256]{1,0:T(8,128)S(1)}, f32[128,256]{1,0:T(8,128)}, u32[]{:S(2)}) copy-start(f32[128,256]{1,0:T(8,128)} %old_ref.1) | copy-start | bytes 393220
  0.6 2.3 %copy-start.2 = (s32[128,256]{1,0:T(8,128)S(1)}, s32[128,256]{1,0:T(8,128)}, u32[]{:S(2)}) copy-start(s32[128,256]{1,0:T(8,128)} %code_ref.1) | copy-start | bytes 393220
  0.7 2.3 %copy-start.3 = (f32[128,256]{1,0:T(8,128)S(1)}, f32[128,256]{1,0:T(8,128)}, u32[]{:S(2)}) copy-start(f32[128,256]{1,0:T(8,128)} %section_ref.1) | copy-start | bytes 393220
  3.1 10.8 %collective-permute-start.1 = (f32[3,128,256]{2,1,0:T(8,128)S(1)}, f32[3,128,256]{2,1,0:T(8,128)S(1)}, u32[]{:S(2)}, u32[]{:S(2)}) collective-permute-start(f32[3,128,256]{2,1,0:T(8,128)S(1)} %inputs.1.own_ref), channel_id=1, source_target_pairs={{0,8},{8,0},{16,24},{24,16},{1,9},{9,1},{17,25},{25,17},{2,10},{10... | collective-permute-start | bytes 1179656 | tf_op jit(solution)/shard_map/ppermute | solution.py:676
  3.6 15.3 %collective-permute-start = (f32[2,128,1024]{2,1,0:T(8,128)S(1)}, f32[2,128,1024]{2,1,0:T(8,128)S(1)}, u32[]{:S(2)}, u32[]{:S(2)}) collective-permute-start(f32[2,128,1024]{2,1,0:T(8,128)S(1)} %face.1.first), channel_id=1, source_target_pairs={{8,24},{24,16},{16,0},{0,8},{9,25},{25,17},{17,1},{1,9},{10,26},{2... | collective-permute-start | bytes 3145736 | tf_op jit(solution)/shard_map/ppermute | solution.py:684
  13.9 4.8 %collective-permute-start.2 = (f32[9,3,8,1024]{3,2,1,0:T(8,128)S(1)}, f32[9,3,8,1024]{3,2,1,0:T(8,128)S(1)}, u32[]{:S(2)}, u32[]{:S(2)}) collective-permute-start(f32[9,3,8,1024]{3,2,1,0:T(8,128)S(1)} %gate.2), channel_id=1, source_target_pairs={{0,8},{8,0},{16,24},{24,16},{1,9},{9,1},{17,25},{25,17},{2,10},{10... | collective-permute-start | bytes 2654216 | tf_op jit(solution)/shard_map/ppermute | solution.py:676
  19.0 15.2 %copy-start = (f32[128,1024]{1,0:T(8,128)S(1)}, f32[128,1024]{1,0:T(8,128)}, u32[]{:S(2)}) copy-start(f32[128,1024]{1,0:T(8,128)} %rain_ref.1) | copy-start | bytes 1572868
  19.1 15.1 %collective-permute-start.3 = (f32[2,128,1024]{2,1,0:T(8,128)S(1)}, f32[2,128,1024]{2,1,0:T(8,128)S(1)}, u32[]{:S(2)}, u32[]{:S(2)}) collective-permute-start(f32[2,128,1024]{2,1,0:T(8,128)S(1)} %pass_on.1), channel_id=1, source_target_pairs={{0,8},{8,0},{16,24},{24,16},{1,9},{9,1},{17,25},{25,17},{2,10},{10... | collective-permute-start | bytes 3145736 | tf_op jit(solution)/shard_map/ppermute | solution.py:676
  19.5 12.6 %collective-permute-start.4 = (f32[26,8,512]{2,1,0:T(8,128)S(1)}, f32[26,8,512]{2,1,0:T(8,128)S(1)}, u32[]{:S(2)}, u32[]{:S(2)}) collective-permute-start(f32[26,8,512]{2,1,0:T(8,128)S(1)} %pack.1.first), channel_id=1, source_target_pairs={{0,16},{8,24},{16,0},{24,8},{1,17},{9,25},{17,1},{25,9},{2,18},{10... | collective-permute-start | bytes 1277960 | tf_op jit(solution)/shard_map/ppermute | solution.py:680
  20.5 11.0 %collective-permute-start.5 = (f32[7,8,512]{2,1,0:T(8,128)S(1)}, f32[7,8,512]{2,1,0:T(8,128)S(1)}, u32[]{:S(2)}, u32[]{:S(2)}) collective-permute-start(f32[7,8,512]{2,1,0:T(8,128)S(1)} %get-tuple-element.16.first), channel_id=1, source_target_pairs={{8,1},{1,8},{9,2},{2,9},{10,3},{3,10},{11,4},{4,11},{12,5},{5,12},... | collective-permute-start | bytes 344072 | tf_op jit(solution)/shard_map/ppermute | solution.py:694
  24.4 7.0 %collective-permute-start.6 = (f32[2,8,512]{2,1,0:T(8,128)S(1)}, f32[2,8,512]{2,1,0:T(8,128)S(1)}, u32[]{:S(2)}, u32[]{:S(2)}) collective-permute-start(f32[2,8,512]{2,1,0:T(8,128)S(1)} %get-tuple-element.19), channel_id=1, source_target_pairs={{8,17},{17,8},{9,18},{18,9},{10,19},{19,10},{11,20},{20,11},{12,21... | collective-permute-start | bytes 98312 | tf_op jit(solution)/shard_map/ppermute | solution.py:694
  33.2 5.0 %collective-permute-start.8 = (f32[64,512]{1,0:T(8,128)S(1)}, f32[64,512]{1,0:T(8,128)S(1)}, u32[]{:S(2)}, u32[]{:S(2)}) collective-permute-start(f32[64,512]{1,0:T(8,128)S(1)} %sweeps.1.own_ref), channel_id=1, source_target_pairs={{0,16},{8,24},{16,0},{24,8},{1,17},{9,25},{17,1},{25,9},{2,18},{10... | collective-permute-start | bytes 393224 | tf_op jit(solution)/shard_map/ppermute | solution.py:680
  34.2 4.0 %collective-permute-start.7 = (f32[64,512]{1,0:T(8,128)S(1)}, f32[64,512]{1,0:T(8,128)S(1)}, u32[]{:S(2)}, u32[]{:S(2)}) collective-permute-start(f32[64,512]{1,0:T(8,128)S(1)} %sweeps.1.own_ref), channel_id=1, source_target_pairs={{0,8},{8,0},{16,24},{24,16},{1,9},{9,1},{17,25},{25,17},{2,10},{10... | collective-permute-start | bytes 393224 | tf_op jit(solution)/shard_map/ppermute | solution.py:676
  38.2 1.3 %collective-permute-start.9 = (f32[64,512]{1,0:T(8,128)S(1)}, f32[64,512]{1,0:T(8,128)S(1)}, u32[]{:S(2)}, u32[]{:S(2)}) collective-permute-start(f32[64,512]{1,0:T(8,128)S(1)} %gate.3.chip_far), channel_id=1, source_target_pairs={{0,8},{8,0},{16,24},{24,16},{1,9},{9,1},{17,25},{25,17},{2,10},{10... | collective-permute-start | bytes 393224 | tf_op jit(solution)/shard_map/ppermute | solution.py:676

commit v5 on v4

--- a/solution.py
+++ b/solution.py
@@ -10,6 +10,7 @@
 
 SWEEPS = 3
 SUB = 8
+PARTS = 2
 LANE = 128
 WIDTH = 4
 
@@ -125,8 +126,8 @@
 
 
 def soil_kernel(
-    sat_ref, alpha_ref, theta_ref, psi_ref, tex_ref, act_ref,
-    moist_ref, keep_ref, send_ref, core_ref, rest_ref, tab, part,
+    sat_ref, alpha_ref, theta_ref, psi_ref, tex_ref, act_ref, old_ref, code_ref, section_ref,
+    moist_ref, keep_ref, send_ref, mine_ref, give_ref, core_ref, rest_ref, tab, part, tile,
 ):
     step = pl.program_id(0)
     _, core = place()
@@ -182,31 +183,39 @@
     lax.fori_loop(0, cols // LANE, columns, 0, unroll=8)
 
     blocks = rows // SUB
+    for r in range(blocks):
+        at = pl.ds(pl.multiple_of(step * rows + r * SUB, SUB), SUB)
+        code = code_ref[at]
+        river = jnp.where(code == 1, river_cond, jnp.where(code == 2, fixed_cond, 0.0))
+        for a, value in enumerate((old_ref[at], river, river * section_ref[at])):
+            tile[r, a] = value
+
     half = keep_ref.shape[0] - 1
     for r in range(blocks):
         block = step * blocks + r
 
-        def put(ref, at):
+        def put(ref, tile_ref, at):
             ref[at] = part[r]
+            tile_ref[at] = tile[r]
 
         @pl.when((block <= half) & (core == 0))
         def _():
-            put(keep_ref, block)
+            put(keep_ref, mine_ref, block)
 
         @pl.when((block <= half) & (core == 1))
         def _():
-            put(send_ref, block)
+            put(send_ref, give_ref, block)
 
         @pl.when((block >= half - 1) & (core == 0))
         def _():
-            put(send_ref, block - (half - 1))
+            put(send_ref, give_ref, block - (half - 1))
 
         @pl.when((block >= half - 1) & (core == 1))
         def _():
-            put(keep_ref, block - (half - 1))
-
-
-def soil(tables, pressure, texture, active):
+            put(keep_ref, mine_ref, block - (half - 1))
+
+
+def soil(tables, pressure, texture, active, head_old, cell_code, section):
     layers, nrows, cols = pressure.shape
     classes = tables[0].shape[1]
     rows = nrows // 4
@@ -215,23 +224,27 @@
     block = pl.BlockSpec((layers, rows, cols), lambda j: (0, j, 0))
     pair = pl.BlockSpec((2, rows, cols), lambda j: (0, j, 0))
     msg = jax.ShapeDtypeStruct((blocks, 3, SUB, cols), jnp.float32)
-    msg_spec = pl.BlockSpec((blocks, 3, SUB, cols), lambda j: (0, 0, 0, 0))
+    msg_spec = pl.BlockSpec(msg.shape, lambda j: (0, 0, 0, 0))
+    tile = pl.BlockSpec(head_old.shape, lambda j: (0, 0))
+    part = jax.ShapeDtypeStruct((blocks, 3, SUB, head_old.shape[1]), jnp.float32)
+    part_spec = pl.BlockSpec(part.shape, lambda j: (0, 0, 0, 0))
     layer2 = jax.ShapeDtypeStruct((2, nrows, cols), jnp.float32)
     size = layers * nrows * cols
     return pl.pallas_call(
         soil_kernel,
         grid=(nrows // rows,),
-        in_specs=[whole, whole, whole, block, block, block],
-        out_specs=[block, msg_spec, msg_spec, pair, pair],
-        out_shape=[jax.ShapeDtypeStruct((layers, nrows, cols), jnp.float32), msg, msg, layer2, layer2],
+        in_specs=[whole, whole, whole, block, block, block, tile, tile, tile],
+        out_specs=[block, msg_spec, msg_spec, part_spec, part_spec, pair, pair],
+        out_shape=[jax.ShapeDtypeStruct((layers, nrows, cols), jnp.float32), msg, msg, part, part, layer2, layer2],
         scratch_shapes=[
             pltpu.VMEM((3, SUB, LANE), jnp.float32),
             pltpu.VMEM((rows // SUB, 3, SUB, cols), jnp.float32),
+            pltpu.VMEM((rows // SUB, 3, SUB, head_old.shape[1]), jnp.float32),
         ],
         compiler_params=params(32),
         cost_estimate=cost(60 * size, 20 * size, size),
         name="soil",
-    )(*in_hbm(*tables, pressure, texture, active))
+    )(*in_hbm(*tables, pressure, texture, active, head_old, cell_code, section))
 
 
 def edge_lane(chip):
@@ -307,27 +320,22 @@
     return pl.ds(pl.multiple_of(half - LANE + chip * LANE, LANE), LANE)
 
 
-def first_row(core, blocks, b):
-    return pl.multiple_of((core * (blocks - 2) + b) * SUB, SUB)
-
-
-def tile_rows(own_ref, other_ref, core, which, array, first, lanes):
-    mine = own_ref[array, pl.ds(first, SUB), lanes]
-    theirs = other_ref[array, pl.ds(first, SUB), lanes]
-    return jnp.where(core == which, mine, theirs)
-
-
-def edge_inputs(own_ref, other_ref, chip, core, first):
-    tile = own_ref.shape[2]
+def tile_rows(mine_ref, other_ref, b, core, which, array, start, stop):
+    lanes = slice(start, stop)
+    return jnp.where(core == which, mine_ref[b, array, :, lanes], other_ref[b, array, :, lanes])
+
+
+def edge_inputs(mine_ref, other_ref, b, chip, core):
+    tile = mine_ref.shape[3]
     out = []
     for a in range(3):
-        left = tile_rows(own_ref, other_ref, core, 1, a, first, slice(tile - LANE, tile))
-        right = tile_rows(own_ref, other_ref, core, 0, a, first, slice(0, LANE))
+        left = tile_rows(mine_ref, other_ref, b, core, 1, a, tile - LANE, tile)
+        right = tile_rows(mine_ref, other_ref, b, core, 0, a, 0, LANE)
         out.append(jnp.where(chip == 0, left, right))
     return out
 
 
-def pack_kernel(keep_ref, recv_ref, own_ref, other_ref, out_ref):
+def pack_kernel(keep_ref, recv_ref, mine_ref, other_ref, out_ref):
     chip, core = place()
     blocks, _, _, cols = keep_ref.shape
     half = cols // 2
@@ -344,14 +352,14 @@
         else:
             rows = [nearest(v, core) for v in sums]
         pieces = [keep_ref[b, a, :, slab] + recv_ref[b, a, :, slab] for a in range(3)]
-        pieces += edge_inputs(own_ref, other_ref, chip, core, first_row(core, blocks, b))
+        pieces += edge_inputs(mine_ref, other_ref, b, chip, core)
         piece = packed(pieces, chip, j % SHARE)
         i = j // SHARE
         tiles[i] = piece if tiles[i] is None else tiles[i] + piece
     put_rows(out_ref, main, [*rows, fold(tiles)])
 
 
-def pack(keep, recv, own, other):
+def pack(keep, recv, mine, other):
     blocks, _, _, cols = keep.shape
     half = cols // 2
     return pl.pallas_call(
@@ -362,50 +370,49 @@
         compiler_params=params(8),
         cost_estimate=cost(keep.size, 12 * keep.size),
         name="pack",
-    )(keep, recv, own, other)
-
-
-def rim_kernel(keep_ref, recv_ref, own_ref, other_ref, first, second, side_ref, cross_ref):
-    del first, second
+    )(keep, recv, mine, other)
+
+
+def rim_kernel(keep_ref, recv_ref, mine_ref, other_ref, *refs):
+    side_ref, cross_ref = refs[-2:]
     chip, core = place()
     blocks, _, _, cols = keep_ref.shape
     half = cols // 2
     tile = half // 2
     b = core * (blocks - 1)
-    row = first_row(core, blocks, b)
     near, away = half_lanes(chip, half), half_lanes(1 - chip, half)
     side_ref[:3] = keep_ref[b, :, :, near] + recv_ref[b, :, :, near]
     rows = [nearest(keep_ref[b, a, :, away] + recv_ref[b, a, :, away], core) for a in range(3)]
     for which in range(2):
         for a in range(3):
             side_ref[3 + a, :, which * tile : (which + 1) * tile] = tile_rows(
-                own_ref, other_ref, core, which, a, row, slice(0, tile)
+                mine_ref, other_ref, b, core, which, a, 0, tile
             )
 
     def sums(slab):
         return [keep_ref[b, a, :, slab] + recv_ref[b, a, :, slab] for a in range(3)]
 
     side_ref[6, :, :LANE] = packed(sums(slab_lanes(1 - chip, half)), 1 - chip)
-    inputs = edge_inputs(own_ref, other_ref, chip, core, row)
+    inputs = edge_inputs(mine_ref, other_ref, b, chip, core)
     halo = nearest(packed(sums(slab_lanes(chip, half)) + inputs, chip), core)
     spare = jnp.zeros((SWEEPS, half - LANE), jnp.float32)
     put_rows(cross_ref, 0, [*rows, jnp.concatenate([halo, spare], 1)])
 
 
-def rim(keep, recv, own, other, *first):
+def rim(keep, recv, mine, other, *first):
     half = keep.shape[3] // 2
     return pl.pallas_call(
         rim_kernel,
-        in_specs=[VMEM] * 4 + [ANY] * 2,
+        in_specs=[VMEM] * 4 + [ANY] * len(first),
         out_specs=[VMEM] * 2,
         out_shape=[jax.ShapeDtypeStruct((n, SUB, half), jnp.float32) for n in (7, 2)],
         compiler_params=params(8),
         cost_estimate=cost(keep.size // 8, keep.size),
         name="rim",
-    )(keep, recv, own, other, *first)
-
-
-def sweep_kernel(keep_ref, recv_ref, own_ref, other_ref, far_ref, side_ref, cross_ref, out_ref, work):
+    )(keep, recv, mine, other, *first)
+
+
+def sweep_kernel(keep_ref, recv_ref, mine_ref, other_ref, far_ref, side_ref, cross_ref, out_ref, left_ref, right_ref, work):
     chip, core = place()
     strip = lax.axis_index("strips")
     blocks, _, _, cols = keep_ref.shape
@@ -437,10 +444,9 @@
         else:
             far = [spread(v, core) for v in beyond]
         sums = [keep_ref[b, a, :, near] + recv_ref[b, a, :, near] + far[a] for a in range(3)]
-        first_at = first_row(core, blocks, b)
         for which in range(2):
             lanes = slice(which * tile, (which + 1) * tile)
-            inputs = [tile_rows(own_ref, other_ref, core, which, a, first_at, slice(0, tile)) for a in range(3)]
+            inputs = [tile_rows(mine_ref, other_ref, b, core, which, a, 0, tile) for a in range(3)]
             cells(b, lanes, [s[:, lanes] for s in sums], inputs)
         far = [unpacked(tiles[j // SHARE], a, j % SHARE) for a in range(6)]
         sums = [keep_ref[b, a, :, slab] + recv_ref[b, a, :, slab] + far[a] for a in range(3)]
@@ -474,50 +480,58 @@
         )
     work[0] = head
     out_ref[...] = work[0, pl.ds(pl.multiple_of(core * SUB, SUB), out_ref.shape[0]), :half]
-
-
-def sweeps(keep, recv, own, other, far, side, cross):
+    left_ref[...] = out_ref[:, :tile]
+    right_ref[...] = out_ref[:, tile:]
+
+
+def sweeps(keep, recv, mine, other, far, side, cross):
     blocks = keep.shape[0]
     half = keep.shape[3] // 2
     return pl.pallas_call(
         sweep_kernel,
         in_specs=[VMEM] * 7,
-        out_specs=VMEM,
-        out_shape=jax.ShapeDtypeStruct(((blocks - 1) * SUB, half), jnp.float32),
+        out_specs=[VMEM] * 3,
+        out_shape=[
+            jax.ShapeDtypeStruct(((blocks - 1) * SUB, half // part), jnp.float32) for part in (1, 2, 2)
+        ],
         scratch_shapes=[pltpu.VMEM((4, (blocks + 1) * SUB, half + LANE), jnp.float32)],
         compiler_params=params(12),
         cost_estimate=cost(20 * keep.size, 12 * keep.size),
         name="sweeps",
-    )(keep, recv, own, other, far, side, cross)
-
-
-def pass_on_kernel(core_ref, ring_ref, first, out_ref):
+    )(keep, recv, mine, other, far, side, cross)
+
+
+def pass_on_kernel(core_ref, ring_ref, first, *out_refs):
     del first
     chip, core = place()
-
-    @pl.when(chip == core)
-    def _():
-        out_ref[...] = ring_ref[...]
-
-    @pl.when(chip != core)
-    def _():
-        out_ref[...] = core_ref[...]
+    rows = out_refs[0].shape[1]
+    for i, out_ref in enumerate(out_refs):
+        part = slice(i * rows, (i + 1) * rows)
+
+        @pl.when(chip == core)
+        def _():
+            out_ref[...] = ring_ref[:, part]
+
+        @pl.when(chip != core)
+        def _():
+            out_ref[...] = core_ref[:, part]
 
 
 def pass_on(core_pair, ring, first):
     return pl.pallas_call(
         pass_on_kernel,
         in_specs=[VMEM] * 2 + [ANY],
-        out_specs=VMEM,
-        out_shape=jax.ShapeDtypeStruct(ring.shape, ring.dtype),
+        out_specs=[VMEM] * PARTS,
+        out_shape=[jax.ShapeDtypeStruct((2, ring.shape[1] // PARTS, ring.shape[2]), ring.dtype)] * PARTS,
         compiler_params=params(8),
         cost_estimate=cost(ring.size, 8 * ring.size),
         name="pass_on",
     )(core_pair, ring, first)
 
 
-def faces_kernel(moist_in, core_ref, rest_ref, ring_ref, got_ref, rain_ref, moist_out, tail_ref, ends, sems):
+def faces_kernel(moist_in, core_ref, rest_ref, ring_ref, rain_ref, *refs):
     del moist_in
+    got_refs, (moist_out, tail_ref, ends, sems) = refs[:PARTS], refs[PARTS:]
     chip, core = place()
     layers = moist_out.shape[0]
     copies = [
@@ -536,24 +550,32 @@
     def flux(upper, lower):
         return (upper[1] + lower[1]) * ((upper[0] - lower[0]) * (face / layer_thick) + face)
 
+    def got_faces(which, sign, ref, below):
+        for i, got in enumerate(got_refs):
+            rows = got.shape[1]
+            part = slice(i * rows, (i + 1) * rows)
+            mine = ref[0, part], ref[1, part]
+            change = flux(mine, got) if below else flux(got, mine)
+            ends[which, part] = ends[which, part] + sign * change
+
     @pl.when((core == 0) & (chip == 0))
     def _():
         ends[0] = ends[0] + gain * rain_ref[...]
-        ends[1] = ends[1] - flux(core_ref, got_ref)
+        got_faces(1, -1.0, core_ref, True)
 
     @pl.when((core == 1) & (chip == 0))
     def _():
         ends[0] = ends[0] + flux(ring_ref, core_ref)
-        ends[1] = ends[1] - flux(rest_ref, got_ref)
+        got_faces(1, -1.0, rest_ref, True)
 
     @pl.when((core == 0) & (chip == 1))
     def _():
-        ends[0] = ends[0] + flux(got_ref, rest_ref)
+        got_faces(0, 1.0, rest_ref, False)
         ends[1] = ends[1] - flux(core_ref, ring_ref)
 
     @pl.when(last)
     def _():
-        ends[0] = ends[0] + flux(got_ref, core_ref)
+        got_faces(0, 1.0, core_ref, False)
 
     stores[0].start()
 
@@ -574,7 +596,7 @@
 def faces(moist, core_pair, rest_pair, ring, got, rain):
     return pl.pallas_call(
         faces_kernel,
-        in_specs=[ANY] + [VMEM] * 5,
+        in_specs=[ANY] + [VMEM] * (4 + PARTS),
         out_specs=[ANY, VMEM],
         out_shape=[
             jax.ShapeDtypeStruct(moist.shape, moist.dtype),
@@ -585,10 +607,10 @@
         compiler_params=params(12),
         cost_estimate=cost(20 * rain.size, 32 * rain.size),
         name="faces",
-    )(moist, core_pair, rest_pair, ring, got, rain)
-
-
-def bottom_kernel(moist_in, tail_ref, own_ref, core_far, chip_far, both_far, moist_out, head_ref, last, sems):
+    )(moist, core_pair, rest_pair, ring, rain, *got)
+
+
+def near_bottom_kernel(moist_in, tail_ref, own_ref, left_ref, right_ref, moist_out, head_ref, done, sem):
     del moist_in
     chip, core = place()
     layers = moist_out.shape[0]
@@ -596,63 +618,70 @@
     tile = half // 2
     mine = pl.ds(pl.multiple_of(core * rows, rows), rows)
     theirs = pl.ds(pl.multiple_of((1 - core) * rows, rows), rows)
+    store = pltpu.make_async_copy(done, moist_out.at[layers - 1, :, half:], sem)
 
     @pl.when((core == 1) & (chip == 1))
     def _():
-        copies = []
-        for i, (left, right) in enumerate(((both_far, core_far), (chip_far, own_ref))):
-            where = slice(i * rows, (i + 1) * rows)
-            for ref, lanes in ((left, slice(0, half)), (right, slice(half, 2 * half))):
-                last[where, lanes] = tail_ref[0, where, lanes] + tail_ref[1, where, lanes] * ref[...]
-            copies.append(
-                pltpu.make_async_copy(last.at[where], moist_out.at[layers - 1, where], sems.at[i])
-            )
-            copies[-1].start()
-        for c in copies:
-            c.wait()
-
-    lanes = pl.ds(pl.multiple_of(core * tile, tile), tile)
-    head_ref[mine, :] = own_ref[:, lanes]
-    head_ref[theirs, :] = core_far[:, lanes]
-
-
-def bottom(moist, tail, own, core_far, chip_far, both_far):
+        for i, ref in enumerate((left_ref, right_ref)):
+            to, at = slice(i * tile, (i + 1) * tile), slice(half + i * tile, half + (i + 1) * tile)
+            done[:rows, to] = tail_ref[0, :rows, at] + tail_ref[1, :rows, at] * ref[...]
+        done[rows:] = tail_ref[0, rows:, half:] + tail_ref[1, rows:, half:] * own_ref[...]
+        store.start()
+
+    head_ref[mine, :] = own_ref[:, pl.ds(pl.multiple_of(core * tile, tile), tile)]
+    head_ref[theirs, :] = jnp.where(core == 0, left_ref[...], right_ref[...])
+
+    @pl.when((core == 1) & (chip == 1))
+    def _():
+        store.wait()
+
+
+def near_bottom(moist, tail, own, left, right):
     rows, half = own.shape
     return pl.pallas_call(
-        bottom_kernel,
-        in_specs=[ANY] + [VMEM] * 5,
+        near_bottom_kernel,
+        in_specs=[ANY] + [VMEM] * 4,
         out_specs=[ANY, VMEM],
         out_shape=[
             jax.ShapeDtypeStruct(moist.shape, moist.dtype),
             jax.ShapeDtypeStruct((2 * rows, half // 2), jnp.float32),
         ],
         input_output_aliases={0: 0},
-        scratch_shapes=[pltpu.VMEM(moist.shape[1:], jnp.float32), pltpu.SemaphoreType.DMA((2,))],
+        scratch_shapes=[pltpu.VMEM((2 * rows, half), jnp.float32), pltpu.SemaphoreType.DMA],
         compiler_params=params(12),
         cost_estimate=cost(10 * own.size, 40 * own.size),
+        name="near_bottom",
+    )(moist, tail, own, left, right)
+
+
+def bottom_kernel(moist_in, tail_ref, chip_far, both_far, moist_out, done, sem):
+    del moist_in
+    chip, core = place()
+    layers = moist_out.shape[0]
+    rows, half = chip_far.shape
+
+    @pl.when((core == 1) & (chip == 1))
+    def _():
+        store = pltpu.make_async_copy(done, moist_out.at[layers - 1, :, :half], sem)
+        for ref, where in ((both_far, slice(0, rows)), (chip_far, slice(rows, 2 * rows))):
+            done[where] = tail_ref[0, where, :half] + tail_ref[1, where, :half] * ref[...]
+        store.start()
+        store.wait()
+
+
+def bottom(moist, tail, chip_far, both_far):
+    rows, half = chip_far.shape
+    return pl.pallas_call(
+        bottom_kernel,
+        in_specs=[ANY] + [VMEM] * 3,
+        out_specs=ANY,
+        out_shape=jax.ShapeDtypeStruct(moist.shape, moist.dtype),
+        input_output_aliases={0: 0},
+        scratch_shapes=[pltpu.VMEM((2 * rows, half), jnp.float32), pltpu.SemaphoreType.DMA],
+        compiler_params=params(12),
+        cost_estimate=cost(4 * chip_far.size, 24 * chip_far.size),
         name="bottom",
-    )(moist, tail, own, core_far, chip_far, both_far)
-
-
-def inputs_kernel(old_ref, code_ref, section_ref, first, out_ref):
-    del first
-    code = code_ref[...]
-    river = jnp.where(code == 1, river_cond, jnp.where(code == 2, fixed_cond, 0.0))
-    out_ref[0] = old_ref[...]
-    out_ref[1] = river
-    out_ref[2] = river * section_ref[...]
-
-
-def inputs(head_old, cell_code, section, first):
-    return pl.pallas_call(
-        inputs_kernel,
-        in_specs=[VMEM] * 3 + [ANY],
-        out_specs=VMEM,
-        out_shape=jax.ShapeDtypeStruct((3,) + head_old.shape, jnp.float32),
-        compiler_params=params(4),
-        cost_estimate=cost(4 * head_old.size, 24 * head_old.size),
-        name="inputs",
-    )(head_old, cell_code, section, first)
+    )(moist, tail, chip_far, both_far)
 
 
 def gate_kernel(*refs):
@@ -698,20 +727,20 @@
     tables = (k_sat[None], alpha[None], theta_sat[None])
     face_pair = face(tables, pressure, texture, active)
     ring = ring_shift(face_pair)
-    own = inputs(head_old, cell_code, section, face_pair)
-    other = core_swap(own)
-    moist, keep, send, core_pair, rest_pair = soil(tables, pressure, texture, active)
-    recv = core_swap(gate(send, other))
-    message = pack(keep, recv, own, other)
+    moist, keep, send, mine, give, core_pair, rest_pair = soil(
+        tables, pressure, texture, active, head_old, cell_code, section
+    )
+    recv, other = core_swap(send), core_swap(give)
+    keep = gate(keep, ring)
+    message = pack(keep, recv, mine, other)
     far = chip_swap(message)
-    side, cross = rim(keep, recv, own, other, message, ring)
-    heads = sweeps(keep, recv, own, other, far, strip_swap(side), strip_swap(cross, 2))
-    got = core_swap(pass_on(core_pair, ring, side))
+    side, cross = rim(keep, recv, mine, other, message)
+    heads, left, right = sweeps(keep, recv, mine, other, far, strip_swap(side), strip_swap(cross, 2))
+    got = [core_swap(part) for part in pass_on(core_pair, ring, side)]
     moist, tail = faces(moist, core_pair, rest_pair, ring, got, rain)
+    moist, head = near_bottom(moist, tail, heads, core_swap(left), core_swap(right))
     heads_chip = gate(chip_swap(heads), stored=(moist,))
-    heads_core = core_swap(heads)
-    heads_both = core_swap(heads_chip)
-    return bottom(moist, tail, heads, heads_core, heads_chip, heads_both)
+    return bottom(moist, tail, heads_chip, core_swap(heads_chip)), head
 
 
 def solution(mesh):

time: 40.4 us -> 39.8 us (0.985)
  waiting for transfers between devices: 11.6 us -> 9.87 us
  starting transfers between devices: 10.7 us -> 11.8 us
    ppermute x1, waiting for transfers between devices: 0.03 us -> 2.75 us  [ring_shift(): return lax.ppermute(value, 'depth', [(1, 3), (3, 2), (2, 0), (0, 1)])]
    ppermute x2, waiting for transfers between devices: 2.22 us -> 0.01 us  [chip_swap(): lax.ppermute(value, 'depth', [(i, i ^ 2) for i in range(lax.axis_size('de...]
    ppermute x5 -> x7, waiting for transfers between devices: 3.4 us -> 1.29 us  [core_swap(): lax.ppermute(value, 'depth', [(i, i ^ 1) for i in range(lax.axis_size('de...]
    ppermute x2, starting transfers between devices: 4.99 us -> 5.67 us  [strip_swap(): return lax.ppermute(value, ('depth', 'strips'), pairs)]
    ppermute x1, starting transfers between devices: 0.06 us -> 0.47 us  [ring_shift(): return lax.ppermute(value, 'depth', [(1, 3), (3, 2), (2, 0), (0, 1)])]
    ppermute x5 -> x7, starting transfers between devices: 3.71 us -> 3.36 us  [core_swap(): lax.ppermute(value, 'depth', [(i, i ^ 1) for i in range(lax.axis_size('de...]
  transfers between devices with their start and end apart: 10 -> 12, of which waited for: 5 -> 3; matrix products, arithmetic and copies ran while one was open for 0% -> 0% of each run, Pallas kernels for 35% -> 37%
where the time goes in v5:
time: 39.8 us; the launch traced here: 39.6 us
  Pallas kernels  17.2 us (43%)
  starting transfers between devices  11.8 us (30%)
  waiting for transfers between devices  9.87 us (25%)
  between operations  0.72 us (2%)
    pallas_call x1, Pallas kernels, soil(): pl.pallas_call(soil_kernel, grid=(nrows // rows,), in_specs=[whole, whole...  10.4 us
    ppermute x2, waiting for transfers between devices, strip_swap(): return lax.ppermute(value, ('depth', 'strips'), pairs)  5.83 us
    ppermute x2, starting transfers between devices, strip_swap(): return lax.ppermute(value, ('depth', 'strips'), pairs)  5.67 us
    ppermute x7, starting transfers between devices, core_swap(): lax.ppermute(value, 'depth', [(i, i ^ 1) for i in range(lax.axis_size('de...  3.36 us
    ppermute x1, waiting for transfers between devices, ring_shift(): return lax.ppermute(value, 'depth', [(1, 3), (3, 2), (2, 0), (0, 1)])  2.75 us
    pallas_call x1, Pallas kernels, faces(): pl.pallas_call(faces_kernel, in_specs=[ANY] + [VMEM] * (4 + PARTS), out_s...  2.4 us
    ppermute x2, starting transfers between devices, chip_swap(): lax.ppermute(value, 'depth', [(i, i ^ 2) for i in range(lax.axis_size('de...  2.31 us
    pallas_call x1, Pallas kernels, face(): pl.pallas_call(face_kernel, in_specs=[HBM] * 5, out_specs=VMEM, out_shape...  2.22 us
  transfers between devices with their start and end apart: 12, of which 3 were waited for; matrix products, arithmetic and copies ran while one was open for 0% of the time, Pallas kernels for 37%

profile of v5, /device:TPU:0, one launch (start us, length us, event | category | flops | bytes accessed | tf_op | source)
XLA Modules:
  0.0 39.6 jit_solution(8432414707934534522)
XLA Ops:
  0.6 2.2 %face.1 = f32[2,128,1024]{2,1,0:T(8,128)S(1)} custom-call(f32[1,12]{1,0:T(1,128)} %bitcast.3, f32[1,12]{1,0:T(1,128)} %bitcast.5, f32[8,128,1024]{2,1,0:T(8,128)} %psi_hbm.1, s32[8,128,1024]{2,1,0:T(8,128)} %tex_hbm.1, s32[8,128,1024]{2,1,0:T(8,128)} %act_hbm.1), custom_call_target="tpu_custom_call" | custom-call | flops 2621440 | bytes 2621440 | tf_op jit(solution)/shard_map/face/pallas_call | solution.py:110
  2.9 0.5 %collective-permute-start = (f32[2,128,1024]{2,1,0:T(8,128)S(1)}, f32[2,128,1024]{2,1,0:T(8,128)S(1)}, u32[]{:S(2)}, u32[]{:S(2)}) collective-permute-start(f32[2,128,1024]{2,1,0:T(8,128)S(1)} %face.1), channel_id=1, source_target_pairs={{8,24},{24,16},{16,0},{0,8},{9,25},{25,17},{17,1},{1,9},{10,26},{2... | collective-permute-start | bytes 3145736 | tf_op jit(solution)/shard_map/ppermute | solution.py:713
  3.3 10.4 %soil.1 = (f32[8,128,1024]{2,1,0:T(8,128)}, f32[9,3,8,1024]{3,2,1,0:T(8,128)S(1)}, f32[9,3,8,1024]{3,2,1,0:T(8,128)S(1)}, f32[9,3,8,256]{3,2,1,0:T(8,128)S(1)}, ...) custom-call(f32[1,12]{1,0:T(1,128)} %bitcast.4, f32[1,12]{1,0:T(1,128)} %bitcast.6, ...), custom_call_target="tpu_custom_call" | custom-call | flops 62914560 | bytes 20971520 | tf_op jit(solution)/shard_map/soil/pallas_call | solution.py:233
  13.7 2.1 %collective-permute-start.1 = (f32[9,3,8,1024]{3,2,1,0:T(8,128)S(1)}, f32[9,3,8,1024]{3,2,1,0:T(8,128)S(1)}, u32[]{:S(2)}, u32[]{:S(2)}) collective-permute-start(f32[9,3,8,1024]{3,2,1,0:T(8,128)S(1)} %get-tuple-element.24), channel_id=1, source_target_pairs={{0,8},{8,0},{16,24},{24,16},{1,9},{9,1},{17,25},{25,17},{2,10},{10... | collective-permute-start | bytes 2654216 | tf_op jit(solution)/shard_map/ppermute | solution.py:705
  15.8 0.1 collective-permute-start.2
  15.9 2.7 %collective-permute-done.refs_1_.ring_ref = f32[2,128,1024]{2,1,0:T(8,128)S(1)} collective-permute-done((f32[2,128,1024]{2,1,0:T(8,128)S(1)}, f32[2,128,1024]{2,1,0:T(8,128)S(1)}, u32[]{:S(2)}, u32[]{:S(2)}) %collective-permute-start) | collective-permute-done | bytes 1048608 | tf_op jit(solution)/shard_map/ppermute | solution.py:713
  18.6 0.0 collective-permute-done.2.other_ref
  18.6 0.0 collective-permute-done.1.recv_ref
  18.6 0.2 pack.1.refs_0_
  18.8 0.0 copy-start
  18.8 0.6 %collective-permute-start.5 = (f32[26,8,512]{2,1,0:T(8,128)S(1)}, f32[26,8,512]{2,1,0:T(8,128)S(1)}, u32[]{:S(2)}, u32[]{:S(2)}) collective-permute-start(f32[26,8,512]{2,1,0:T(8,128)S(1)} %pack.1.refs_0_), channel_id=1, source_target_pairs={{0,16},{8,24},{16,0},{24,8},{1,17},{9,25},{17,1},{25,9},{2,18},{10... | collective-permute-start | bytes 1277960 | tf_op jit(solution)/shard_map/ppermute | solution.py:709
  19.4 0.1 rim.1
  19.5 0.1 pass_on.1
  19.6 0.1 collective-permute-start.3
  19.7 0.4 %collective-permute-start.4 = (f32[2,64,1024]{2,1,0:T(8,128)S(1)}, f32[2,64,1024]{2,1,0:T(8,128)S(1)}, u32[]{:S(2)}, u32[]{:S(2)}) collective-permute-start(f32[2,64,1024]{2,1,0:T(8,128)S(1)} %get-tuple-element.29), channel_id=1, source_target_pairs={{0,8},{8,0},{16,24},{24,16},{1,9},{9,1},{17,25},{25,17},{2,10},{10... | collective-permute-start | bytes 1572872 | tf_op jit(solution)/shard_map/ppermute | solution.py:705
  20.2 4.6 %collective-permute-start.6 = (f32[7,8,512]{2,1,0:T(8,128)S(1)}, f32[7,8,512]{2,1,0:T(8,128)S(1)}, u32[]{:S(2)}, u32[]{:S(2)}) collective-permute-start(f32[7,8,512]{2,1,0:T(8,128)S(1)} %get-tuple-element.27.first), channel_id=1, source_target_pairs={{8,1},{1,8},{9,2},{2,9},{10,3},{3,10},{11,4},{4,11},{12,5},{5,12},... | collective-permute-start | bytes 344072 | tf_op jit(solution)/shard_map/ppermute | solution.py:723
  24.7 1.1 %collective-permute-start.7 = (f32[2,8,512]{2,1,0:T(8,128)S(1)}, f32[2,8,512]{2,1,0:T(8,128)S(1)}, u32[]{:S(2)}, u32[]{:S(2)}) collective-permute-start(f32[2,8,512]{2,1,0:T(8,128)S(1)} %get-tuple-element.32), channel_id=1, source_target_pairs={{8,17},{17,8},{9,18},{18,9},{10,19},{19,10},{11,20},{20,11},{12,21... | collective-permute-start | bytes 98312 | tf_op jit(solution)/shard_map/ppermute | solution.py:723
  25.8 5.8 %collective-permute-done.7.cross_ref = f32[2,8,512]{2,1,0:T(8,128)S(1)} collective-permute-done((f32[2,8,512]{2,1,0:T(8,128)S(1)}, f32[2,8,512]{2,1,0:T(8,128)S(1)}, u32[]{:S(2)}, u32[]{:S(2)}) %collective-permute-start.7) | collective-permute-done | bytes 32800 | tf_op jit(solution)/shard_map/ppermute | solution.py:723
  31.7 0.0 collective-permute-done.6.side_ref
  31.7 0.0 collective-permute-done.5.far_ref
  31.7 1.1 %sweeps.1 = (f32[64,512]{1,0:T(8,128)S(1)}, f32[64,256]{1,0:T(8,128)S(1)}, f32[64,256]{1,0:T(8,128)S(1)}) custom-call(f32[9,3,8,1024]{3,2,1,0:T(8,128)S(1)} %gate.2.keep_ref, f32[9,3,8,1024]{3,2,1,0:T(8,128)S(1)} %collective-permute-done.1.recv_ref, f32[9,3,8,256]{3,2,1,0:T(8,128)S(1)} %get-tuple-element.25.mine_ref, ...), custom_call_target="tpu_custom_call" | custom-call | flops 4423680 | bytes 2654208 | tf_op jit(solution)/shard_map/sweeps/pallas_call | solution.py:490
  32.7 1.7 %collective-permute-start.10 = (f32[64,512]{1,0:T(8,128)S(1)}, f32[64,512]{1,0:T(8,128)S(1)}, u32[]{:S(2)}, u32[]{:S(2)}) collective-permute-start(f32[64,512]{1,0:T(8,128)S(1)} %get-tuple-element.33.own_ref), channel_id=1, source_target_pairs={{0,16},{8,24},{16,0},{24,8},{1,17},{9,25},{17,1},{25,9},{2,18},{10... | collective-permute-start | bytes 393224 | tf_op jit(solution)/shard_map/ppermute | solution.py:709
  34.5 0.0 collective-permute-start.8
  34.5 0.5 %collective-permute-start.9 = (f32[64,256]{1,0:T(8,128)S(1)}, f32[64,256]{1,0:T(8,128)S(1)}, u32[]{:S(2)}, u32[]{:S(2)}) collective-permute-start(f32[64,256]{1,0:T(8,128)S(1)} %get-tuple-element.35), channel_id=1, source_target_pairs={{0,8},{8,0},{16,24},{24,16},{1,9},{9,1},{17,25},{25,17},{2,10},{10... | collective-permute-start | bytes 196616 | tf_op jit(solution)/shard_map/ppermute | solution.py:705
  35.0 0.0 collective-permute-done.3.refs_0_
  35.0 0.0 collective-permute-done.4.refs_1_
  35.0 0.0 copy-done
  35.0 2.4 %faces.1 = (f32[8,128,1024]{2,1,0:T(8,128)}, f32[2,128,1024]{2,1,0:T(8,128)S(1)}) custom-call(f32[8,128,1024]{2,1,0:T(8,128)} %get-tuple-element.20.moist_in, f32[2,128,1024]{2,1,0:T(8,128)S(1)} %get-tuple-element.21.core_ref, f32[2,128,1024]{2,1,0:T(8,128)S(1)} %get-tuple-element.22.rest_ref, ...), custom_call_target="tpu_custom_call", output_to_operand_aliasing={{0}: (0, {})} | custom-call | flops 2621440 | bytes 4194304 | tf_op jit(solution)/shard_map/faces/pallas_call | solution.py:597
  37.4 0.0 collective-permute-done.8.left_ref
  37.4 0.0 collective-permute-done.9.right_ref
  37.4 0.7 %near_bottom.1 = (f32[8,128,1024]{2,1,0:T(8,128)}, f32[128,256]{1,0:T(8,128)}) custom-call(f32[8,128,1024]{2,1,0:T(8,128)} %get-tuple-element.30.moist_in, f32[2,128,1024]{2,1,0:T(8,128)S(1)} %get-tuple-element.31.tail_ref, f32[64,512]{1,0:T(8,128)S(1)} %get-tuple-element.33.own_ref, ...), custom_call_target="tpu_custom_call", output_to_operand_aliasing={{0}: (0, {})} | custom-call | flops 327680 | bytes 1310720 | tf_op jit(solution)/shard_map/near_bottom/pallas_call | solution.py:641
  38.1 0.0 collective-permute-done.10.refs_0_
  38.1 0.1 collective-permute-start.11
  38.3 1.3 %collective-permute-done.11.both_far = f32[64,512]{1,0:T(8,128)S(1)} collective-permute-done((f32[64,512]{1,0:T(8,128)S(1)}, f32[64,512]{1,0:T(8,128)S(1)}, u32[]{:S(2)}, u32[]{:S(2)}) %collective-permute-start.11) | collective-permute-done | bytes 131104 | tf_op jit(solution)/shard_map/ppermute | solution.py:705
  (3 shorter events, 0.0 us)
Async XLA Ops:
  2.9 15.8 %collective-permute-start = (f32[2,128,1024]{2,1,0:T(8,128)S(1)}, f32[2,128,1024]{2,1,0:T(8,128)S(1)}, u32[]{:S(2)}, u32[]{:S(2)}) collective-permute-start(f32[2,128,1024]{2,1,0:T(8,128)S(1)} %face.1), channel_id=1, source_target_pairs={{8,24},{24,16},{16,0},{0,8},{9,25},{25,17},{17,1},{1,9},{10,26},{2... | collective-permute-start | bytes 3145736 | tf_op jit(solution)/shard_map/ppermute | solution.py:713
  13.7 4.9 %collective-permute-start.1 = (f32[9,3,8,1024]{3,2,1,0:T(8,128)S(1)}, f32[9,3,8,1024]{3,2,1,0:T(8,128)S(1)}, u32[]{:S(2)}, u32[]{:S(2)}) collective-permute-start(f32[9,3,8,1024]{3,2,1,0:T(8,128)S(1)} %get-tuple-element.24), channel_id=1, source_target_pairs={{0,8},{8,0},{16,24},{24,16},{1,9},{9,1},{17,25},{25,17},{2,10},{10... | collective-permute-start | bytes 2654216 | tf_op jit(solution)/shard_map/ppermute | solution.py:705
  15.8 2.8 %collective-permute-start.2 = (f32[9,3,8,256]{3,2,1,0:T(8,128)S(1)}, f32[9,3,8,256]{3,2,1,0:T(8,128)S(1)}, u32[]{:S(2)}, u32[]{:S(2)}) collective-permute-start(f32[9,3,8,256]{3,2,1,0:T(8,128)S(1)} %get-tuple-element.26), channel_id=1, source_target_pairs={{0,8},{8,0},{16,24},{24,16},{1,9},{9,1},{17,25},{25,17},{2,10},{10... | collective-permute-start | bytes 663560 | tf_op jit(solution)/shard_map/ppermute | solution.py:705
  18.8 16.2 %copy-start = (f32[128,1024]{1,0:T(8,128)S(1)}, f32[128,1024]{1,0:T(8,128)}, u32[]{:S(2)}) copy-start(f32[128,1024]{1,0:T(8,128)} %rain_ref.1) | copy-start | bytes 1572868
  18.8 12.8 %collective-permute-start.5 = (f32[26,8,512]{2,1,0:T(8,128)S(1)}, f32[26,8,512]{2,1,0:T(8,128)S(1)}, u32[]{:S(2)}, u32[]{:S(2)}) collective-permute-start(f32[26,8,512]{2,1,0:T(8,128)S(1)} %pack.1.refs_0_), channel_id=1, source_target_pairs={{0,16},{8,24},{16,0},{24,8},{1,17},{9,25},{17,1},{25,9},{2,18},{10... | collective-permute-start | bytes 1277960 | tf_op jit(solution)/shard_map/ppermute | solution.py:709
  19.6 15.4 %collective-permute-start.3 = (f32[2,64,1024]{2,1,0:T(8,128)S(1)}, f32[2,64,1024]{2,1,0:T(8,128)S(1)}, u32[]{:S(2)}, u32[]{:S(2)}) collective-permute-start(f32[2,64,1024]{2,1,0:T(8,128)S(1)} %get-tuple-element.28), channel_id=1, source_target_pairs={{0,8},{8,0},{16,24},{24,16},{1,9},{9,1},{17,25},{25,17},{2,10},{10... | collective-permute-start | bytes 1572872 | tf_op jit(solution)/shard_map/ppermute | solution.py:705
  19.7 15.3 %collective-permute-start.4 = (f32[2,64,1024]{2,1,0:T(8,128)S(1)}, f32[2,64,1024]{2,1,0:T(8,128)S(1)}, u32[]{:S(2)}, u32[]{:S(2)}) collective-permute-start(f32[2,64,1024]{2,1,0:T(8,128)S(1)} %get-tuple-element.29), channel_id=1, source_target_pairs={{0,8},{8,0},{16,24},{24,16},{1,9},{9,1},{17,25},{25,17},{2,10},{10... | collective-permute-start | bytes 1572872 | tf_op jit(solution)/shard_map/ppermute | solution.py:705
  20.2 11.5 %collective-permute-start.6 = (f32[7,8,512]{2,1,0:T(8,128)S(1)}, f32[7,8,512]{2,1,0:T(8,128)S(1)}, u32[]{:S(2)}, u32[]{:S(2)}) collective-permute-start(f32[7,8,512]{2,1,0:T(8,128)S(1)} %get-tuple-element.27.first), channel_id=1, source_target_pairs={{8,1},{1,8},{9,2},{2,9},{10,3},{3,10},{11,4},{4,11},{12,5},{5,12},... | collective-permute-start | bytes 344072 | tf_op jit(solution)/shard_map/ppermute | solution.py:723
  24.7 6.9 %collective-permute-start.7 = (f32[2,8,512]{2,1,0:T(8,128)S(1)}, f32[2,8,512]{2,1,0:T(8,128)S(1)}, u32[]{:S(2)}, u32[]{:S(2)}) collective-permute-start(f32[2,8,512]{2,1,0:T(8,128)S(1)} %get-tuple-element.32), channel_id=1, source_target_pairs={{8,17},{17,8},{9,18},{18,9},{10,19},{19,10},{11,20},{20,11},{12,21... | collective-permute-start | bytes 98312 | tf_op jit(solution)/shard_map/ppermute | solution.py:723
  32.7 5.4 %collective-permute-start.10 = (f32[64,512]{1,0:T(8,128)S(1)}, f32[64,512]{1,0:T(8,128)S(1)}, u32[]{:S(2)}, u32[]{:S(2)}) collective-permute-start(f32[64,512]{1,0:T(8,128)S(1)} %get-tuple-element.33.own_ref), channel_id=1, source_target_pairs={{0,16},{8,24},{16,0},{24,8},{1,17},{9,25},{17,1},{25,9},{2,18},{10... | collective-permute-start | bytes 393224 | tf_op jit(solution)/shard_map/ppermute | solution.py:709
  34.5 2.9 %collective-permute-start.8 = (f32[64,256]{1,0:T(8,128)S(1)}, f32[64,256]{1,0:T(8,128)S(1)}, u32[]{:S(2)}, u32[]{:S(2)}) collective-permute-start(f32[64,256]{1,0:T(8,128)S(1)} %get-tuple-element.34), channel_id=1, source_target_pairs={{0,8},{8,0},{16,24},{24,16},{1,9},{9,1},{17,25},{25,17},{2,10},{10... | collective-permute-start | bytes 196616 | tf_op jit(solution)/shard_map/ppermute | solution.py:705
  34.5 2.9 %collective-permute-start.9 = (f32[64,256]{1,0:T(8,128)S(1)}, f32[64,256]{1,0:T(8,128)S(1)}, u32[]{:S(2)}, u32[]{:S(2)}) collective-permute-start(f32[64,256]{1,0:T(8,128)S(1)} %get-tuple-element.35), channel_id=1, source_target_pairs={{0,8},{8,0},{16,24},{24,16},{1,9},{9,1},{17,25},{25,17},{2,10},{10... | collective-permute-start | bytes 196616 | tf_op jit(solution)/shard_map/ppermute | solution.py:705
  38.1 1.4 %collective-permute-start.11 = (f32[64,512]{1,0:T(8,128)S(1)}, f32[64,512]{1,0:T(8,128)S(1)}, u32[]{:S(2)}, u32[]{:S(2)}) collective-permute-start(f32[64,512]{1,0:T(8,128)S(1)} %gate.3.chip_far), channel_id=1, source_target_pairs={{0,8},{8,0},{16,24},{24,16},{1,9},{9,1},{17,25},{25,17},{2,10},{10... | collective-permute-start | bytes 393224 | tf_op jit(solution)/shard_map/ppermute | solution.py:705

commit v6 on v5

--- a/solution.py
+++ b/solution.py
@@ -68,36 +68,46 @@
     layer = (1 - chip) * (psi_hbm.shape[0] - 1)
     cols = psi_hbm.shape[2]
     classes = sat_hbm.shape[1]
-    copies = [
-        pltpu.make_async_copy(src, dst, sems.at[i])
-        for i, (src, dst) in enumerate(
-            (
-                (sat_hbm, given.at[0]),
-                (alpha_hbm, given.at[1]),
-                (psi_hbm.at[layer], out_ref.at[0]),
-                (tex_hbm.at[layer], kinds),
-                (act_hbm.at[layer], acts),
-            )
+    chunks = 2
+    rows = kinds.shape[0] // chunks
+
+    def copies(i):
+        part = pl.ds(i * rows, rows)
+        pairs = (
+            (psi_hbm.at[layer, part], out_ref.at[0, part]),
+            (tex_hbm.at[layer, part], kinds.at[part]),
+            (act_hbm.at[layer, part], acts.at[part]),
         )
+        return [pltpu.make_async_copy(src, dst, sems.at[i, k]) for k, (src, dst) in enumerate(pairs)]
+
+    tables = [
+        pltpu.make_async_copy(src, given.at[k], sems.at[chunks, k]) for k, src in enumerate((sat_hbm, alpha_hbm))
     ]
-    for c in copies:
+    for c in tables:
         c.start()
-    for c in copies:
+    for i in range(chunks):
+        for c in copies(i):
+            c.start()
+    for c in tables:
         c.wait()
     for i, scale in enumerate((1.0, 0.5 * math.log2(math.e))):
         tab[i, :, :classes] = jnp.broadcast_to(given[i] * scale, (SUB, classes))
 
-    def columns(q, carry):
-        lanes = pl.ds(pl.multiple_of(q * LANE, LANE), LANE)
-        for r in range(0, kinds.shape[0], SUB):
-            rws = slice(r, r + SUB)
-            kind = kinds[rws, lanes]
-            wet = jnp.exp2(gathered(tab[1], kind) * jnp.minimum(out_ref[0, rws, lanes], 0.0))
-            active = acts[rws, lanes].astype(jnp.float32)
-            out_ref[1, rws, lanes] = gathered(tab[0], kind) * active * (wet * wet)
-        return carry
-
-    lax.fori_loop(0, cols // LANE, columns, 0, unroll=4)
+    for i in range(chunks):
+        for c in copies(i):
+            c.wait()
+
+        def columns(q, carry):
+            lanes = pl.ds(pl.multiple_of(q * LANE, LANE), LANE)
+            for r in range(i * rows, (i + 1) * rows, SUB):
+                rws = slice(r, r + SUB)
+                kind = kinds[rws, lanes]
+                wet = jnp.exp2(gathered(tab[1], kind) * jnp.minimum(out_ref[0, rws, lanes], 0.0))
+                active = acts[rws, lanes].astype(jnp.float32)
+                out_ref[1, rws, lanes] = gathered(tab[0], kind) * active * (wet * wet)
+            return carry
+
+        lax.fori_loop(0, cols // LANE, columns, 0, unroll=8)
 
 
 def in_hbm(*arrays):
@@ -117,7 +127,7 @@
             pltpu.VMEM((nrows, cols), jnp.int32),
             pltpu.VMEM((2,) + tables[0].shape, jnp.float32),
             pltpu.VMEM((2, SUB, LANE), jnp.float32),
-            pltpu.SemaphoreType.DMA((5,)),
+            pltpu.SemaphoreType.DMA((3, 3)),
         ],
         compiler_params=params(8),
         cost_estimate=cost(20 * size, 20 * size, size),
@@ -731,10 +741,9 @@
         tables, pressure, texture, active, head_old, cell_code, section
     )
     recv, other = core_swap(send), core_swap(give)
-    keep = gate(keep, ring)
     message = pack(keep, recv, mine, other)
     far = chip_swap(message)
-    side, cross = rim(keep, recv, mine, other, message)
+    side, cross = rim(keep, recv, mine, other, message, ring)
     heads, left, right = sweeps(keep, recv, mine, other, far, strip_swap(side), strip_swap(cross, 2))
     got = [core_swap(part) for part in pass_on(core_pair, ring, side)]
     moist, tail = faces(moist, core_pair, rest_pair, ring, got, rain)

time: 39.8 us -> 39.1 us (0.982)
  starting transfers between devices: 11.8 us -> 10.5 us
  waiting for transfers between devices: 9.87 us -> 10.8 us
    ppermute x1, waiting for transfers between devices: 2.75 us -> 0.01 us  [ring_shift(): return lax.ppermute(value, 'depth', [(1, 3), (3, 2), (2, 0), (0, 1)])]
    ppermute x7, waiting for transfers between devices: 1.29 us -> 3.66 us  [core_swap(): lax.ppermute(value, 'depth', [(i, i ^ 1) for i in range(lax.axis_size('de...]
    ppermute x2, starting transfers between devices: 5.67 us -> 4.96 us  [strip_swap(): return lax.ppermute(value, ('depth', 'strips'), pairs)]
    ppermute x2, waiting for transfers between devices: 5.83 us -> 6.54 us  [strip_swap(): return lax.ppermute(value, ('depth', 'strips'), pairs)]
    ppermute x2, waiting for transfers between devices: 0.01 us -> 0.58 us  [chip_swap(): lax.ppermute(value, 'depth', [(i, i ^ 2) for i in range(lax.axis_size('de...]
    ppermute x2, starting transfers between devices: 2.31 us -> 1.83 us  [chip_swap(): lax.ppermute(value, 'depth', [(i, i ^ 2) for i in range(lax.axis_size('de...]
  transfers between devices with their start and end apart: 12 -> 12, of which waited for: 3 -> 4; matrix products, arithmetic and copies ran while one was open for 0% -> 0% of each run, Pallas kernels for 37% -> 38%
where the time goes in v6:
time: 39.1 us; the launch traced here: 38.9 us
  Pallas kernels  16.9 us (43%)
  waiting for transfers between devices  10.8 us (28%)
  starting transfers between devices  10.5 us (27%)
  between operations  0.71 us (2%)
    pallas_call x1, Pallas kernels, soil(): pl.pallas_call(soil_kernel, grid=(nrows // rows,), in_specs=[whole, whole...  10.4 us
    ppermute x2, waiting for transfers between devices, strip_swap(): return lax.ppermute(value, ('depth', 'strips'), pairs)  6.54 us
    ppermute x2, starting transfers between devices, strip_swap(): return lax.ppermute(value, ('depth', 'strips'), pairs)  4.96 us
    ppermute x7, waiting for transfers between devices, core_swap(): lax.ppermute(value, 'depth', [(i, i ^ 1) for i in range(lax.axis_size('de...  3.66 us
    ppermute x7, starting transfers between devices, core_swap(): lax.ppermute(value, 'depth', [(i, i ^ 1) for i in range(lax.axis_size('de...  3.23 us
    pallas_call x1, Pallas kernels, faces(): pl.pallas_call(faces_kernel, in_specs=[ANY] + [VMEM] * (4 + PARTS), out_s...  2.4 us
    pallas_call x1, Pallas kernels, face(): pl.pallas_call(face_kernel, in_specs=[HBM] * 5, out_specs=VMEM, out_shape...  2 us
    ppermute x2, starting transfers between devices, chip_swap(): lax.ppermute(value, 'depth', [(i, i ^ 2) for i in range(lax.axis_size('de...  1.83 us
  transfers between devices with their start and end apart: 12, of which 4 were waited for; matrix products, arithmetic and copies ran while one was open for 0% of the time, Pallas kernels for 38%

profile of v6, /device:TPU:0, one launch (start us, length us, event | category | flops | bytes accessed | tf_op | source)
XLA Modules:
  0.0 38.9 jit_solution(6306094071761904070)
XLA Ops:
  0.6 2.0 %face.1 = f32[2,128,1024]{2,1,0:T(8,128)S(1)} custom-call(f32[1,12]{1,0:T(1,128)} %bitcast.3, f32[1,12]{1,0:T(1,128)} %bitcast.5, f32[8,128,1024]{2,1,0:T(8,128)} %psi_hbm.1, s32[8,128,1024]{2,1,0:T(8,128)} %tex_hbm.1, s32[8,128,1024]{2,1,0:T(8,128)} %act_hbm.1), custom_call_target="tpu_custom_call" | custom-call | flops 2621440 | bytes 2621440 | tf_op jit(solution)/shard_map/face/pallas_call | solution.py:120
  2.6 0.5 %collective-permute-start = (f32[2,128,1024]{2,1,0:T(8,128)S(1)}, f32[2,128,1024]{2,1,0:T(8,128)S(1)}, u32[]{:S(2)}, u32[]{:S(2)}) collective-permute-start(f32[2,128,1024]{2,1,0:T(8,128)S(1)} %face.1), channel_id=1, source_target_pairs={{8,24},{24,16},{16,0},{0,8},{9,25},{25,17},{17,1},{1,9},{10,26},{2... | collective-permute-start | bytes 3145736 | tf_op jit(solution)/shard_map/ppermute | solution.py:723
  3.1 10.4 %soil.1 = (f32[8,128,1024]{2,1,0:T(8,128)}, f32[9,3,8,1024]{3,2,1,0:T(8,128)S(1)}, f32[9,3,8,1024]{3,2,1,0:T(8,128)S(1)}, f32[9,3,8,256]{3,2,1,0:T(8,128)S(1)}, ...) custom-call(f32[1,12]{1,0:T(1,128)} %bitcast.4, f32[1,12]{1,0:T(1,128)} %bitcast.6, ...), custom_call_target="tpu_custom_call" | custom-call | flops 62914560 | bytes 20971520 | tf_op jit(solution)/shard_map/soil/pallas_call | solution.py:243
  13.5 2.1 %collective-permute-start.1 = (f32[9,3,8,1024]{3,2,1,0:T(8,128)S(1)}, f32[9,3,8,1024]{3,2,1,0:T(8,128)S(1)}, u32[]{:S(2)}, u32[]{:S(2)}) collective-permute-start(f32[9,3,8,1024]{3,2,1,0:T(8,128)S(1)} %get-tuple-element.24), channel_id=1, source_target_pairs={{0,8},{8,0},{16,24},{24,16},{1,9},{9,1},{17,25},{25,17},{2,10},{10... | collective-permute-start | bytes 2654216 | tf_op jit(solution)/shard_map/ppermute | solution.py:715
  15.6 0.1 collective-permute-start.2
  15.6 2.3 %collective-permute-done.2.other_ref = f32[9,3,8,256]{3,2,1,0:T(8,128)S(1)} collective-permute-done((f32[9,3,8,256]{3,2,1,0:T(8,128)S(1)}, f32[9,3,8,256]{3,2,1,0:T(8,128)S(1)}, u32[]{:S(2)}, u32[]{:S(2)}) %collective-permute-start.2) | collective-permute-done | bytes 221216 | tf_op jit(solution)/shard_map/ppermute | solution.py:715
  18.0 0.0 collective-permute-done.1.recv_ref
  18.0 0.2 pack.1.refs_0_
  18.1 0.0 copy-start
  18.2 1.0 %collective-permute-start.5 = (f32[26,8,512]{2,1,0:T(8,128)S(1)}, f32[26,8,512]{2,1,0:T(8,128)S(1)}, u32[]{:S(2)}, u32[]{:S(2)}) collective-permute-start(f32[26,8,512]{2,1,0:T(8,128)S(1)} %pack.1.refs_0_), channel_id=1, source_target_pairs={{0,16},{8,24},{16,0},{24,8},{1,17},{9,25},{17,1},{25,9},{2,18},{10... | collective-permute-start | bytes 1277960 | tf_op jit(solution)/shard_map/ppermute | solution.py:719
  19.2 0.0 collective-permute-done.refs_1_.ring_ref
  19.2 0.1 rim.1
  19.3 0.1 pass_on.1
  19.4 0.1 collective-permute-start.3
  19.5 0.4 %collective-permute-start.4 = (f32[2,64,1024]{2,1,0:T(8,128)S(1)}, f32[2,64,1024]{2,1,0:T(8,128)S(1)}, u32[]{:S(2)}, u32[]{:S(2)}) collective-permute-start(f32[2,64,1024]{2,1,0:T(8,128)S(1)} %get-tuple-element.29), channel_id=1, source_target_pairs={{0,8},{8,0},{16,24},{24,16},{1,9},{9,1},{17,25},{25,17},{2,10},{10... | collective-permute-start | bytes 1572872 | tf_op jit(solution)/shard_map/ppermute | solution.py:715
  19.9 4.6 %collective-permute-start.6 = (f32[7,8,512]{2,1,0:T(8,128)S(1)}, f32[7,8,512]{2,1,0:T(8,128)S(1)}, u32[]{:S(2)}, u32[]{:S(2)}) collective-permute-start(f32[7,8,512]{2,1,0:T(8,128)S(1)} %get-tuple-element.27.first), channel_id=1, source_target_pairs={{8,1},{1,8},{9,2},{2,9},{10,3},{3,10},{11,4},{4,11},{12,5},{5,12},... | collective-permute-start | bytes 344072 | tf_op jit(solution)/shard_map/ppermute | solution.py:733
  24.5 0.4 %collective-permute-start.7 = (f32[2,8,512]{2,1,0:T(8,128)S(1)}, f32[2,8,512]{2,1,0:T(8,128)S(1)}, u32[]{:S(2)}, u32[]{:S(2)}) collective-permute-start(f32[2,8,512]{2,1,0:T(8,128)S(1)} %get-tuple-element.32), channel_id=1, source_target_pairs={{8,17},{17,8},{9,18},{18,9},{10,19},{19,10},{11,20},{20,11},{12,21... | collective-permute-start | bytes 98312 | tf_op jit(solution)/shard_map/ppermute | solution.py:733
  24.9 6.5 %collective-permute-done.7.cross_ref = f32[2,8,512]{2,1,0:T(8,128)S(1)} collective-permute-done((f32[2,8,512]{2,1,0:T(8,128)S(1)}, f32[2,8,512]{2,1,0:T(8,128)S(1)}, u32[]{:S(2)}, u32[]{:S(2)}) %collective-permute-start.7) | collective-permute-done | bytes 32800 | tf_op jit(solution)/shard_map/ppermute | solution.py:733
  31.4 0.0 collective-permute-done.6.side_ref
  31.4 0.0 collective-permute-done.5.far_ref
  31.4 1.1 %sweeps.1 = (f32[64,512]{1,0:T(8,128)S(1)}, f32[64,256]{1,0:T(8,128)S(1)}, f32[64,256]{1,0:T(8,128)S(1)}) custom-call(f32[9,3,8,1024]{3,2,1,0:T(8,128)S(1)} %get-tuple-element.23.keep_ref, f32[9,3,8,1024]{3,2,1,0:T(8,128)S(1)} %collective-permute-done.1.recv_ref, f32[9,3,8,256]{3,2,1,0:T(8,128)S(1)} %get-tuple-element.25.mine_ref, ...), custom_call_target="tpu_custom_call" | custom-call | flops 4423680 | bytes 2654208 | tf_op jit(solution)/shard_map/sweeps/pallas_call | solution.py:500
  32.5 0.8 %collective-permute-start.10 = (f32[64,512]{1,0:T(8,128)S(1)}, f32[64,512]{1,0:T(8,128)S(1)}, u32[]{:S(2)}, u32[]{:S(2)}) collective-permute-start(f32[64,512]{1,0:T(8,128)S(1)} %get-tuple-element.33.own_ref), channel_id=1, source_target_pairs={{0,16},{8,24},{16,0},{24,8},{1,17},{9,25},{17,1},{25,9},{2,18},{10... | collective-permute-start | bytes 393224 | tf_op jit(solution)/shard_map/ppermute | solution.py:719
  33.3 0.0 collective-permute-start.8
  33.3 0.5 %collective-permute-start.9 = (f32[64,256]{1,0:T(8,128)S(1)}, f32[64,256]{1,0:T(8,128)S(1)}, u32[]{:S(2)}, u32[]{:S(2)}) collective-permute-start(f32[64,256]{1,0:T(8,128)S(1)} %get-tuple-element.35), channel_id=1, source_target_pairs={{0,8},{8,0},{16,24},{24,16},{1,9},{9,1},{17,25},{25,17},{2,10},{10... | collective-permute-start | bytes 196616 | tf_op jit(solution)/shard_map/ppermute | solution.py:715
  33.8 0.0 collective-permute-done.3.refs_0_
  33.8 0.0 collective-permute-done.4.refs_1_
  33.8 0.0 copy-done
  33.8 2.4 %faces.1 = (f32[8,128,1024]{2,1,0:T(8,128)}, f32[2,128,1024]{2,1,0:T(8,128)S(1)}) custom-call(f32[8,128,1024]{2,1,0:T(8,128)} %get-tuple-element.20.moist_in, f32[2,128,1024]{2,1,0:T(8,128)S(1)} %get-tuple-element.21.core_ref, f32[2,128,1024]{2,1,0:T(8,128)S(1)} %get-tuple-element.22.rest_ref, ...), custom_call_target="tpu_custom_call", output_to_operand_aliasing={{0}: (0, {})} | custom-call | flops 2621440 | bytes 4194304 | tf_op jit(solution)/shard_map/faces/pallas_call | solution.py:607
  36.2 0.0 collective-permute-done.8.left_ref
  36.2 0.0 collective-permute-done.9.right_ref
  36.3 0.7 %near_bottom.1 = (f32[8,128,1024]{2,1,0:T(8,128)}, f32[128,256]{1,0:T(8,128)}) custom-call(f32[8,128,1024]{2,1,0:T(8,128)} %get-tuple-element.30.moist_in, f32[2,128,1024]{2,1,0:T(8,128)S(1)} %get-tuple-element.31.tail_ref, f32[64,512]{1,0:T(8,128)S(1)} %get-tuple-element.33.own_ref, ...), custom_call_target="tpu_custom_call", output_to_operand_aliasing={{0}: (0, {})} | custom-call | flops 327680 | bytes 1310720 | tf_op jit(solution)/shard_map/near_bottom/pallas_call | solution.py:651
  37.0 0.6 %collective-permute-done.10.refs_0_ = f32[64,512]{1,0:T(8,128)S(1)} collective-permute-done((f32[64,512]{1,0:T(8,128)S(1)}, f32[64,512]{1,0:T(8,128)S(1)}, u32[]{:S(2)}, u32[]{:S(2)}) %collective-permute-start.10) | collective-permute-done | bytes 131104 | tf_op jit(solution)/shard_map/ppermute | solution.py:719
  37.5 0.0 collective-permute-start.11
  37.5 1.3 %collective-permute-done.11.both_far = f32[64,512]{1,0:T(8,128)S(1)} collective-permute-done((f32[64,512]{1,0:T(8,128)S(1)}, f32[64,512]{1,0:T(8,128)S(1)}, u32[]{:S(2)}, u32[]{:S(2)}) %collective-permute-start.11) | collective-permute-done | bytes 131104 | tf_op jit(solution)/shard_map/ppermute | solution.py:715
  (2 shorter events, 0.0 us)
Async XLA Ops:
  2.6 16.6 %collective-permute-start = (f32[2,128,1024]{2,1,0:T(8,128)S(1)}, f32[2,128,1024]{2,1,0:T(8,128)S(1)}, u32[]{:S(2)}, u32[]{:S(2)}) collective-permute-start(f32[2,128,1024]{2,1,0:T(8,128)S(1)} %face.1), channel_id=1, source_target_pairs={{8,24},{24,16},{16,0},{0,8},{9,25},{25,17},{17,1},{1,9},{10,26},{2... | collective-permute-start | bytes 3145736 | tf_op jit(solution)/shard_map/ppermute | solution.py:723
  13.5 4.4 %collective-permute-start.1 = (f32[9,3,8,1024]{3,2,1,0:T(8,128)S(1)}, f32[9,3,8,1024]{3,2,1,0:T(8,128)S(1)}, u32[]{:S(2)}, u32[]{:S(2)}) collective-permute-start(f32[9,3,8,1024]{3,2,1,0:T(8,128)S(1)} %get-tuple-element.24), channel_id=1, source_target_pairs={{0,8},{8,0},{16,24},{24,16},{1,9},{9,1},{17,25},{25,17},{2,10},{10... | collective-permute-start | bytes 2654216 | tf_op jit(solution)/shard_map/ppermute | solution.py:715
  15.6 2.4 %collective-permute-start.2 = (f32[9,3,8,256]{3,2,1,0:T(8,128)S(1)}, f32[9,3,8,256]{3,2,1,0:T(8,128)S(1)}, u32[]{:S(2)}, u32[]{:S(2)}) collective-permute-start(f32[9,3,8,256]{3,2,1,0:T(8,128)S(1)} %get-tuple-element.26), channel_id=1, source_target_pairs={{0,8},{8,0},{16,24},{24,16},{1,9},{9,1},{17,25},{25,17},{2,10},{10... | collective-permute-start | bytes 663560 | tf_op jit(solution)/shard_map/ppermute | solution.py:715
  18.1 15.7 %copy-start = (f32[128,1024]{1,0:T(8,128)S(1)}, f32[128,1024]{1,0:T(8,128)}, u32[]{:S(2)}) copy-start(f32[128,1024]{1,0:T(8,128)} %rain_ref.1) | copy-start | bytes 1572868
  18.2 13.3 %collective-permute-start.5 = (f32[26,8,512]{2,1,0:T(8,128)S(1)}, f32[26,8,512]{2,1,0:T(8,128)S(1)}, u32[]{:S(2)}, u32[]{:S(2)}) collective-permute-start(f32[26,8,512]{2,1,0:T(8,128)S(1)} %pack.1.refs_0_), channel_id=1, source_target_pairs={{0,16},{8,24},{16,0},{24,8},{1,17},{9,25},{17,1},{25,9},{2,18},{10... | collective-permute-start | bytes 1277960 | tf_op jit(solution)/shard_map/ppermute | solution.py:719
  19.4 14.5 %collective-permute-start.3 = (f32[2,64,1024]{2,1,0:T(8,128)S(1)}, f32[2,64,1024]{2,1,0:T(8,128)S(1)}, u32[]{:S(2)}, u32[]{:S(2)}) collective-permute-start(f32[2,64,1024]{2,1,0:T(8,128)S(1)} %get-tuple-element.28), channel_id=1, source_target_pairs={{0,8},{8,0},{16,24},{24,16},{1,9},{9,1},{17,25},{25,17},{2,10},{10... | collective-permute-start | bytes 1572872 | tf_op jit(solution)/shard_map/ppermute | solution.py:715
  19.5 14.3 %collective-permute-start.4 = (f32[2,64,1024]{2,1,0:T(8,128)S(1)}, f32[2,64,1024]{2,1,0:T(8,128)S(1)}, u32[]{:S(2)}, u32[]{:S(2)}) collective-permute-start(f32[2,64,1024]{2,1,0:T(8,128)S(1)} %get-tuple-element.29), channel_id=1, source_target_pairs={{0,8},{8,0},{16,24},{24,16},{1,9},{9,1},{17,25},{25,17},{2,10},{10... | collective-permute-start | bytes 1572872 | tf_op jit(solution)/shard_map/ppermute | solution.py:715
  19.9 11.5 %collective-permute-start.6 = (f32[7,8,512]{2,1,0:T(8,128)S(1)}, f32[7,8,512]{2,1,0:T(8,128)S(1)}, u32[]{:S(2)}, u32[]{:S(2)}) collective-permute-start(f32[7,8,512]{2,1,0:T(8,128)S(1)} %get-tuple-element.27.first), channel_id=1, source_target_pairs={{8,1},{1,8},{9,2},{2,9},{10,3},{3,10},{11,4},{4,11},{12,5},{5,12},... | collective-permute-start | bytes 344072 | tf_op jit(solution)/shard_map/ppermute | solution.py:733
  24.5 6.9 %collective-permute-start.7 = (f32[2,8,512]{2,1,0:T(8,128)S(1)}, f32[2,8,512]{2,1,0:T(8,128)S(1)}, u32[]{:S(2)}, u32[]{:S(2)}) collective-permute-start(f32[2,8,512]{2,1,0:T(8,128)S(1)} %get-tuple-element.32), channel_id=1, source_target_pairs={{8,17},{17,8},{9,18},{18,9},{10,19},{19,10},{11,20},{20,11},{12,21... | collective-permute-start | bytes 98312 | tf_op jit(solution)/shard_map/ppermute | solution.py:733
  32.5 5.0 %collective-permute-start.10 = (f32[64,512]{1,0:T(8,128)S(1)}, f32[64,512]{1,0:T(8,128)S(1)}, u32[]{:S(2)}, u32[]{:S(2)}) collective-permute-start(f32[64,512]{1,0:T(8,128)S(1)} %get-tuple-element.33.own_ref), channel_id=1, source_target_pairs={{0,16},{8,24},{16,0},{24,8},{1,17},{9,25},{17,1},{25,9},{2,18},{10... | collective-permute-start | bytes 393224 | tf_op jit(solution)/shard_map/ppermute | solution.py:719
  33.3 2.9 %collective-permute-start.8 = (f32[64,256]{1,0:T(8,128)S(1)}, f32[64,256]{1,0:T(8,128)S(1)}, u32[]{:S(2)}, u32[]{:S(2)}) collective-permute-start(f32[64,256]{1,0:T(8,128)S(1)} %get-tuple-element.34), channel_id=1, source_target_pairs={{0,8},{8,0},{16,24},{24,16},{1,9},{9,1},{17,25},{25,17},{2,10},{10... | collective-permute-start | bytes 196616 | tf_op jit(solution)/shard_map/ppermute | solution.py:715
  33.3 2.9 %collective-permute-start.9 = (f32[64,256]{1,0:T(8,128)S(1)}, f32[64,256]{1,0:T(8,128)S(1)}, u32[]{:S(2)}, u32[]{:S(2)}) collective-permute-start(f32[64,256]{1,0:T(8,128)S(1)} %get-tuple-element.35), channel_id=1, source_target_pairs={{0,8},{8,0},{16,24},{24,16},{1,9},{9,1},{17,25},{25,17},{2,10},{10... | collective-permute-start | bytes 196616 | tf_op jit(solution)/shard_map/ppermute | solution.py:715
  37.5 1.3 %collective-permute-start.11 = (f32[64,512]{1,0:T(8,128)S(1)}, f32[64,512]{1,0:T(8,128)S(1)}, u32[]{:S(2)}, u32[]{:S(2)}) collective-permute-start(f32[64,512]{1,0:T(8,128)S(1)} %gate.1.chip_far), channel_id=1, source_target_pairs={{0,8},{8,0},{16,24},{24,16},{1,9},{9,1},{17,25},{25,17},{2,10},{10... | collective-permute-start | bytes 393224 | tf_op jit(solution)/shard_map/ppermute | solution.py:715

commit v7 on v6

--- a/solution.py
+++ b/solution.py
@@ -296,15 +296,16 @@
 
 
 def put_rows(ref, plane, pieces):
+    planes = ref.shape[0] - plane
     used = sum(piece.shape[0] for piece in pieces)
-    spare = jnp.zeros((2 * SUB - used, pieces[0].shape[1]), jnp.float32)
+    spare = jnp.zeros((planes * SUB - used, pieces[0].shape[1]), jnp.float32)
     rows = jnp.concatenate([*pieces, spare], 0)
-    ref[plane] = rows[:SUB]
-    ref[plane + 1] = rows[SUB:]
+    for i in range(planes):
+        ref[plane + i] = rows[i * SUB : (i + 1) * SUB]
 
 
 def get_rows(ref, plane, counts):
-    rows = jnp.concatenate([ref[plane], ref[plane + 1]], 0)
+    rows = jnp.concatenate([ref[i] for i in range(plane, ref.shape[0])], 0)
     out, at = [], 0
     for count in counts:
         out.append(rows[at : at + count])
@@ -391,22 +392,23 @@
     tile = half // 2
     b = core * (blocks - 1)
     near, away = half_lanes(chip, half), half_lanes(1 - chip, half)
-    side_ref[:3] = keep_ref[b, :, :, near] + recv_ref[b, :, :, near]
-    rows = [nearest(keep_ref[b, a, :, away] + recv_ref[b, a, :, away], core) for a in range(3)]
-    for which in range(2):
-        for a in range(3):
-            side_ref[3 + a, :, which * tile : (which + 1) * tile] = tile_rows(
-                mine_ref, other_ref, b, core, which, a, 0, tile
-            )
-
-    def sums(slab):
-        return [keep_ref[b, a, :, slab] + recv_ref[b, a, :, slab] for a in range(3)]
-
-    side_ref[6, :, :LANE] = packed(sums(slab_lanes(1 - chip, half)), 1 - chip)
+    spare = jnp.zeros((SWEEPS, half - LANE), jnp.float32)
+
+    def sums(lanes):
+        return [keep_ref[b, a, :, lanes] + recv_ref[b, a, :, lanes] for a in range(3)]
+
+    def rows(values):
+        return [nearest(v, core) for v in values]
+
+    tiles = [
+        jnp.concatenate([tile_rows(mine_ref, other_ref, b, core, which, a, 0, tile) for which in range(2)], 1)
+        for a in range(3)
+    ]
+    halo = nearest(packed(sums(slab_lanes(1 - chip, half)), 1 - chip), core)
+    put_rows(side_ref, 0, [*rows(sums(near)), *rows(tiles), jnp.concatenate([halo, spare], 1)])
     inputs = edge_inputs(mine_ref, other_ref, b, chip, core)
     halo = nearest(packed(sums(slab_lanes(chip, half)) + inputs, chip), core)
-    spare = jnp.zeros((SWEEPS, half - LANE), jnp.float32)
-    put_rows(cross_ref, 0, [*rows, jnp.concatenate([halo, spare], 1)])
+    put_rows(cross_ref, 0, [*rows(sums(away)), jnp.concatenate([halo, spare], 1)])
 
 
 def rim(keep, recv, mine, other, *first):
@@ -415,7 +417,7 @@
         rim_kernel,
         in_specs=[VMEM] * 4 + [ANY] * len(first),
         out_specs=[VMEM] * 2,
-        out_shape=[jax.ShapeDtypeStruct((n, SUB, half), jnp.float32) for n in (7, 2)],
+        out_shape=[jax.ShapeDtypeStruct((n, SUB, half), jnp.float32) for n in (3, 2)],
         compiler_params=params(8),
         cost_estimate=cost(keep.size // 8, keep.size),
         name="rim",
@@ -466,10 +468,10 @@
     def inside(value):
         return jnp.where(outside, 0.0, value)
 
-    *cross, corner = [spread(v, 1 - core) for v in get_rows(cross_ref, 0, (SWEEPS,) * 4)]
-    sums = [inside(side_ref[a] + cross[a]) for a in range(3)]
-    cells(blocks, slice(0, half), sums, [inside(side_ref[3 + a]) for a in range(3)])
-    side, cross = side_ref[6, :, :LANE], corner[:, :LANE]
+    side = [spread(v, 1 - core) for v in get_rows(side_ref, 0, (SWEEPS,) * 7)]
+    cross = [spread(v, 1 - core) for v in get_rows(cross_ref, 0, (SWEEPS,) * 4)]
+    cells(blocks, slice(0, half), [inside(side[a] + cross[a]) for a in range(3)], [inside(v) for v in side[3:6]])
+    side, cross = side[6][:, :LANE], cross[3][:, :LANE]
     sums = [inside(unpacked(side, a) + unpacked(cross, a)) for a in range(3)]
     halo(blocks, sums, [inside(unpacked(cross, a)) for a in range(3, 6)])
 

time: 39.1 us -> 39 us (level)
  no operation moved by 1% of the time
where the time goes in v7:
time: 39 us; the launch traced here: 38.9 us
  Pallas kernels  16.9 us (43%)
  waiting for transfers between devices  10.8 us (28%)
  starting transfers between devices  10.5 us (27%)
  between operations  0.72 us (2%)
    pallas_call x1, Pallas kernels, soil(): pl.pallas_call(soil_kernel, grid=(nrows // rows,), in_specs=[whole, whole...  10.4 us
    ppermute x2, waiting for transfers between devices, strip_swap(): return lax.ppermute(value, ('depth', 'strips'), pairs)  6.54 us
    ppermute x2, starting transfers between devices, strip_swap(): return lax.ppermute(value, ('depth', 'strips'), pairs)  4.96 us
    ppermute x7, waiting for transfers between devices, core_swap(): lax.ppermute(value, 'depth', [(i, i ^ 1) for i in range(lax.axis_size('de...  3.66 us
    ppermute x7, starting transfers between devices, core_swap(): lax.ppermute(value, 'depth', [(i, i ^ 1) for i in range(lax.axis_size('de...  3.23 us
    pallas_call x1, Pallas kernels, faces(): pl.pallas_call(faces_kernel, in_specs=[ANY] + [VMEM] * (4 + PARTS), out_s...  2.4 us
    pallas_call x1, Pallas kernels, face(): pl.pallas_call(face_kernel, in_specs=[HBM] * 5, out_specs=VMEM, out_shape...  2 us
    ppermute x2, starting transfers between devices, chip_swap(): lax.ppermute(value, 'depth', [(i, i ^ 2) for i in range(lax.axis_size('de...  1.82 us
  transfers between devices with their start and end apart: 12, of which 4 were waited for; matrix products, arithmetic and copies ran while one was open for 0% of the time, Pallas kernels for 38%

profile of v7, /device:TPU:0, one launch (start us, length us, event | category | flops | bytes accessed | tf_op | source)
XLA Modules:
  0.0 38.9 jit_solution(4661376725072351931)
XLA Ops:
  0.6 2.0 %face.1 = f32[2,128,1024]{2,1,0:T(8,128)S(1)} custom-call(f32[1,12]{1,0:T(1,128)} %bitcast.3, f32[1,12]{1,0:T(1,128)} %bitcast.5, f32[8,128,1024]{2,1,0:T(8,128)} %psi_hbm.1, s32[8,128,1024]{2,1,0:T(8,128)} %tex_hbm.1, s32[8,128,1024]{2,1,0:T(8,128)} %act_hbm.1), custom_call_target="tpu_custom_call" | custom-call | flops 2621440 | bytes 2621440 | tf_op jit(solution)/shard_map/face/pallas_call | solution.py:120
  2.6 0.5 %collective-permute-start = (f32[2,128,1024]{2,1,0:T(8,128)S(1)}, f32[2,128,1024]{2,1,0:T(8,128)S(1)}, u32[]{:S(2)}, u32[]{:S(2)}) collective-permute-start(f32[2,128,1024]{2,1,0:T(8,128)S(1)} %face.1), channel_id=1, source_target_pairs={{8,24},{24,16},{16,0},{0,8},{9,25},{25,17},{17,1},{1,9},{10,26},{2... | collective-permute-start | bytes 3145736 | tf_op jit(solution)/shard_map/ppermute | solution.py:725
  3.1 10.4 %soil.1 = (f32[8,128,1024]{2,1,0:T(8,128)}, f32[9,3,8,1024]{3,2,1,0:T(8,128)S(1)}, f32[9,3,8,1024]{3,2,1,0:T(8,128)S(1)}, f32[9,3,8,256]{3,2,1,0:T(8,128)S(1)}, ...) custom-call(f32[1,12]{1,0:T(1,128)} %bitcast.4, f32[1,12]{1,0:T(1,128)} %bitcast.6, ...), custom_call_target="tpu_custom_call" | custom-call | flops 62914560 | bytes 20971520 | tf_op jit(solution)/shard_map/soil/pallas_call | solution.py:243
  13.5 2.1 %collective-permute-start.1 = (f32[9,3,8,1024]{3,2,1,0:T(8,128)S(1)}, f32[9,3,8,1024]{3,2,1,0:T(8,128)S(1)}, u32[]{:S(2)}, u32[]{:S(2)}) collective-permute-start(f32[9,3,8,1024]{3,2,1,0:T(8,128)S(1)} %get-tuple-element.24), channel_id=1, source_target_pairs={{0,8},{8,0},{16,24},{24,16},{1,9},{9,1},{17,25},{25,17},{2,10},{10... | collective-permute-start | bytes 2654216 | tf_op jit(solution)/shard_map/ppermute | solution.py:717
  15.6 0.1 collective-permute-start.2
  15.6 2.3 %collective-permute-done.2.other_ref = f32[9,3,8,256]{3,2,1,0:T(8,128)S(1)} collective-permute-done((f32[9,3,8,256]{3,2,1,0:T(8,128)S(1)}, f32[9,3,8,256]{3,2,1,0:T(8,128)S(1)}, u32[]{:S(2)}, u32[]{:S(2)}) %collective-permute-start.2) | collective-permute-done | bytes 221216 | tf_op jit(solution)/shard_map/ppermute | solution.py:717
  18.0 0.0 collective-permute-done.1.recv_ref
  18.0 0.2 pack.1.refs_0_
  18.1 0.0 copy-start
  18.2 1.0 %collective-permute-start.5 = (f32[26,8,512]{2,1,0:T(8,128)S(1)}, f32[26,8,512]{2,1,0:T(8,128)S(1)}, u32[]{:S(2)}, u32[]{:S(2)}) collective-permute-start(f32[26,8,512]{2,1,0:T(8,128)S(1)} %pack.1.refs_0_), channel_id=1, source_target_pairs={{0,16},{8,24},{16,0},{24,8},{1,17},{9,25},{17,1},{25,9},{2,18},{10... | collective-permute-start | bytes 1277960 | tf_op jit(solution)/shard_map/ppermute | solution.py:721
  19.2 0.0 collective-permute-done.refs_1_.ring_ref
  19.2 0.1 rim.1
  19.3 0.1 pass_on.1
  19.4 0.1 collective-permute-start.3
  19.5 0.4 %collective-permute-start.4 = (f32[2,64,1024]{2,1,0:T(8,128)S(1)}, f32[2,64,1024]{2,1,0:T(8,128)S(1)}, u32[]{:S(2)}, u32[]{:S(2)}) collective-permute-start(f32[2,64,1024]{2,1,0:T(8,128)S(1)} %get-tuple-element.29), channel_id=1, source_target_pairs={{0,8},{8,0},{16,24},{24,16},{1,9},{9,1},{17,25},{25,17},{2,10},{10... | collective-permute-start | bytes 1572872 | tf_op jit(solution)/shard_map/ppermute | solution.py:717
  20.0 4.6 %collective-permute-start.6 = (f32[3,8,512]{2,1,0:T(8,128)S(1)}, f32[3,8,512]{2,1,0:T(8,128)S(1)}, u32[]{:S(2)}, u32[]{:S(2)}) collective-permute-start(f32[3,8,512]{2,1,0:T(8,128)S(1)} %get-tuple-element.27.first), channel_id=1, source_target_pairs={{8,1},{1,8},{9,2},{2,9},{10,3},{3,10},{11,4},{4,11},{12,5},{5,12},... | collective-permute-start | bytes 147464 | tf_op jit(solution)/shard_map/ppermute | solution.py:735
  24.5 0.4 %collective-permute-start.7 = (f32[2,8,512]{2,1,0:T(8,128)S(1)}, f32[2,8,512]{2,1,0:T(8,128)S(1)}, u32[]{:S(2)}, u32[]{:S(2)}) collective-permute-start(f32[2,8,512]{2,1,0:T(8,128)S(1)} %get-tuple-element.32), channel_id=1, source_target_pairs={{8,17},{17,8},{9,18},{18,9},{10,19},{19,10},{11,20},{20,11},{12,21... | collective-permute-start | bytes 98312 | tf_op jit(solution)/shard_map/ppermute | solution.py:735
  24.9 6.5 %collective-permute-done.7.cross_ref = f32[2,8,512]{2,1,0:T(8,128)S(1)} collective-permute-done((f32[2,8,512]{2,1,0:T(8,128)S(1)}, f32[2,8,512]{2,1,0:T(8,128)S(1)}, u32[]{:S(2)}, u32[]{:S(2)}) %collective-permute-start.7) | collective-permute-done | bytes 32800 | tf_op jit(solution)/shard_map/ppermute | solution.py:735
  31.5 0.0 collective-permute-done.6.side_ref
  31.5 0.0 collective-permute-done.5.far_ref
  31.5 1.0 %sweeps.1 = (f32[64,512]{1,0:T(8,128)S(1)}, f32[64,256]{1,0:T(8,128)S(1)}, f32[64,256]{1,0:T(8,128)S(1)}) custom-call(f32[9,3,8,1024]{3,2,1,0:T(8,128)S(1)} %get-tuple-element.23.keep_ref, f32[9,3,8,1024]{3,2,1,0:T(8,128)S(1)} %collective-permute-done.1.recv_ref, f32[9,3,8,256]{3,2,1,0:T(8,128)S(1)} %get-tuple-element.25.mine_ref, ...), custom_call_target="tpu_custom_call" | custom-call | flops 4423680 | bytes 2654208 | tf_op jit(solution)/shard_map/sweeps/pallas_call | solution.py:502
  32.5 0.8 %collective-permute-start.10 = (f32[64,512]{1,0:T(8,128)S(1)}, f32[64,512]{1,0:T(8,128)S(1)}, u32[]{:S(2)}, u32[]{:S(2)}) collective-permute-start(f32[64,512]{1,0:T(8,128)S(1)} %get-tuple-element.33.own_ref), channel_id=1, source_target_pairs={{0,16},{8,24},{16,0},{24,8},{1,17},{9,25},{17,1},{25,9},{2,18},{10... | collective-permute-start | bytes 393224 | tf_op jit(solution)/shard_map/ppermute | solution.py:721
  33.3 0.0 collective-permute-start.8
  33.3 0.5 %collective-permute-start.9 = (f32[64,256]{1,0:T(8,128)S(1)}, f32[64,256]{1,0:T(8,128)S(1)}, u32[]{:S(2)}, u32[]{:S(2)}) collective-permute-start(f32[64,256]{1,0:T(8,128)S(1)} %get-tuple-element.35), channel_id=1, source_target_pairs={{0,8},{8,0},{16,24},{24,16},{1,9},{9,1},{17,25},{25,17},{2,10},{10... | collective-permute-start | bytes 196616 | tf_op jit(solution)/shard_map/ppermute | solution.py:717
  33.8 0.0 collective-permute-done.3.refs_0_
  33.8 0.0 collective-permute-done.4.refs_1_
  33.8 0.0 copy-done
  33.8 2.4 %faces.1 = (f32[8,128,1024]{2,1,0:T(8,128)}, f32[2,128,1024]{2,1,0:T(8,128)S(1)}) custom-call(f32[8,128,1024]{2,1,0:T(8,128)} %get-tuple-element.20.moist_in, f32[2,128,1024]{2,1,0:T(8,128)S(1)} %get-tuple-element.21.core_ref, f32[2,128,1024]{2,1,0:T(8,128)S(1)} %get-tuple-element.22.rest_ref, ...), custom_call_target="tpu_custom_call", output_to_operand_aliasing={{0}: (0, {})} | custom-call | flops 2621440 | bytes 4194304 | tf_op jit(solution)/shard_map/faces/pallas_call | solution.py:609
  36.2 0.0 collective-permute-done.8.left_ref
  36.2 0.0 collective-permute-done.9.right_ref
  36.2 0.7 %near_bottom.1 = (f32[8,128,1024]{2,1,0:T(8,128)}, f32[128,256]{1,0:T(8,128)}) custom-call(f32[8,128,1024]{2,1,0:T(8,128)} %get-tuple-element.30.moist_in, f32[2,128,1024]{2,1,0:T(8,128)S(1)} %get-tuple-element.31.tail_ref, f32[64,512]{1,0:T(8,128)S(1)} %get-tuple-element.33.own_ref, ...), custom_call_target="tpu_custom_call", output_to_operand_aliasing={{0}: (0, {})} | custom-call | flops 327680 | bytes 1310720 | tf_op jit(solution)/shard_map/near_bottom/pallas_call | solution.py:653
  36.9 0.6 %collective-permute-done.10.refs_0_ = f32[64,512]{1,0:T(8,128)S(1)} collective-permute-done((f32[64,512]{1,0:T(8,128)S(1)}, f32[64,512]{1,0:T(8,128)S(1)}, u32[]{:S(2)}, u32[]{:S(2)}) %collective-permute-start.10) | collective-permute-done | bytes 131104 | tf_op jit(solution)/shard_map/ppermute | solution.py:721
  37.5 0.0 collective-permute-start.11
  37.5 1.3 %collective-permute-done.11.both_far = f32[64,512]{1,0:T(8,128)S(1)} collective-permute-done((f32[64,512]{1,0:T(8,128)S(1)}, f32[64,512]{1,0:T(8,128)S(1)}, u32[]{:S(2)}, u32[]{:S(2)}) %collective-permute-start.11) | collective-permute-done | bytes 131104 | tf_op jit(solution)/shard_map/ppermute | solution.py:717
  (2 shorter events, 0.0 us)
Async XLA Ops:
  2.6 16.6 %collective-permute-start = (f32[2,128,1024]{2,1,0:T(8,128)S(1)}, f32[2,128,1024]{2,1,0:T(8,128)S(1)}, u32[]{:S(2)}, u32[]{:S(2)}) collective-permute-start(f32[2,128,1024]{2,1,0:T(8,128)S(1)} %face.1), channel_id=1, source_target_pairs={{8,24},{24,16},{16,0},{0,8},{9,25},{25,17},{17,1},{1,9},{10,26},{2... | collective-permute-start | bytes 3145736 | tf_op jit(solution)/shard_map/ppermute | solution.py:725
  13.5 4.4 %collective-permute-start.1 = (f32[9,3,8,1024]{3,2,1,0:T(8,128)S(1)}, f32[9,3,8,1024]{3,2,1,0:T(8,128)S(1)}, u32[]{:S(2)}, u32[]{:S(2)}) collective-permute-start(f32[9,3,8,1024]{3,2,1,0:T(8,128)S(1)} %get-tuple-element.24), channel_id=1, source_target_pairs={{0,8},{8,0},{16,24},{24,16},{1,9},{9,1},{17,25},{25,17},{2,10},{10... | collective-permute-start | bytes 2654216 | tf_op jit(solution)/shard_map/ppermute | solution.py:717
  15.6 2.4 %collective-permute-start.2 = (f32[9,3,8,256]{3,2,1,0:T(8,128)S(1)}, f32[9,3,8,256]{3,2,1,0:T(8,128)S(1)}, u32[]{:S(2)}, u32[]{:S(2)}) collective-permute-start(f32[9,3,8,256]{3,2,1,0:T(8,128)S(1)} %get-tuple-element.26), channel_id=1, source_target_pairs={{0,8},{8,0},{16,24},{24,16},{1,9},{9,1},{17,25},{25,17},{2,10},{10... | collective-permute-start | bytes 663560 | tf_op jit(solution)/shard_map/ppermute | solution.py:717
  18.1 15.6 %copy-start = (f32[128,1024]{1,0:T(8,128)S(1)}, f32[128,1024]{1,0:T(8,128)}, u32[]{:S(2)}) copy-start(f32[128,1024]{1,0:T(8,128)} %rain_ref.1) | copy-start | bytes 1572868
  18.2 13.3 %collective-permute-start.5 = (f32[26,8,512]{2,1,0:T(8,128)S(1)}, f32[26,8,512]{2,1,0:T(8,128)S(1)}, u32[]{:S(2)}, u32[]{:S(2)}) collective-permute-start(f32[26,8,512]{2,1,0:T(8,128)S(1)} %pack.1.refs_0_), channel_id=1, source_target_pairs={{0,16},{8,24},{16,0},{24,8},{1,17},{9,25},{17,1},{25,9},{2,18},{10... | collective-permute-start | bytes 1277960 | tf_op jit(solution)/shard_map/ppermute | solution.py:721
  19.4 14.4 %collective-permute-start.3 = (f32[2,64,1024]{2,1,0:T(8,128)S(1)}, f32[2,64,1024]{2,1,0:T(8,128)S(1)}, u32[]{:S(2)}, u32[]{:S(2)}) collective-permute-start(f32[2,64,1024]{2,1,0:T(8,128)S(1)} %get-tuple-element.28), channel_id=1, source_target_pairs={{0,8},{8,0},{16,24},{24,16},{1,9},{9,1},{17,25},{25,17},{2,10},{10... | collective-permute-start | bytes 1572872 | tf_op jit(solution)/shard_map/ppermute | solution.py:717
  19.5 14.3 %collective-permute-start.4 = (f32[2,64,1024]{2,1,0:T(8,128)S(1)}, f32[2,64,1024]{2,1,0:T(8,128)S(1)}, u32[]{:S(2)}, u32[]{:S(2)}) collective-permute-start(f32[2,64,1024]{2,1,0:T(8,128)S(1)} %get-tuple-element.29), channel_id=1, source_target_pairs={{0,8},{8,0},{16,24},{24,16},{1,9},{9,1},{17,25},{25,17},{2,10},{10... | collective-permute-start | bytes 1572872 | tf_op jit(solution)/shard_map/ppermute | solution.py:717
  20.0 11.5 %collective-permute-start.6 = (f32[3,8,512]{2,1,0:T(8,128)S(1)}, f32[3,8,512]{2,1,0:T(8,128)S(1)}, u32[]{:S(2)}, u32[]{:S(2)}) collective-permute-start(f32[3,8,512]{2,1,0:T(8,128)S(1)} %get-tuple-element.27.first), channel_id=1, source_target_pairs={{8,1},{1,8},{9,2},{2,9},{10,3},{3,10},{11,4},{4,11},{12,5},{5,12},... | collective-permute-start | bytes 147464 | tf_op jit(solution)/shard_map/ppermute | solution.py:735
  24.5 6.9 %collective-permute-start.7 = (f32[2,8,512]{2,1,0:T(8,128)S(1)}, f32[2,8,512]{2,1,0:T(8,128)S(1)}, u32[]{:S(2)}, u32[]{:S(2)}) collective-permute-start(f32[2,8,512]{2,1,0:T(8,128)S(1)} %get-tuple-element.32), channel_id=1, source_target_pairs={{8,17},{17,8},{9,18},{18,9},{10,19},{19,10},{11,20},{20,11},{12,21... | collective-permute-start | bytes 98312 | tf_op jit(solution)/shard_map/ppermute | solution.py:735
  32.5 5.0 %collective-permute-start.10 = (f32[64,512]{1,0:T(8,128)S(1)}, f32[64,512]{1,0:T(8,128)S(1)}, u32[]{:S(2)}, u32[]{:S(2)}) collective-permute-start(f32[64,512]{1,0:T(8,128)S(1)} %get-tuple-element.33.own_ref), channel_id=1, source_target_pairs={{0,16},{8,24},{16,0},{24,8},{1,17},{9,25},{17,1},{25,9},{2,18},{10... | collective-permute-start | bytes 393224 | tf_op jit(solution)/shard_map/ppermute | solution.py:721
  33.3 2.9 %collective-permute-start.8 = (f32[64,256]{1,0:T(8,128)S(1)}, f32[64,256]{1,0:T(8,128)S(1)}, u32[]{:S(2)}, u32[]{:S(2)}) collective-permute-start(f32[64,256]{1,0:T(8,128)S(1)} %get-tuple-element.34), channel_id=1, source_target_pairs={{0,8},{8,0},{16,24},{24,16},{1,9},{9,1},{17,25},{25,17},{2,10},{10... | collective-permute-start | bytes 196616 | tf_op jit(solution)/shard_map/ppermute | solution.py:717
  33.3 2.9 %collective-permute-start.9 = (f32[64,256]{1,0:T(8,128)S(1)}, f32[64,256]{1,0:T(8,128)S(1)}, u32[]{:S(2)}, u32[]{:S(2)}) collective-permute-start(f32[64,256]{1,0:T(8,128)S(1)} %get-tuple-element.35), channel_id=1, source_target_pairs={{0,8},{8,0},{16,24},{24,16},{1,9},{9,1},{17,25},{25,17},{2,10},{10... | collective-permute-start | bytes 196616 | tf_op jit(solution)/shard_map/ppermute | solution.py:717
  37.5 1.3 %collective-permute-start.11 = (f32[64,512]{1,0:T(8,128)S(1)}, f32[64,512]{1,0:T(8,128)S(1)}, u32[]{:S(2)}, u32[]{:S(2)}) collective-permute-start(f32[64,512]{1,0:T(8,128)S(1)} %gate.1.chip_far), channel_id=1, source_target_pairs={{0,8},{8,0},{16,24},{24,16},{1,9},{9,1},{17,25},{25,17},{2,10},{10... | collective-permute-start | bytes 393224 | tf_op jit(solution)/shard_map/ppermute | solution.py:717

commit v8 on v7

--- a/solution.py
+++ b/solution.py
@@ -164,7 +164,7 @@
                 kind = tex_ref[layer, rws, lanes]
                 psi = psi_ref[layer, rws, lanes]
                 active = act_ref[layer, rws, lanes].astype(jnp.float32)
-                bits = [(kind & (1 << b)) != 0 for b in range(nbits)]
+                bits = [(kind & (1 << b)) != 0 for b in range(nbits - 1)] + [kind >= 1 << (nbits - 1)]
                 wet = jnp.exp2(gathered(par_tab, kind) * jnp.minimum(psi, 0.0))
                 cond = gathered(sat_tab, kind) * active * (wet * wet)
                 mob = picked(theta, bits)

time: 39 us -> 38.9 us (level)
  no operation moved by 1% of the time
where the time goes in v8:
time: 38.9 us; the launch traced here: 38.7 us
  Pallas kernels  16.8 us (43%)
  waiting for transfers between devices  10.8 us (28%)
  starting transfers between devices  10.5 us (27%)
  between operations  0.72 us (2%)
    pallas_call x1, Pallas kernels, soil(): pl.pallas_call(soil_kernel, grid=(nrows // rows,), in_specs=[whole, whole...  10.3 us
    ppermute x2, waiting for transfers between devices, strip_swap(): return lax.ppermute(value, ('depth', 'strips'), pairs)  6.54 us
    ppermute x2, starting transfers between devices, strip_swap(): return lax.ppermute(value, ('depth', 'strips'), pairs)  4.96 us
    ppermute x7, waiting for transfers between devices, core_swap(): lax.ppermute(value, 'depth', [(i, i ^ 1) for i in range(lax.axis_size('de...  3.66 us
    ppermute x7, starting transfers between devices, core_swap(): lax.ppermute(value, 'depth', [(i, i ^ 1) for i in range(lax.axis_size('de...  3.23 us
    pallas_call x1, Pallas kernels, faces(): pl.pallas_call(faces_kernel, in_specs=[ANY] + [VMEM] * (4 + PARTS), out_s...  2.4 us
    pallas_call x1, Pallas kernels, face(): pl.pallas_call(face_kernel, in_specs=[HBM] * 5, out_specs=VMEM, out_shape...  2 us
    ppermute x2, starting transfers between devices, chip_swap(): lax.ppermute(value, 'depth', [(i, i ^ 2) for i in range(lax.axis_size('de...  1.82 us
  transfers between devices with their start and end apart: 12, of which 4 were waited for; matrix products, arithmetic and copies ran while one was open for 0% of the time, Pallas kernels for 38%

profile of v8, /device:TPU:0, one launch (start us, length us, event | category | flops | bytes accessed | tf_op | source)
XLA Modules:
  0.0 38.7 jit_solution(10013454041155205702)
XLA Ops:
  0.6 2.0 %face.1 = f32[2,128,1024]{2,1,0:T(8,128)S(1)} custom-call(f32[1,12]{1,0:T(1,128)} %bitcast.3, f32[1,12]{1,0:T(1,128)} %bitcast.5, f32[8,128,1024]{2,1,0:T(8,128)} %psi_hbm.1, s32[8,128,1024]{2,1,0:T(8,128)} %tex_hbm.1, s32[8,128,1024]{2,1,0:T(8,128)} %act_hbm.1), custom_call_target="tpu_custom_call" | custom-call | flops 2621440 | bytes 2621440 | tf_op jit(solution)/shard_map/face/pallas_call | solution.py:120
  2.6 0.5 %collective-permute-start = (f32[2,128,1024]{2,1,0:T(8,128)S(1)}, f32[2,128,1024]{2,1,0:T(8,128)S(1)}, u32[]{:S(2)}, u32[]{:S(2)}) collective-permute-start(f32[2,128,1024]{2,1,0:T(8,128)S(1)} %face.1), channel_id=1, source_target_pairs={{8,24},{24,16},{16,0},{0,8},{9,25},{25,17},{17,1},{1,9},{10,26},{2... | collective-permute-start | bytes 3145736 | tf_op jit(solution)/shard_map/ppermute | solution.py:725
  3.1 10.3 %soil.1 = (f32[8,128,1024]{2,1,0:T(8,128)}, f32[9,3,8,1024]{3,2,1,0:T(8,128)S(1)}, f32[9,3,8,1024]{3,2,1,0:T(8,128)S(1)}, f32[9,3,8,256]{3,2,1,0:T(8,128)S(1)}, ...) custom-call(f32[1,12]{1,0:T(1,128)} %bitcast.4, f32[1,12]{1,0:T(1,128)} %bitcast.6, ...), custom_call_target="tpu_custom_call" | custom-call | flops 62914560 | bytes 20971520 | tf_op jit(solution)/shard_map/soil/pallas_call | solution.py:243
  13.4 2.1 %collective-permute-start.1 = (f32[9,3,8,1024]{3,2,1,0:T(8,128)S(1)}, f32[9,3,8,1024]{3,2,1,0:T(8,128)S(1)}, u32[]{:S(2)}, u32[]{:S(2)}) collective-permute-start(f32[9,3,8,1024]{3,2,1,0:T(8,128)S(1)} %get-tuple-element.24), channel_id=1, source_target_pairs={{0,8},{8,0},{16,24},{24,16},{1,9},{9,1},{17,25},{25,17},{2,10},{10... | collective-permute-start | bytes 2654216 | tf_op jit(solution)/shard_map/ppermute | solution.py:717
  15.5 0.1 collective-permute-start.2
  15.5 2.3 %collective-permute-done.2.other_ref = f32[9,3,8,256]{3,2,1,0:T(8,128)S(1)} collective-permute-done((f32[9,3,8,256]{3,2,1,0:T(8,128)S(1)}, f32[9,3,8,256]{3,2,1,0:T(8,128)S(1)}, u32[]{:S(2)}, u32[]{:S(2)}) %collective-permute-start.2) | collective-permute-done | bytes 221216 | tf_op jit(solution)/shard_map/ppermute | solution.py:717
  17.8 0.0 collective-permute-done.1.recv_ref
  17.8 0.2 pack.1.refs_0_
  18.0 0.0 copy-start
  18.0 1.0 %collective-permute-start.5 = (f32[26,8,512]{2,1,0:T(8,128)S(1)}, f32[26,8,512]{2,1,0:T(8,128)S(1)}, u32[]{:S(2)}, u32[]{:S(2)}) collective-permute-start(f32[26,8,512]{2,1,0:T(8,128)S(1)} %pack.1.refs_0_), channel_id=1, source_target_pairs={{0,16},{8,24},{16,0},{24,8},{1,17},{9,25},{17,1},{25,9},{2,18},{10... | collective-permute-start | bytes 1277960 | tf_op jit(solution)/shard_map/ppermute | solution.py:721
  19.1 0.0 collective-permute-done.refs_1_.ring_ref
  19.1 0.1 rim.1
  19.2 0.1 pass_on.1
  19.3 0.1 collective-permute-start.3
  19.4 0.4 %collective-permute-start.4 = (f32[2,64,1024]{2,1,0:T(8,128)S(1)}, f32[2,64,1024]{2,1,0:T(8,128)S(1)}, u32[]{:S(2)}, u32[]{:S(2)}) collective-permute-start(f32[2,64,1024]{2,1,0:T(8,128)S(1)} %get-tuple-element.29), channel_id=1, source_target_pairs={{0,8},{8,0},{16,24},{24,16},{1,9},{9,1},{17,25},{25,17},{2,10},{10... | collective-permute-start | bytes 1572872 | tf_op jit(solution)/shard_map/ppermute | solution.py:717
  19.8 4.6 %collective-permute-start.6 = (f32[3,8,512]{2,1,0:T(8,128)S(1)}, f32[3,8,512]{2,1,0:T(8,128)S(1)}, u32[]{:S(2)}, u32[]{:S(2)}) collective-permute-start(f32[3,8,512]{2,1,0:T(8,128)S(1)} %get-tuple-element.27.first), channel_id=1, source_target_pairs={{8,1},{1,8},{9,2},{2,9},{10,3},{3,10},{11,4},{4,11},{12,5},{5,12},... | collective-permute-start | bytes 147464 | tf_op jit(solution)/shard_map/ppermute | solution.py:735
  24.4 0.4 %collective-permute-start.7 = (f32[2,8,512]{2,1,0:T(8,128)S(1)}, f32[2,8,512]{2,1,0:T(8,128)S(1)}, u32[]{:S(2)}, u32[]{:S(2)}) collective-permute-start(f32[2,8,512]{2,1,0:T(8,128)S(1)} %get-tuple-element.32), channel_id=1, source_target_pairs={{8,17},{17,8},{9,18},{18,9},{10,19},{19,10},{11,20},{20,11},{12,21... | collective-permute-start | bytes 98312 | tf_op jit(solution)/shard_map/ppermute | solution.py:735
  24.8 6.5 %collective-permute-done.7.cross_ref = f32[2,8,512]{2,1,0:T(8,128)S(1)} collective-permute-done((f32[2,8,512]{2,1,0:T(8,128)S(1)}, f32[2,8,512]{2,1,0:T(8,128)S(1)}, u32[]{:S(2)}, u32[]{:S(2)}) %collective-permute-start.7) | collective-permute-done | bytes 32800 | tf_op jit(solution)/shard_map/ppermute | solution.py:735
  31.3 0.0 collective-permute-done.6.side_ref
  31.3 0.0 collective-permute-done.5.far_ref
  31.3 1.0 %sweeps.1 = (f32[64,512]{1,0:T(8,128)S(1)}, f32[64,256]{1,0:T(8,128)S(1)}, f32[64,256]{1,0:T(8,128)S(1)}) custom-call(f32[9,3,8,1024]{3,2,1,0:T(8,128)S(1)} %get-tuple-element.23.keep_ref, f32[9,3,8,1024]{3,2,1,0:T(8,128)S(1)} %collective-permute-done.1.recv_ref, f32[9,3,8,256]{3,2,1,0:T(8,128)S(1)} %get-tuple-element.25.mine_ref, ...), custom_call_target="tpu_custom_call" | custom-call | flops 4423680 | bytes 2654208 | tf_op jit(solution)/shard_map/sweeps/pallas_call | solution.py:502
  32.3 0.8 %collective-permute-start.10 = (f32[64,512]{1,0:T(8,128)S(1)}, f32[64,512]{1,0:T(8,128)S(1)}, u32[]{:S(2)}, u32[]{:S(2)}) collective-permute-start(f32[64,512]{1,0:T(8,128)S(1)} %get-tuple-element.33.own_ref), channel_id=1, source_target_pairs={{0,16},{8,24},{16,0},{24,8},{1,17},{9,25},{17,1},{25,9},{2,18},{10... | collective-permute-start | bytes 393224 | tf_op jit(solution)/shard_map/ppermute | solution.py:721
  33.1 0.0 collective-permute-start.8
  33.1 0.5 %collective-permute-start.9 = (f32[64,256]{1,0:T(8,128)S(1)}, f32[64,256]{1,0:T(8,128)S(1)}, u32[]{:S(2)}, u32[]{:S(2)}) collective-permute-start(f32[64,256]{1,0:T(8,128)S(1)} %get-tuple-element.35), channel_id=1, source_target_pairs={{0,8},{8,0},{16,24},{24,16},{1,9},{9,1},{17,25},{25,17},{2,10},{10... | collective-permute-start | bytes 196616 | tf_op jit(solution)/shard_map/ppermute | solution.py:717
  33.7 0.0 collective-permute-done.3.refs_0_
  33.7 0.0 collective-permute-done.4.refs_1_
  33.7 0.0 copy-done
  33.7 2.4 %faces.1 = (f32[8,128,1024]{2,1,0:T(8,128)}, f32[2,128,1024]{2,1,0:T(8,128)S(1)}) custom-call(f32[8,128,1024]{2,1,0:T(8,128)} %get-tuple-element.20.moist_in, f32[2,128,1024]{2,1,0:T(8,128)S(1)} %get-tuple-element.21.core_ref, f32[2,128,1024]{2,1,0:T(8,128)S(1)} %get-tuple-element.22.rest_ref, ...), custom_call_target="tpu_custom_call", output_to_operand_aliasing={{0}: (0, {})} | custom-call | flops 2621440 | bytes 4194304 | tf_op jit(solution)/shard_map/faces/pallas_call | solution.py:609
  36.1 0.0 collective-permute-done.8.left_ref
  36.1 0.0 collective-permute-done.9.right_ref
  36.1 0.7 %near_bottom.1 = (f32[8,128,1024]{2,1,0:T(8,128)}, f32[128,256]{1,0:T(8,128)}) custom-call(f32[8,128,1024]{2,1,0:T(8,128)} %get-tuple-element.30.moist_in, f32[2,128,1024]{2,1,0:T(8,128)S(1)} %get-tuple-element.31.tail_ref, f32[64,512]{1,0:T(8,128)S(1)} %get-tuple-element.33.own_ref, ...), custom_call_target="tpu_custom_call", output_to_operand_aliasing={{0}: (0, {})} | custom-call | flops 327680 | bytes 1310720 | tf_op jit(solution)/shard_map/near_bottom/pallas_call | solution.py:653
  36.8 0.6 %collective-permute-done.10.refs_0_ = f32[64,512]{1,0:T(8,128)S(1)} collective-permute-done((f32[64,512]{1,0:T(8,128)S(1)}, f32[64,512]{1,0:T(8,128)S(1)}, u32[]{:S(2)}, u32[]{:S(2)}) %collective-permute-start.10) | collective-permute-done | bytes 131104 | tf_op jit(solution)/shard_map/ppermute | solution.py:721
  37.4 0.0 collective-permute-start.11
  37.4 1.3 %collective-permute-done.11.both_far = f32[64,512]{1,0:T(8,128)S(1)} collective-permute-done((f32[64,512]{1,0:T(8,128)S(1)}, f32[64,512]{1,0:T(8,128)S(1)}, u32[]{:S(2)}, u32[]{:S(2)}) %collective-permute-start.11) | collective-permute-done | bytes 131104 | tf_op jit(solution)/shard_map/ppermute | solution.py:717
  (2 shorter events, 0.0 us)
Async XLA Ops:
  2.6 16.4 %collective-permute-start = (f32[2,128,1024]{2,1,0:T(8,128)S(1)}, f32[2,128,1024]{2,1,0:T(8,128)S(1)}, u32[]{:S(2)}, u32[]{:S(2)}) collective-permute-start(f32[2,128,1024]{2,1,0:T(8,128)S(1)} %face.1), channel_id=1, source_target_pairs={{8,24},{24,16},{16,0},{0,8},{9,25},{25,17},{17,1},{1,9},{10,26},{2... | collective-permute-start | bytes 3145736 | tf_op jit(solution)/shard_map/ppermute | solution.py:725
  13.4 4.4 %collective-permute-start.1 = (f32[9,3,8,1024]{3,2,1,0:T(8,128)S(1)}, f32[9,3,8,1024]{3,2,1,0:T(8,128)S(1)}, u32[]{:S(2)}, u32[]{:S(2)}) collective-permute-start(f32[9,3,8,1024]{3,2,1,0:T(8,128)S(1)} %get-tuple-element.24), channel_id=1, source_target_pairs={{0,8},{8,0},{16,24},{24,16},{1,9},{9,1},{17,25},{25,17},{2,10},{10... | collective-permute-start | bytes 2654216 | tf_op jit(solution)/shard_map/ppermute | solution.py:717
  15.5 2.4 %collective-permute-start.2 = (f32[9,3,8,256]{3,2,1,0:T(8,128)S(1)}, f32[9,3,8,256]{3,2,1,0:T(8,128)S(1)}, u32[]{:S(2)}, u32[]{:S(2)}) collective-permute-start(f32[9,3,8,256]{3,2,1,0:T(8,128)S(1)} %get-tuple-element.26), channel_id=1, source_target_pairs={{0,8},{8,0},{16,24},{24,16},{1,9},{9,1},{17,25},{25,17},{2,10},{10... | collective-permute-start | bytes 663560 | tf_op jit(solution)/shard_map/ppermute | solution.py:717
  18.0 15.6 %copy-start = (f32[128,1024]{1,0:T(8,128)S(1)}, f32[128,1024]{1,0:T(8,128)}, u32[]{:S(2)}) copy-start(f32[128,1024]{1,0:T(8,128)} %rain_ref.1) | copy-start | bytes 1572868
  18.0 13.3 %collective-permute-start.5 = (f32[26,8,512]{2,1,0:T(8,128)S(1)}, f32[26,8,512]{2,1,0:T(8,128)S(1)}, u32[]{:S(2)}, u32[]{:S(2)}) collective-permute-start(f32[26,8,512]{2,1,0:T(8,128)S(1)} %pack.1.refs_0_), channel_id=1, source_target_pairs={{0,16},{8,24},{16,0},{24,8},{1,17},{9,25},{17,1},{25,9},{2,18},{10... | collective-permute-start | bytes 1277960 | tf_op jit(solution)/shard_map/ppermute | solution.py:721
  19.3 14.4 %collective-permute-start.3 = (f32[2,64,1024]{2,1,0:T(8,128)S(1)}, f32[2,64,1024]{2,1,0:T(8,128)S(1)}, u32[]{:S(2)}, u32[]{:S(2)}) collective-permute-start(f32[2,64,1024]{2,1,0:T(8,128)S(1)} %get-tuple-element.28), channel_id=1, source_target_pairs={{0,8},{8,0},{16,24},{24,16},{1,9},{9,1},{17,25},{25,17},{2,10},{10... | collective-permute-start | bytes 1572872 | tf_op jit(solution)/shard_map/ppermute | solution.py:717
  19.4 14.3 %collective-permute-start.4 = (f32[2,64,1024]{2,1,0:T(8,128)S(1)}, f32[2,64,1024]{2,1,0:T(8,128)S(1)}, u32[]{:S(2)}, u32[]{:S(2)}) collective-permute-start(f32[2,64,1024]{2,1,0:T(8,128)S(1)} %get-tuple-element.29), channel_id=1, source_target_pairs={{0,8},{8,0},{16,24},{24,16},{1,9},{9,1},{17,25},{25,17},{2,10},{10... | collective-permute-start | bytes 1572872 | tf_op jit(solution)/shard_map/ppermute | solution.py:717
  19.8 11.5 %collective-permute-start.6 = (f32[3,8,512]{2,1,0:T(8,128)S(1)}, f32[3,8,512]{2,1,0:T(8,128)S(1)}, u32[]{:S(2)}, u32[]{:S(2)}) collective-permute-start(f32[3,8,512]{2,1,0:T(8,128)S(1)} %get-tuple-element.27.first), channel_id=1, source_target_pairs={{8,1},{1,8},{9,2},{2,9},{10,3},{3,10},{11,4},{4,11},{12,5},{5,12},... | collective-permute-start | bytes 147464 | tf_op jit(solution)/shard_map/ppermute | solution.py:735
  24.4 6.9 %collective-permute-start.7 = (f32[2,8,512]{2,1,0:T(8,128)S(1)}, f32[2,8,512]{2,1,0:T(8,128)S(1)}, u32[]{:S(2)}, u32[]{:S(2)}) collective-permute-start(f32[2,8,512]{2,1,0:T(8,128)S(1)} %get-tuple-element.32), channel_id=1, source_target_pairs={{8,17},{17,8},{9,18},{18,9},{10,19},{19,10},{11,20},{20,11},{12,21... | collective-permute-start | bytes 98312 | tf_op jit(solution)/shard_map/ppermute | solution.py:735
  32.3 5.0 %collective-permute-start.10 = (f32[64,512]{1,0:T(8,128)S(1)}, f32[64,512]{1,0:T(8,128)S(1)}, u32[]{:S(2)}, u32[]{:S(2)}) collective-permute-start(f32[64,512]{1,0:T(8,128)S(1)} %get-tuple-element.33.own_ref), channel_id=1, source_target_pairs={{0,16},{8,24},{16,0},{24,8},{1,17},{9,25},{17,1},{25,9},{2,18},{10... | collective-permute-start | bytes 393224 | tf_op jit(solution)/shard_map/ppermute | solution.py:721
  33.1 2.9 %collective-permute-start.8 = (f32[64,256]{1,0:T(8,128)S(1)}, f32[64,256]{1,0:T(8,128)S(1)}, u32[]{:S(2)}, u32[]{:S(2)}) collective-permute-start(f32[64,256]{1,0:T(8,128)S(1)} %get-tuple-element.34), channel_id=1, source_target_pairs={{0,8},{8,0},{16,24},{24,16},{1,9},{9,1},{17,25},{25,17},{2,10},{10... | collective-permute-start | bytes 196616 | tf_op jit(solution)/shard_map/ppermute | solution.py:717
  33.1 2.9 %collective-permute-start.9 = (f32[64,256]{1,0:T(8,128)S(1)}, f32[64,256]{1,0:T(8,128)S(1)}, u32[]{:S(2)}, u32[]{:S(2)}) collective-permute-start(f32[64,256]{1,0:T(8,128)S(1)} %get-tuple-element.35), channel_id=1, source_target_pairs={{0,8},{8,0},{16,24},{24,16},{1,9},{9,1},{17,25},{25,17},{2,10},{10... | collective-permute-start | bytes 196616 | tf_op jit(solution)/shard_map/ppermute | solution.py:717
  37.4 1.3 %collective-permute-start.11 = (f32[64,512]{1,0:T(8,128)S(1)}, f32[64,512]{1,0:T(8,128)S(1)}, u32[]{:S(2)}, u32[]{:S(2)}) collective-permute-start(f32[64,512]{1,0:T(8,128)S(1)} %gate.1.chip_far), channel_id=1, source_target_pairs={{0,8},{8,0},{16,24},{24,16},{1,9},{9,1},{17,25},{25,17},{2,10},{10... | collective-permute-start | bytes 393224 | tf_op jit(solution)/shard_map/ppermute | solution.py:717
